TPU v7x, 256 devices: a whole 4x4x8 slice. The times are simulated.
256 devices in a mesh: ctx: 32 (over y, z_hi, x), exp: 8 (over z_lo, core).
Axes of the slice: x: 4, y: 4, z: 8 (z_hi: 2, z_lo: 4; z = z_hi * 4 + z_lo), core: 2. Of those that a mesh axis runs over, the one named last changes fastest.
Arguments:
- resid: bfloat16 [4096, 4096], P('ctx'), may hold values from -6 to 6
- out_grad: bfloat16 [4096, 4096], P('ctx'), may hold values from -6 to 6
- norm_gain: float32 [4096], replicated, may hold values from 0.1 to 1.9
- expert_ids: int32 [4096, 8], P('ctx'), may hold values from 0 to 127, all different within a row; in each aligned block of 128 rows (0 to 127, 128 to 255, ...) at most 16 rows name the same one
- combine: float32 [4096, 8], P('ctx'), may hold values from 0.3 to 1.2
- w_gate: bfloat16 [4096, 1536], P(None, 'exp'), may hold values from -0.09375 to 0.09375
- w_up: bfloat16 [4096, 1536], P(None, 'exp'), may hold values from -0.09375 to 0.09375
- w_down: bfloat16 [1536, 4096], P('exp'), may hold values from -0.15625 to 0.15625
- w_out: bfloat16 [4096, 4096], P('exp'), may hold values from -0.09375 to 0.09375
- queries: bfloat16 [4096, 4096], P('ctx', 'exp'), may hold values from -6 to 6
- keys: bfloat16 [4096, 256], P('ctx'), may hold values from -6 to 6
- values: bfloat16 [4096, 256], P('ctx'), may hold values from -6 to 6
- span_order: int32 [64], replicated, may hold values from 0 to 63, each once
Outputs:
- resid_grad: bfloat16 [4096, 4096], P('ctx')
- query_grad: bfloat16 [4096, 4096], P('ctx', 'exp')
- key_grad: bfloat16 [4096, 256], P(('ctx', 'exp'))
- value_grad: bfloat16 [4096, 256], P(('ctx', 'exp'))
Inputs may be any that keep to these rules, and one draw needn't show every extreme that they name: `expert_ids`: the 8 entries of a token differ; among the 128 stored rows of one index of ctx at most 16 name any one expert. `span_order`: each block of positions appears once.
All inputs are finite; a program needn't handle non-finite values.
Results may differ from a plain program's by a relative error of at most 0.013.
Values may be sent and summed in bfloat16 or wider, within the bound.
No kernel may reach another device: no remote copies, remote signals or barrier semaphores. Data moves between devices by JAX's collectives and lax.ppermute only.
A program may use at most 128 MiB of HBM per device.

v0:
```python
import math

import jax
import jax.numpy as jnp
from jax import lax
from jax.sharding import PartitionSpec as P

DH = 128
GROUP = 16
CAP = 16


eps_norm = 1e-06


def contract_last(left, right):
    return lax.dot_general(
        left, right, (((1,), (1,)), ((), ())), preferred_element_type=jnp.float32
    )


def expert_grads(normed_rows, grad_rows, w_gate, w_up, w_down):
    gate_pre = jnp.dot(normed_rows, w_gate, preferred_element_type=jnp.float32)
    up_pre = jnp.dot(normed_rows, w_up, preferred_element_type=jnp.float32)
    hidden_grad = contract_last(grad_rows, w_down)
    sig_gate = jax.nn.sigmoid(gate_pre)
    gate_grad = (hidden_grad * up_pre * sig_gate * (1.0 + gate_pre * (1.0 - sig_gate))).astype(
        jnp.bfloat16
    )
    up_grad = (hidden_grad * gate_pre * sig_gate).astype(jnp.bfloat16)
    return contract_last(gate_grad, w_gate) + contract_last(up_grad, w_up)


def softmax_stats(query_block, grad_block, keys_all, values_all, allowed, scale):
    scores = (
        jnp.einsum("shd,td->hst", query_block, keys_all, preferred_element_type=jnp.float32) * scale
    )
    scores = jnp.where(allowed[None], scores, -jnp.inf)
    row_max = jnp.max(scores, axis=2, keepdims=True)
    log_total = row_max + jnp.log(jnp.sum(jnp.exp(scores - row_max), axis=2, keepdims=True))
    probs = jnp.exp(scores - log_total)
    probs_low = probs.astype(jnp.bfloat16)
    attn_out = jnp.einsum("hst,td->hsd", probs_low, values_all, preferred_element_type=jnp.float32)
    delta = jnp.sum(jnp.swapaxes(grad_block, 0, 1).astype(jnp.float32) * attn_out, axis=2)
    prob_grad = jnp.einsum(
        "shd,td->hst", grad_block, values_all, preferred_element_type=jnp.float32
    )
    score_grad = (probs * (prob_grad - delta[..., None])).astype(jnp.bfloat16)
    query_part = (
        jnp.einsum("hst,td->shd", score_grad, keys_all, preferred_element_type=jnp.float32) * scale
    )
    return (log_total[..., 0], delta, query_part)


def key_term(query_block, grad_block, log_total, delta, key_rows, value_rows, allowed, scale):
    scores = (
        jnp.einsum("shd,td->hst", query_block, key_rows, preferred_element_type=jnp.float32) * scale
    )
    scores = jnp.where(allowed[None], scores, -jnp.inf)
    probs = jnp.exp(scores - log_total[..., None])
    probs_low = probs.astype(jnp.bfloat16)
    prob_grad = jnp.einsum(
        "shd,td->hst", grad_block, value_rows, preferred_element_type=jnp.float32
    )
    score_grad = (probs * (prob_grad - delta[..., None])).astype(jnp.bfloat16)
    key_part = (
        jnp.einsum("hst,shd->td", score_grad, query_block, preferred_element_type=jnp.float32)
        * scale
    )
    value_part = jnp.einsum(
        "hst,shd->td", probs_low, grad_block, preferred_element_type=jnp.float32
    )
    return jnp.concatenate([key_part, value_part], axis=1)


def head_columns(received, kv_count):
    lead = received.shape[:-3]
    slice_rows = received.shape[-2]
    grouped = jnp.sum(received.reshape(lead + (kv_count, -1, slice_rows, 2 * DH)), axis=-3)
    moved = jnp.moveaxis(grouped, -3, -2)
    key_cols = moved[..., :DH].reshape(lead + (slice_rows, kv_count * DH))
    value_cols = moved[..., DH:].reshape(lead + (slice_rows, kv_count * DH))
    return jnp.concatenate([key_cols, value_cols], axis=-1)


def on_device(
    resid,
    out_grad,
    norm_gain,
    expert_ids,
    combine,
    w_gate,
    w_up,
    w_down,
    w_out,
    queries,
    keys,
    values,
    span_order,
):
    row_count = resid.shape[0]
    head_count = queries.shape[1] // DH
    kv_count = keys.shape[1] // DH
    block_rows = row_count // 2
    scale = 1.0 / math.sqrt(DH)
    exp_count = lax.axis_size("exp")
    slice_rows = row_count // exp_count
    resid_wide = resid.astype(jnp.float32)
    rms_scale = lax.rsqrt(jnp.mean(resid_wide * resid_wide, axis=1, keepdims=True) + eps_norm)
    normed = (resid_wide * rms_scale * norm_gain).astype(jnp.bfloat16)
    expert_weight = jnp.sum(jnp.where(expert_ids == 0, combine, jnp.zeros_like(combine)), axis=1)
    scaled_grad = (out_grad.astype(jnp.float32) * expert_weight[:, None]).astype(jnp.bfloat16)
    chosen = jnp.any(expert_ids == 0, axis=1)
    rank = jnp.cumsum(chosen.astype(jnp.int32)) - 1
    slot_ids = lax.iota(jnp.int32, CAP)
    selector = ((rank[None, :] == slot_ids[:, None]) & chosen[None, :]).astype(jnp.bfloat16)
    normed_rows = jnp.dot(selector, normed, preferred_element_type=jnp.float32).astype(jnp.bfloat16)
    grad_rows = jnp.dot(selector, scaled_grad, preferred_element_type=jnp.float32).astype(
        jnp.bfloat16
    )
    partial_grad = expert_grads(normed_rows, grad_rows, w_gate, w_up, w_down)
    summed_rows = lax.psum(partial_grad, "exp")
    normed_grad = jnp.dot(
        selector.astype(jnp.float32).T, summed_rows, precision=lax.Precision.HIGHEST
    )
    gained = normed_grad * norm_gain
    inner = jnp.mean(gained * resid_wide, axis=1, keepdims=True)
    resid_grad = (
        out_grad.astype(jnp.float32)
        + rms_scale * (gained - resid_wide * rms_scale * rms_scale * inner)
    ).astype(jnp.bfloat16)
    attn_grad = contract_last(resid_grad, w_out).astype(jnp.bfloat16)
    grad_block = attn_grad.reshape(row_count, head_count, DH)
    query_block = queries.reshape(row_count, head_count, DH)
    kv_index = lax.axis_index("exp") * head_count // GROUP
    own_keys = lax.dynamic_slice_in_dim(keys, kv_index * DH, DH, 1)
    own_values = lax.dynamic_slice_in_dim(values, kv_index * DH, DH, 1)
    keys_all, values_all = (
        lax.all_gather(own_keys, "ctx", axis=0, tiled=True),
        lax.all_gather(own_values, "ctx", axis=0, tiled=True),
    )
    key_pos = (span_order[:, None] * block_rows + lax.iota(jnp.int32, block_rows)[None, :]).reshape(
        -1
    )
    query_pos = lax.dynamic_slice_in_dim(key_pos, lax.axis_index("ctx") * row_count, row_count)
    allowed = key_pos[None, :] <= query_pos[:, None]
    log_total, delta, query_part = softmax_stats(
        query_block, grad_block, keys_all, values_all, allowed, scale
    )
    query_grad = query_part.reshape(row_count, head_count * DH).astype(jnp.bfloat16)
    rows_allowed = key_pos[None, :] <= query_pos[:, None]
    owned = lax.psum_scatter(
        key_term(
            query_block, grad_block, log_total, delta, keys_all, values_all, rows_allowed, scale
        ),
        "ctx",
        scatter_dimension=0,
        tiled=True,
    )
    received = lax.all_to_all(
        owned.reshape(exp_count, slice_rows, 2 * DH), "exp", split_axis=0, concat_axis=0, tiled=True
    )
    summed = head_columns(received, kv_count)
    key_grad = summed[:, : kv_count * DH].astype(jnp.bfloat16)
    value_grad = summed[:, kv_count * DH :].astype(jnp.bfloat16)
    return (resid_grad, query_grad, key_grad, value_grad)


def solution(mesh):
    return jax.shard_map(
        on_device,
        mesh=mesh,
        in_specs=(
            P("ctx", None),
            P("ctx", None),
            P(),
            P("ctx", None),
            P("ctx", None),
            P(None, "exp"),
            P(None, "exp"),
            P("exp", None),
            P("exp", None),
            P("ctx", "exp"),
            P("ctx", None),
            P("ctx", None),
            P(),
        ),
        out_specs=(
            P("ctx", None),
            P("ctx", "exp"),
            P(("ctx", "exp"), None),
            P(("ctx", "exp"), None),
        ),
        check_vma=False,
    )
```

profile of v0, /device:TPU:32, one launch (start us, length us, event | category | flops | bytes accessed | tf_op | source)
XLA Modules:
  0.0 454.3 jit_solution(14953303910813531079)
XLA Ops:
  8.0 0.0 copy-start
  8.0 0.0 all-reduce.2.cloned.1.call-start
  8.1 0.9 fusion.54
  8.9 0.1 copy.58
  9.0 0.2 reduce-window.8
  9.2 0.1 add_reduce_fusion
  9.3 0.0 copy-start.15
  9.3 1.5 fusion.12
  10.9 0.7 select_reduce_fusion
  11.6 1.6 convolution_convert_fusion
  13.2 0.5 fusion.56
  13.7 0.0 copy-done.16
  13.7 0.0 copy-done.15
  13.8 3.1 fusion.16
  16.9 1.9 fusion.20
  18.8 0.0 copy-start.19
  18.9 0.0 copy-start.4
  18.9 1.9 convolution_add_fusion
  20.7 0.0 all-reduce.2.cloned.1.call-update
  20.7 0.0 all-gather.3.cloned.1.call-start
  20.8 0.6 constant_dynamic-slice_fusion.1
  21.5 0.0 all-gather.3.cloned.1.call-update
  21.5 0.0 all-gather.5.cloned.1.call-start
  21.5 0.6 constant_dynamic-slice_fusion
  22.2 0.0 all-gather.5.cloned.1.call-update
  22.2 0.2 reduce-scatter.2.cloned.1.call-start
  22.4 0.1 copy.82
  22.6 0.1 iota_add_fusion
  22.6 0.1 add.80
  22.7 0.1 dynamic_slice.10
  22.8 1.8 broadcast_compare_fusion
  24.7 69.0 %all-reduce.2.cloned.1.call-done = f32[16,4096]{1,0:T(8,128)} async-done(((f32[16,4096]{1,0:T(8,128)}), f32[16,4096]{1,0:T(8,128)}) %all-reduce.2.cloned.1.call-update) | async-done | bytes 262160 | tf_op jit(solution)/shard_map/psum | solution.py:122
  93.6 0.0 copy-done.4
  93.6 2.4 fusion.13
  96.1 0.0 copy-start.8
  96.1 0.7 fusion.11
  96.8 0.0 copy-start.10
  96.8 1.0 copy-done.10
  97.7 0.9 copy-done.8
  98.6 1.5 convolution_convert_fusion.2
  100.2 0.1 copy.83
  100.3 8.5 %all-gather.3.cloned.1.call-done = bf16[4096,128]{1,0:T(8,128)(2,1)} async-done(((bf16[128,128]{1,0:T(8,128)(2,1)}), bf16[4096,128]{1,0:T(8,128)(2,1)}) %all-gather.3.cloned.1.call-update) | async-done | bytes 1048592 | tf_op jit(solution)/shard_map/all_gather | solution.py:139
  108.8 2.5 fusion.55
  111.2 1.1 exponential_reduce_fusion
  112.4 2.1 copy-done.1
  114.5 2.9 convolution_bitcast_fusion
  117.4 71.2 %all-gather.5.cloned.1.call-done = bf16[4096,128]{1,0:T(8,128)(2,1)} async-done(((bf16[128,128]{1,0:T(8,128)(2,1)}), bf16[4096,128]{1,0:T(8,128)(2,1)}) %all-gather.5.cloned.1.call-update) | async-done | bytes 1048592 | tf_op jit(solution)/shard_map/all_gather | solution.py:140
  188.6 5.1 %fusion.15 = f32[4,128]{1,0:T(4,128)S(1)} fusion(f32[4,128,4096]{1,2,0:T(8,128)} %copy-done.1, f32[4,128]{1,0:T(4,128)S(1)} %log_add_fusion, bf16[4096,128]{1,0:T(8,128)(2,1)} %all-gather.5.cloned.1.call-done, bf16[128,4,128]{0,2,1:T(8,128)(2,1)S(1)} %bitcast.68), kind=kOutput, calls=%fused_computation.34 | convolution fusion | flops 541261312 | bytes 9572352 | tf_op jit(solution)/shard_map/hst,td->hsd/dot_general | solution.py:43
  193.7 1.0 copy-done.2
  194.7 0.2 copy-done.7
  194.9 1.9 fusion.1
  196.8 0.0 copy-start.3
  196.8 1.5 fusion.3
  198.3 0.6 copy-done.3
  198.9 1.0 copy-done.5
  199.9 2.3 pad_maximum_fusion
  202.2 0.0 reduce-scatter.2.cloned.1.call-update
  202.2 230.8 %reduce-scatter.2.cloned.1.call-done = f32[128,256]{0,1:T(8,128)} async-done(((f32[4096,256]{0,1:T(8,128)}), f32[128,256]{0,1:T(8,128)}) %reduce-scatter.2.cloned.1.call-update) | async-done | bytes 131088 | tf_op jit(solution)/shard_map/reduce_scatter | solution.py:152
  433.0 1.7 copy.70
  434.7 5.7 %all-to-all-start = ((f32[8,16,256]{2,1,0:T(8,128)}), f32[8,16,256]{2,1,0:T(8,128)S(1)}, u32[]{:S(2)}, u32[]{:S(2)}) async-start(f32[8,16,256]{2,1,0:T(8,128)} %bitcast.12), calls=%async_computation.1 | async-start | bytes 262144 | tf_op jit(solution)/shard_map/all_to_all | solution.py:160
  440.4 2.9 fusion.14
  443.3 0.8 copy.73
  444.1 2.0 all-to-all-done
  446.1 0.6 copy_bitcast_fusion
  (30 shorter events, 0.1 us)
Async XLA Ops:
  8.0 8.9 %copy-start = (bf16[4096,192]{0,1:T(8,128)(2,1)S(1)}, bf16[4096,192]{0,1:T(8,128)(2,1)}, u32[]{:S(2)}) copy-start(bf16[4096,192]{0,1:T(8,128)(2,1)} %param.19) | copy-start | bytes 4718596
  8.0 5.2 %copy-start.6 = (bf16[4096,192]{0,1:T(8,128)(2,1)S(1)}, bf16[4096,192]{0,1:T(8,128)(2,1)}, u32[]{:S(2)}) copy-start(bf16[4096,192]{0,1:T(8,128)(2,1)} %param.18) | copy-start | bytes 4718596
  8.0 85.6 %all-reduce.2.cloned.1.call-start = ((), (), s32[]{:S(2)}) async-start(), calls=%async_computation.2 | async-start | bytes 524288 | tf_op jit(solution)/shard_map/psum | solution.py:122
  8.9 4.8 %copy-start.16 = (pred[128]{0:T(512)(128)(4,1)}, pred[128]{0:T(512)(128)(4,1)S(1)}, u32[]{:S(2)}) copy-start(pred[128]{0:T(512)(128)(4,1)S(1)} %get-tuple-element.20) | copy-start | bytes 388
  9.3 4.4 copy-start.15
  10.9 2.9 copy-start.17
  18.8 2.0 copy-start.13
  18.8 2.7 copy-start.14
  18.8 3.6 copy-start.12
  18.8 3.7 copy-start.19
  18.9 74.8 %copy-start.4 = (bf16[128,4096]{1,0:T(8,128)(2,1)S(1)}, bf16[128,4096]{1,0:T(8,128)(2,1)}, u32[]{:S(2)}) copy-start(bf16[128,4096]{1,0:T(8,128)(2,1)} %param.13) | copy-start | bytes 3145732
  20.7 88.0 %all-gather.3.cloned.1.call-start = ((), (), s32[]{:S(2)}) async-start(), calls=%async_computation.3 | async-start | bytes 1081344 | tf_op jit(solution)/shard_map/all_gather | solution.py:139
  21.5 167.1 %all-gather.5.cloned.1.call-start = ((), (), s32[]{:S(2)}) async-start(), calls=%async_computation.4 | async-start | bytes 1081344 | tf_op jit(solution)/shard_map/all_gather | solution.py:140
  22.2 410.9 %reduce-scatter.2.cloned.1.call-start = ((), (), s32[]{:S(2)}) async-start(), calls=%async_computation.5 | async-start | bytes 4325376 | tf_op jit(solution)/shard_map/reduce_scatter | solution.py:152
  22.6 73.5 %copy-start.18 = (f32[128]{0:T(128)S(1)}, f32[128]{0:T(128)}, u32[]{:S(2)}) copy-start(f32[128]{0:T(128)} %copy-done.17) | copy-start | bytes 1540
  93.6 2.4 copy-start.9
  96.1 2.6 copy-start.8
  96.8 1.0 copy-start.10
  111.2 3.2 copy-start.1
  188.6 6.1 %copy-start.2 = (f32[4,128,4096]{1,2,0:T(8,128)S(1)}, f32[4,128,4096]{1,2,0:T(8,128)}, u32[]{:S(2)}) copy-start(f32[4,128,4096]{1,2,0:T(8,128)} %copy-done.1) | copy-start | bytes 25165828
  188.6 6.3 %copy-start.7 = (bf16[4096,128]{1,0:T(8,128)(2,1)S(1)}, bf16[4096,128]{1,0:T(8,128)(2,1)}, u32[]{:S(2)}) copy-start(bf16[4096,128]{1,0:T(8,128)(2,1)} %all-gather.5.cloned.1.call-done) | copy-start | bytes 3145732
  196.8 2.1 copy-start.3
  196.8 3.1 copy-start.5
  202.2 238.2 %copy-start.11 = (bf16[4096,128]{1,0:T(8,128)(2,1)S(1)}, bf16[4096,128]{1,0:T(8,128)(2,1)}, u32[]{:S(2)}) copy-start(bf16[4096,128]{1,0:T(8,128)(2,1)} %all-gather.3.cloned.1.call-done) | copy-start | bytes 3145732
  434.7 11.4 %all-to-all-start = ((f32[8,16,256]{2,1,0:T(8,128)}), f32[8,16,256]{2,1,0:T(8,128)S(1)}, u32[]{:S(2)}, u32[]{:S(2)}) async-start(f32[8,16,256]{2,1,0:T(8,128)} %bitcast.12), calls=%async_computation.1 | async-start | bytes 262144 | tf_op jit(solution)/shard_map/all_to_all | solution.py:160
Sparse Core Ops, SparseCore 0:
  20.9 72.7 all-reduce.1
Sparse Core Ops, SparseCore 1:
  25.8 82.9 all-gather.2
  112.6 76.0 all-gather.4
  202.3 230.7 reduce-scatter.1
where the time goes:
time: 456 us; the launch traced here: 454 us
  waiting for transfers between devices  382 us (84%)
  matrix products  29.8 us (7%)
  between operations  16 us (4%)
  local copies, waits for them, and re-layouts  11.6 us (3%)
  other arithmetic  9.39 us (2%)
  starting transfers between devices  6.05 us (1%)
    reduce_scatter x1, waiting for transfers between devices, on_device(): lax.psum_scatter(key_term(query_block, grad_block, log_total, delta, keys...  231 us
    all_gather x1, waiting for transfers between devices, on_device(): lax.all_gather(own_values, 'ctx', axis=0, tiled=True)  71.2 us
    psum x1, waiting for transfers between devices, on_device(): summed_rows = lax.psum(partial_grad, 'exp')  69 us
  transfers between devices with their start and end apart: 5, of which 5 were waited for; matrix products, arithmetic and copies ran while one was open for 4% of the time, Pallas kernels for 0%

commit v1 on v0

v1 whole, which is shorter than its diff:
```python
import math

import jax
import jax.numpy as jnp
from jax import lax
from jax.sharding import PartitionSpec as P

DH = 128
GROUP = 16
CAP = 16
EPS = 1e-06
LOW = -1e30

bf16 = jnp.bfloat16
f32 = jnp.float32


def contract_last(left, right):
    return lax.dot_general(left, right, (((1,), (1,)), ((), ())), preferred_element_type=f32)


def contract_first(left, right):
    return lax.dot_general(left, right, (((0,), (0,)), ((), ())), preferred_element_type=f32)


def dot(left, right):
    return jnp.dot(left, right, preferred_element_type=f32)


def across(array, mask):
    count = lax.axis_size("exp")
    return lax.ppermute(array, "exp", [(i, i ^ mask) for i in range(count)])


def on_device(
    resid,
    out_grad,
    norm_gain,
    expert_ids,
    combine,
    w_gate,
    w_up,
    w_down,
    w_out,
    queries,
    keys,
    values,
    span_order,
):
    rows, width = resid.shape
    heads = queries.shape[1] // DH
    n_ctx = lax.axis_size("ctx")
    n_exp = lax.axis_size("exp")
    ctx, exp = lax.axis_index("ctx"), lax.axis_index("exp")
    core, z_lo = exp % 2, exp // 2
    chunk = rows // n_exp
    n_z = n_exp // 2
    block = rows // 2
    scale = 1.0 / math.sqrt(DH)

    kv_index = exp * heads // GROUP
    own_kv = jnp.concatenate(
        [
            lax.dynamic_slice_in_dim(keys, kv_index * DH, DH, 1),
            lax.dynamic_slice_in_dim(values, kv_index * DH, DH, 1),
        ],
        axis=1,
    ).reshape(n_z, 2, chunk, 2 * DH)
    mine = jnp.where(core == 0, own_kv[:, 0], own_kv[:, 1]).reshape(n_z * chunk, 2 * DH)
    sent = jnp.broadcast_to(mine[None], (n_ctx,) + mine.shape)
    kv = lax.all_to_all(sent, "ctx", 0, 0, tiled=True).reshape(-1, 2 * DH)
    k_all, v_all = kv[:, :DH], kv[:, DH:]
    q_own = queries
    q_par = across(queries, 1)

    chosen = jnp.any(expert_ids == 0, axis=1)
    weight = jnp.sum(jnp.where(expert_ids == 0, combine, 0.0), axis=1)
    rank = jnp.cumsum(chosen.astype(jnp.int32)) - 1
    slots = lax.iota(jnp.int32, CAP)
    picks = (rank[None, :] == slots[:, None]) & chosen[None, :]
    selector = picks.astype(bf16)
    weight16 = jnp.sum(jnp.where(picks, weight[None, :], 0.0), axis=1, keepdims=True)
    resid16 = dot(selector, resid)
    grad16 = dot(selector, out_grad)
    rms16 = lax.rsqrt(jnp.mean(resid16 * resid16, axis=1, keepdims=True) + EPS)
    normed16 = (resid16 * rms16 * norm_gain).astype(bf16)
    scaled16 = (grad16 * weight16).astype(bf16)
    gate_pre = dot(normed16, w_gate)
    up_pre = dot(normed16, w_up)
    hidden = contract_last(scaled16, w_down)
    sig = jax.nn.sigmoid(gate_pre)
    gate_grad = (hidden * up_pre * sig * (1.0 + gate_pre * (1.0 - sig))).astype(bf16)
    up_grad = (hidden * gate_pre * sig).astype(bf16)
    partial = contract_last(gate_grad, w_gate) + contract_last(up_grad, w_up)

    half = width // 2
    left, right = partial[:, :half], partial[:, half:]
    keep = jnp.where(core == 0, left, right)
    give = jnp.where(core == 0, right, left).astype(bf16)
    pair = lax.optimization_barrier((keep + across(give, 1).astype(f32)).astype(bf16))
    r1, r2, r3 = across(pair, 2), across(pair, 4), across(pair, 6)
    total = (pair.astype(f32) + r1.astype(f32)) + (r2.astype(f32) + r3.astype(f32))
    total = lax.optimization_barrier(total.astype(bf16))
    other = across(total, 1)
    normed_grad = jnp.concatenate(
        [jnp.where(core == 0, total, other), jnp.where(core == 0, other, total)], axis=1
    ).astype(f32)
    gained = normed_grad * norm_gain
    inner = jnp.mean(gained * resid16, axis=1, keepdims=True)
    rows16 = (grad16 + rms16 * (gained - resid16 * rms16 * rms16 * inner)).astype(bf16)

    base_own = contract_last(out_grad, w_out).astype(bf16)
    base_par = across(base_own, 1)
    late_own = contract_last(rows16, w_out).astype(bf16)
    late_par = across(late_own, 1)
    resid_grad = jnp.where(
        chosen[:, None], contract_first(selector, rows16).astype(bf16), out_grad
    )
    d_own = jnp.where(chosen[:, None], contract_first(selector, late_own).astype(bf16), base_own)
    d_par = jnp.where(chosen[:, None], contract_first(selector, late_par).astype(bf16), base_par)

    def by_head(own, par):
        both = jnp.concatenate([own, par], axis=1)
        return both.reshape(rows, 2 * heads, DH).swapaxes(0, 1).reshape(2 * heads * rows, DH)

    spans = span_order.reshape(n_ctx, 2)
    place = lax.iota(jnp.int32, rows)
    row_pos = spans[:, :, None] * block + lax.iota(jnp.int32, block)
    query_pos = lax.dynamic_index_in_dim(row_pos, ctx, 0, keepdims=False).reshape(rows)
    split_pos = row_pos.reshape(n_ctx, n_z, 2, chunk)
    key_pos = jnp.where(core == 0, split_pos[:, :, 0], split_pos[:, :, 1]).reshape(-1)
    allowed = key_pos[None, :] <= query_pos[:, None]
    n_keys = key_pos.shape[0]
    q = by_head(q_own, q_par)
    scores = contract_last(q, k_all) * scale
    scores = jnp.where(
        allowed[None], scores.reshape(2 * heads, rows, n_keys), LOW
    )
    top = jnp.max(scores, axis=2)
    weights = jnp.exp(scores - top[..., None])
    mass = jnp.sum(weights, axis=2)
    out_part = dot(weights.astype(bf16).reshape(-1, n_keys), v_all).reshape(2 * heads, rows, DH)
    stats = jnp.stack([top, mass])
    stats_par = across(jnp.concatenate([stats[:, heads:], stats[:, :heads]], axis=1), 1)
    out_low = out_part.astype(bf16)
    out_par = across(jnp.concatenate([out_low[heads:], out_low[:heads]], axis=0), 1)
    peak = jnp.maximum(top, stats_par[0])
    near, far = jnp.exp(top - peak), jnp.exp(stats_par[0] - peak)
    inverse = 1.0 / (mass * near + stats_par[1] * far)
    out = (out_part * (near * inverse)[..., None]) + out_par.astype(f32) * (far * inverse)[..., None]
    probs = weights * (near * inverse)[..., None]
    probs_low = probs.astype(bf16).reshape(-1, n_keys)

    d = by_head(d_own, d_par)
    delta = jnp.sum(d.astype(f32) * out.reshape(-1, DH), axis=1)
    prob_grad = contract_last(d, v_all)
    score_grad = (probs.reshape(-1, n_keys) * (prob_grad - delta[:, None])).astype(bf16)
    key_part = contract_first(score_grad, q) * scale
    value_part = contract_first(probs_low, d)
    kv_part = jnp.concatenate([key_part, value_part], axis=1).astype(bf16)
    got = lax.all_to_all(
        kv_part.reshape(n_ctx, n_z * chunk, 2 * DH), "ctx", 0, 0, tiled=True
    )
    query_part = (dot(score_grad, k_all) * scale).reshape(2 * heads, rows, DH).swapaxes(0, 1)
    query_part = query_part.reshape(rows, 2 * heads * DH)
    query_give = query_part[:, heads * DH :].astype(bf16)
    query_grad = (query_part[:, : heads * DH] + across(query_give, 1).astype(f32)).astype(bf16)

    owned = jnp.sum(got.astype(f32), axis=0).reshape(n_z, chunk, 2 * DH)

    def chunk_of(index):
        return lax.dynamic_index_in_dim(owned, index, 0, keepdims=False)

    same = chunk_of(z_lo) + across(chunk_of(z_lo ^ 1), 2)
    rest = across(chunk_of(z_lo ^ 2), 4) + across(chunk_of(z_lo ^ 3), 6)
    first = jnp.where(z_lo < n_z // 2, same, rest)
    second = jnp.where(z_lo < n_z // 2, rest, same)
    key_grad = jnp.concatenate([first[:, :DH], second[:, :DH]], axis=1).astype(bf16)
    value_grad = jnp.concatenate([first[:, DH:], second[:, DH:]], axis=1).astype(bf16)
    return (resid_grad, query_grad, key_grad, value_grad)


def solution(mesh):
    return jax.shard_map(
        on_device,
        mesh=mesh,
        in_specs=(
            P("ctx", None),
            P("ctx", None),
            P(),
            P("ctx", None),
            P("ctx", None),
            P(None, "exp"),
            P(None, "exp"),
            P("exp", None),
            P("exp", None),
            P("ctx", "exp"),
            P("ctx", None),
            P("ctx", None),
            P(),
        ),
        out_specs=(
            P("ctx", None),
            P("ctx", "exp"),
            P(("ctx", "exp"), None),
            P(("ctx", "exp"), None),
        ),
        check_vma=False,
    )
```

time: 456 us -> 167 us (0.37)
  waiting for transfers between devices: 382 us -> 44.7 us
  starting transfers between devices: 6.05 us -> 37.3 us
  other arithmetic: 9.39 us -> 24.3 us
  between operations: 16 us -> 1.21 us
  local copies, waits for them, and re-layouts: 11.6 us -> 20.5 us
  matrix products: 29.8 us -> 36.7 us
    reduce_scatter x1 -> x0, waiting for transfers between devices: 231 us -> none  [on_device(): lax.psum_scatter(key_term(query_block, grad_block, log_total, delta, keys...]
    all_gather x2 -> x0, waiting for transfers between devices: 79.7 us -> none  [the longest x1 71.2 us: on_device(): lax.all_gather(own_values, 'ctx', axis=0, tiled=True)]
    psum x1 -> x0, waiting for transfers between devices: 69 us -> none  [on_device(): summed_rows = lax.psum(partial_grad, 'exp')]
    ppermute x0 -> x14, waiting for transfers between devices: none -> 22 us  [across(): return lax.ppermute(array, 'exp', [(i, i ^ mask) for i in range(count)])]
    all_to_all x1 -> x2, waiting for transfers between devices: 1.96 us -> 22.7 us  [the longest x1 22.7 us: on_device(): lax.all_to_all(kv_part.reshape(n_ctx, n_z * chunk, 2 * DH), 'ctx', 0, 0,...]
    all_to_all x1 -> x2, starting transfers between devices: 5.7 us -> 25.2 us  [the longest x1 13.2 us: on_device(): kv = lax.all_to_all(sent, 'ctx', 0, 0, tiled=True).reshape(-1, 2 * DH)]
    dot_general x4 -> x7, matrix products: 8.43 us -> 21.1 us  [contract_last(): lax.dot_general(left, right, (((1,), (1,)), ((), ())), preferred_element_...]
    ppermute x0 -> x14, starting transfers between devices: none -> 12.1 us  [across(): return lax.ppermute(array, 'exp', [(i, i ^ mask) for i in range(count)])]
  transfers between devices with their start and end apart: 5 -> 16, of which waited for: 5 -> 5; matrix products, arithmetic and copies ran while one was open for 4% -> 33% of each run, Pallas kernels for 0% -> 0%
where the time goes in v1:
time: 167 us; the launch traced here: 165 us
  waiting for transfers between devices  44.7 us (27%)
  starting transfers between devices  37.3 us (22%)
  matrix products  36.7 us (22%)
  other arithmetic  24.3 us (15%)
  local copies, waits for them, and re-layouts  20.5 us (12%)
    all_to_all x1, waiting for transfers between devices, on_device(): lax.all_to_all(kv_part.reshape(n_ctx, n_z * chunk, 2 * DH), 'ctx', 0, 0,...  22.7 us
    ppermute x14, waiting for transfers between devices, across(): return lax.ppermute(array, 'exp', [(i, i ^ mask) for i in range(count)])  22 us
    dot_general x7, matrix products, contract_last(): lax.dot_general(left, right, (((1,), (1,)), ((), ())), preferred_element_...  21.1 us
    all_to_all x1, starting transfers between devices, on_device(): kv = lax.all_to_all(sent, 'ctx', 0, 0, tiled=True).reshape(-1, 2 * DH)  13.2 us
    ppermute x14, starting transfers between devices, across(): return lax.ppermute(array, 'exp', [(i, i ^ mask) for i in range(count)])  12.1 us
    all_to_all x1, starting transfers between devices, on_device(): lax.all_to_all(kv_part.reshape(n_ctx, n_z * chunk, 2 * DH), 'ctx', 0, 0,...  12.1 us
    dot_general x5, matrix products, dot(): return jnp.dot(left, right, preferred_element_type=f32)  9.33 us
    reshape x1, local copies, waits for them, and re-layouts, on_device(): scores.reshape(2 * heads, rows, n_keys)  9.27 us
  transfers between devices with their start and end apart: 16, of which 5 were waited for; matrix products, arithmetic and copies ran while one was open for 33% of the time, Pallas kernels for 0%

profile of v1, /device:TPU:32, one launch (start us, length us, event | category | flops | bytes accessed | tf_op | source)
XLA Modules:
  0.0 164.8 jit_solution(15557839464152580796)
XLA Ops:
  0.7 4.8 %convolution_convert_fusion.2 = bf16[128,512]{1,0:T(8,128)(2,1)} fusion(bf16[128,4096]{1,0:T(8,128)(2,1)} %param.14, bf16[512,4096]{1,0:T(8,128)(2,1)} %param.21), kind=kOutput, calls=%fused_computation.20 | convolution fusion | flops 536936448 | bytes 5373952 | tf_op jit(solution)/shard_map/dot_general | solution.py:19
  5.7 0.6 collective-permute-start.5
  6.4 0.2 reduce-window.8
  6.7 0.2 fusion.40
  7.1 1.7 %multiply_reduce_fusion.2 = (f32[16]{0:T(128)S(1)}, f32[16,4096]{1,0:T(8,128)S(1)}) fusion(bf16[128,4096]{1,0:T(8,128)(2,1)} %param.13, s32[128]{0:T(128)S(1)} %add_reduce_fusion, pred[128]{0:T(512)(128)(4,1)S(1)} %reduce_or.9), kind=kOutput, calls=%fused_computation.51 | convolution fusion | flops 16912368 | bytes 1311424 | tf_op jit(solution)/shard_map/dot_general | solution.py:27
  8.8 1.9 %fusion.26 = f32[16,192]{1,0:T(8,128)S(1)} fusion(bf16[192,4096]{1,0:T(8,128)(2,1)} %param.20, f32[16,4096]{1,0:T(8,128)S(1)} %fusion.40, f32[16]{0:T(128)S(1)} %select_reduce_fusion), kind=kOutput, calls=%fused_computation.52 | convolution fusion | flops 25296896 | bytes 1847360 | tf_op jit(solution)/shard_map/dot_general | solution.py:19
  10.8 0.5 fusion.68
  11.4 0.6 copy-done.11
  12.0 2.6 %fusion.18 = f32[16,4096]{1,0:T(8,128)S(1)} fusion(bf16[4096,192]{0,1:T(8,128)(2,1)} %param.18, f32[16,192]{1,0:T(8,128)S(1)} %fusion.26, bf16[4096,192]{0,1:T(8,128)(2,1)S(1)} %copy-done, f32[16,192]{1,0:T(8,128)S(1)} %fusion.68, f32[16,4096]{1,0:T(8,128)S(1)} %get-tuple-element.24, f32[4096]{0:T(1024)S(1)} %copy-done.9, f32[16]{0:T(128)S(1)} %add_rsqrt_fusion), kind=kOutput, calls=%fused_computation.29 | convolution fusion | flops 50558976 | bytes 3711040 | tf_op jit(solution)/shard_map/dot_general | solution.py:19
  14.6 1.1 convolution_add_fusion
  15.8 0.8 constant_dynamic-slice_fusion
  16.7 1.1 broadcast_in_dim.81
  17.7 13.2 %all-to-all-start = ((bf16[32,64,256]{2,1,0:T(8,128)(2,1)}), bf16[32,64,256]{2,1,0:T(8,128)(2,1)}, u32[]{:S(2)}, u32[]{:S(2)}) async-start(bf16[32,64,256]{2,1,0:T(8,128)(2,1)} %broadcast_in_dim.81), calls=%async_computation | async-start | bytes 2097152 | tf_op jit(solution)/shard_map/all_to_all | solution.py:71
  30.9 0.7 broadcast_multiply_fusion
  32.1 0.6 le.20
  32.8 0.7 select_n.139
  33.5 1.5 add_convert_fusion.2
  34.9 1.0 collective-permute-start.3
  36.0 2.4 %collective-permute-start.2 = (bf16[16,2048]{1,0:T(8,128)(2,1)}, bf16[16,2048]{1,0:T(8,128)(2,1)}, u32[]{:S(2)}, u32[]{:S(2)}) collective-permute-start(bf16[16,2048]{1,0:T(8,128)(2,1)} %add_convert_fusion.2), channel_id=1, source_target_pairs={{0,4},{1,5},{2,6},{3,7},{4,0},{5,1},{6,2},{7,3},{8,12},{9,13},{10,... | collective-permute-start | bytes 196616 | tf_op jit(solution)/shard_map/ppermute | solution.py:32
  38.4 1.0 broadcast_compare_fusion
  39.5 0.4 copy.73
  39.9 12.7 %collective-permute-done.3 = bf16[16,2048]{1,0:T(8,128)(2,1)} collective-permute-done((bf16[16,2048]{1,0:T(8,128)(2,1)}, bf16[16,2048]{1,0:T(8,128)(2,1)}, u32[]{:S(2)}, u32[]{:S(2)}) %collective-permute-start.3) | collective-permute-done | bytes 65568 | tf_op jit(solution)/shard_map/ppermute | solution.py:32
  52.6 6.8 %collective-permute-done.2 = bf16[16,2048]{1,0:T(8,128)(2,1)} collective-permute-done((bf16[16,2048]{1,0:T(8,128)(2,1)}, bf16[16,2048]{1,0:T(8,128)(2,1)}, u32[]{:S(2)}, u32[]{:S(2)}) %collective-permute-start.2) | collective-permute-done | bytes 65568 | tf_op jit(solution)/shard_map/ppermute | solution.py:32
  59.4 1.6 add_convert_fusion.1
  61.0 1.6 pad_maximum_fusion.1
  62.6 1.8 %copy.58 = bf16[8,128,128]{2,1,0:T(8,128)(2,1)} copy(bf16[8,128,128]{1,2,0:T(8,128)(2,1)} %bitcast.157) | data formatting | bytes 524288 | tf_op jit(solution)/shard_map/transpose | solution.py:124
  64.4 0.9 broadcast_select_fusion.1
  65.3 0.2 multiply_reduce_fusion.1
  65.5 1.1 add_convert_fusion
  66.6 3.4 %convolution_convert_fusion.4 = bf16[16,512]{1,0:T(8,128)(2,1)S(1)} fusion(bf16[16,4096]{1,0:T(8,128)(2,1)S(1)} %add_convert_fusion, bf16[512,4096]{1,0:T(8,128)(2,1)} %param.21), kind=kOutput, calls=%fused_computation.24 | convolution fusion | flops 67117056 | bytes 4341760 | tf_op jit(solution)/shard_map/dot_general | solution.py:19
  70.0 0.7 collective-permute-start.7
  70.6 1.1 fusion.13
  71.8 1.1 fusion.14
  72.9 0.7 pad_maximum_fusion.2
  73.7 1.1 copy.69
  74.8 0.9 copy.60
  75.7 2.8 %fusion = (f32[1024]{0:T(1024)S(1)}, f32[1024,2048]{1,0:T(8,128)S(1)}) fusion(pred[128,2048]{1,0:T(8,128)(4,1)S(1)} %copy.73, bf16[1024,128]{1,0:T(8,128)(2,1)} %bitcast.154, bf16[2048,256]{1,0:T(8,128)(2,1)} %bitcast.9), kind=kOutput, calls=%fused_computation.4 | convolution fusion | flops 543161344 | bytes 9441280 | tf_op jit(solution)/shard_map/dot_general | solution.py:19
  78.4 2.7 %fusion.2 = (f32[1024]{0:T(1024)S(1)}, bf16[1024,2048]{1,0:T(8,128)(2,1)S(1)}) fusion(f32[1024,2048]{1,0:T(8,128)S(1)} %get-tuple-element.26, f32[1024]{0:T(1024)S(1)} %get-tuple-element.25, pred[128,2048]{1,0:T(8,128)(4,1)S(1)} %copy.73), kind=kLoop, calls=%fused_computation.6 | loop fusion | flops 8387584 | bytes 12853248 | tf_op jit(solution)/shard_map/reduce_sum | solution.py:141
  81.1 0.6 copy-done.1
  81.7 3.4 %fusion.72 = (bf16[8,128,128]{1,2,0:T(8,128)(2,1)S(1)}, f32[8,128,128]{1,2,0:T(8,128)}) fusion(bf16[8,128,2048]{2,1,0:T(8,128)(2,1)S(1)} %bitcast.148, bf16[2048,256]{1,0:T(8,128)(2,1)} %bitcast.9), kind=kOutput, calls=%fused_computation.136 | convolution fusion | flops 537001984 | bytes 5505024 | tf_op jit(solution)/shard_map/dot_general | solution.py:27
  85.1 0.6 fusion.31
  85.7 0.7 pad_maximum_fusion.3
  86.4 0.5 collective-permute-start.9
  86.9 9.3 %copy.63 = f32[8,128,2048]{1,0,2:T(8,128)} copy(f32[8,128,2048]{2,1,0:T(8,128)} %bitcast.145) | data formatting | bytes 16777216 | tf_op jit(solution)/shard_map/reshape | solution.py:137
  96.2 4.8 %multiply_convert_fusion = bf16[8,128,2048]{1,0,2:T(8,128)(2,1)S(1)} fusion(f32[8,128,2048]{1,0,2:T(8,128)} %copy.63, f32[8,128]{1,0:T(8,128)S(1)} %get-tuple-element.17, f32[8,128]{1,0:T(8,128)S(1)} %bitcast.162, pred[128,2048]{0,1:T(8,128)(4,1)S(1)} %broadcast_compare_fusion), kind=kLoop, calls=%fused_computation | loop fusion | flops 8388608 | bytes 12853248 | tf_op jit(solution)/shard_map/convert_element_type | solution.py:152
  101.1 1.3 fusion.10
  102.3 1.1 multiply_reduce_fusion
  103.5 4.4 %multiply_convert_fusion.1 = bf16[1024,2048]{1,0:T(8,128)(2,1)S(1)} fusion(f32[1024,2048]{1,0:T(8,128)S(1)} %bitcast.147, bf16[1024,128]{1,0:T(8,128)(2,1)S(1)} %bitcast.156, f32[1024]{0:T(1024)S(1)} %bitcast.169, f32[1024]{0:T(1024)S(1)} %fusion.47, f32[1024]{0:T(1024)S(1)} %get-tuple-element.25, pred[128,2048]{1,0:T(8,128)(4,1)S(1)} %copy.73, ...), kind=kOutput, calls=%fused_computation.1 | convolution fusion | flops 549453824 | bytes 13643776 | tf_op jit(solution)/shard_map/dot_general | solution.py:19
  107.9 1.9 %copy-done.4 = bf16[1024,2048]{1,0:T(8,128)(2,1)} copy-done((bf16[1024,2048]{1,0:T(8,128)(2,1)}, bf16[1024,2048]{1,0:T(8,128)(2,1)S(1)}, u32[]{:S(2)}) %copy-start.4) | copy-done | bytes 4194328
  109.9 1.3 fusion.6
  111.2 1.1 pad_maximum_fusion
  112.4 12.1 %all-to-all-start.1 = ((bf16[32,64,256]{2,1,0:T(8,128)(2,1)}), bf16[32,64,256]{2,1,0:T(8,128)(2,1)}, u32[]{:S(2)}, u32[]{:S(2)}) async-start(bf16[32,64,256]{2,1,0:T(8,128)(2,1)} %pad_maximum_fusion), calls=%async_computation.1 | async-start | bytes 2097152 | tf_op jit(solution)/shard_map/all_to_all | solution.py:161
  124.5 1.5 fusion.3
  125.9 3.5 %convolution_multiply_fusion.2 = f32[1024,128]{1,0:T(8,128)S(1)} fusion(bf16[1024,2048]{1,0:T(8,128)(2,1)} %copy-done.4, bf16[2048,256]{1,0:T(8,128)(2,1)} %bitcast.9), kind=kOutput, calls=%fused_computation.18 | convolution fusion | flops 537001984 | bytes 5242880 | tf_op jit(solution)/shard_map/dot_general | solution.py:27
  129.7 22.7 %all-to-all-done.1 = bf16[32,64,256]{2,1,0:T(8,128)(2,1)} async-done(((bf16[32,64,256]{2,1,0:T(8,128)(2,1)}), bf16[32,64,256]{2,1,0:T(8,128)(2,1)}, u32[]{:S(2)}, u32[]{:S(2)}) %all-to-all-start.1) | async-done | bytes 1048608 | tf_op jit(solution)/shard_map/all_to_all | solution.py:161
  152.3 1.4 convert_reduce_fusion
  153.7 4.1 %collective-permute-start.11 = (f32[16,256]{1,0:T(8,128)S(1)}, f32[16,256]{1,0:T(8,128)S(1)}, u32[]{:S(2)}, u32[]{:S(2)}) collective-permute-start(f32[16,256]{1,0:T(8,128)S(1)} %get-tuple-element.14), channel_id=1, source_target_pairs={{0,2},{1,3},{2,0},{3,1},{4,6},{5,7},{6,4},{7,5},{8,10},{9,11},{10,... | collective-permute-start | bytes 49160 | tf_op jit(solution)/shard_map/ppermute | solution.py:32
  157.9 1.0 collective-permute-start.13
  158.9 1.5 collective-permute-start.12
  160.3 0.7 fusion.25
  161.0 0.6 collective-permute-done.13
  161.6 1.9 %collective-permute-done.12 = f32[16,256]{1,0:T(8,128)S(1)} collective-permute-done((f32[16,256]{1,0:T(8,128)S(1)}, f32[16,256]{1,0:T(8,128)S(1)}, u32[]{:S(2)}, u32[]{:S(2)}) %collective-permute-start.12) | collective-permute-done | bytes 16416 | tf_op jit(solution)/shard_map/ppermute | solution.py:32
  163.6 0.6 pad_maximum_fusion.8
  164.2 0.6 pad_maximum_fusion.7
  (96 shorter events, 1.7 us)
Async XLA Ops:
  0.6 11.3 %copy-start = (bf16[4096,192]{0,1:T(8,128)(2,1)S(1)}, bf16[4096,192]{0,1:T(8,128)(2,1)}, u32[]{:S(2)}) copy-start(bf16[4096,192]{0,1:T(8,128)(2,1)} %param.19) | copy-start | bytes 4718596
  0.6 6.1 %copy-start.2 = (bf16[128,4096]{1,0:T(8,128)(2,1)S(1)}, bf16[128,4096]{1,0:T(8,128)(2,1)}, u32[]{:S(2)}) copy-start(bf16[128,4096]{1,0:T(8,128)(2,1)} %param.14) | copy-start | bytes 3145732
  0.7 4.9 %copy-start.12 = (bf16[128,512]{1,0:T(8,128)(2,1)S(1)}, bf16[128,512]{1,0:T(8,128)(2,1)}, u32[]{:S(2)}) copy-start(bf16[128,512]{1,0:T(8,128)(2,1)} %param.22) | copy-start | bytes 393220
  0.7 5.6 %copy-start.20 = (f32[128,8]{0,1:T(8,128)S(1)}, f32[128,8]{0,1:T(8,128)}, u32[]{:S(2)}) copy-start(f32[128,8]{0,1:T(8,128)} %param.17) | copy-start | bytes 12292
  0.7 5.6 %copy-start.21 = (s32[128,8]{0,1:T(8,128)S(1)}, s32[128,8]{0,1:T(8,128)}, u32[]{:S(2)}) copy-start(s32[128,8]{0,1:T(8,128)} %param.16) | copy-start | bytes 12292
  0.7 10.1 %copy-start.9 = (f32[4096]{0:T(1024)S(1)}, f32[4096]{0:T(1024)}, u32[]{:S(2)}) copy-start(f32[4096]{0:T(1024)} %param.15) | copy-start | bytes 49156
  5.5 66.2 %collective-permute-start.8 = (bf16[128,512]{1,0:T(8,128)(2,1)}, bf16[128,512]{1,0:T(8,128)(2,1)}, u32[]{:S(2)}, u32[]{:S(2)}) collective-permute-start(bf16[128,512]{1,0:T(8,128)(2,1)} %convolution_convert_fusion.2), channel_id=1, source_target_pairs={{0,1},{1,0},{2,3},{3,2},{4,5},{5,4},{6,7},{7,6},{8,9},{9,8},{10,11... | collective-permute-start | bytes 393224 | tf_op jit(solution)/shard_map/ppermute | solution.py:32
  5.7 55.3 %collective-permute-start.5 = (bf16[128,512]{0,1:T(8,128)(2,1)S(1)}, bf16[128,512]{0,1:T(8,128)(2,1)}, u32[]{:S(2)}, u32[]{:S(2)}) collective-permute-start(bf16[128,512]{0,1:T(8,128)(2,1)S(1)} %copy.57), channel_id=1, source_target_pairs={{0,1},{1,0},{2,3},{3,2},{4,5},{5,4},{6,7},{7,6},{8,9},{9,8},{10,11... | collective-permute-start | bytes 393224 | tf_op jit(solution)/shard_map/ppermute | solution.py:32
  6.3 2.5 %copy-start.16 = (pred[128]{0:T(512)(128)(4,1)}, pred[128]{0:T(512)(128)(4,1)S(1)}, u32[]{:S(2)}) copy-start(pred[128]{0:T(512)(128)(4,1)S(1)} %reduce_or.9) | copy-start | bytes 388
  6.6 4.2 %copy-start.3 = (bf16[4096,192]{0,1:T(8,128)(2,1)S(1)}, bf16[4096,192]{0,1:T(8,128)(2,1)}, u32[]{:S(2)}) copy-start(bf16[4096,192]{0,1:T(8,128)(2,1)} %param.18) | copy-start | bytes 4718596
  6.7 2.0 %copy-start.13 = (s32[128]{0:T(128)}, s32[128]{0:T(128)S(1)}, u32[]{:S(2)}) copy-start(s32[128]{0:T(128)S(1)} %add_reduce_fusion) | copy-start | bytes 1540
  7.0 1.8 %copy-start.5 = (f32[16,4096]{1,0:T(8,128)}, f32[16,4096]{1,0:T(8,128)S(1)}, u32[]{:S(2)}) copy-start(f32[16,4096]{1,0:T(8,128)S(1)} %fusion.40) | copy-start | bytes 786436
  8.8 2.5 %copy-start.19 = (f32[16]{0:T(128)}, f32[16]{0:T(128)S(1)}, u32[]{:S(2)}) copy-start(f32[16]{0:T(128)S(1)} %add_rsqrt_fusion) | copy-start | bytes 196
  10.7 0.6 copy-start.10
  11.4 0.6 copy-start.11
  15.7 17.7 %collective-permute-start = (bf16[16,2048]{1,0:T(8,128)(2,1)S(1)}, bf16[16,2048]{1,0:T(8,128)(2,1)}, u32[]{:S(2)}, u32[]{:S(2)}) collective-permute-start(bf16[16,2048]{1,0:T(8,128)(2,1)S(1)} %select_convert_fusion), channel_id=1, source_target_pairs={{0,1},{1,0},{2,3},{3,2},{4,5},{5,4},{6,7},{7,6},{8,9},{9,8},{10,11... | collective-permute-start | bytes 196616 | tf_op jit(solution)/shard_map/ppermute | solution.py:32
  17.7 57.9 %all-to-all-start = ((bf16[32,64,256]{2,1,0:T(8,128)(2,1)}), bf16[32,64,256]{2,1,0:T(8,128)(2,1)}, u32[]{:S(2)}, u32[]{:S(2)}) async-start(bf16[32,64,256]{2,1,0:T(8,128)(2,1)} %broadcast_in_dim.81), calls=%async_computation | async-start | bytes 2097152 | tf_op jit(solution)/shard_map/all_to_all | solution.py:71
  34.9 17.6 %collective-permute-start.3 = (bf16[16,2048]{1,0:T(8,128)(2,1)}, bf16[16,2048]{1,0:T(8,128)(2,1)}, u32[]{:S(2)}, u32[]{:S(2)}) collective-permute-start(bf16[16,2048]{1,0:T(8,128)(2,1)} %add_convert_fusion.2), channel_id=1, source_target_pairs={{0,6},{1,7},{2,4},{3,5},{4,2},{5,3},{6,0},{7,1},{8,14},{9,15},{10,... | collective-permute-start | bytes 196616 | tf_op jit(solution)/shard_map/ppermute | solution.py:32
  36.0 23.4 %collective-permute-start.2 = (bf16[16,2048]{1,0:T(8,128)(2,1)}, bf16[16,2048]{1,0:T(8,128)(2,1)}, u32[]{:S(2)}, u32[]{:S(2)}) collective-permute-start(bf16[16,2048]{1,0:T(8,128)(2,1)} %add_convert_fusion.2), channel_id=1, source_target_pairs={{0,4},{1,5},{2,6},{3,7},{4,0},{5,1},{6,2},{7,3},{8,12},{9,13},{10,... | collective-permute-start | bytes 196616 | tf_op jit(solution)/shard_map/ppermute | solution.py:32
  38.3 21.1 %collective-permute-start.1 = (bf16[16,2048]{1,0:T(8,128)(2,1)}, bf16[16,2048]{1,0:T(8,128)(2,1)}, u32[]{:S(2)}, u32[]{:S(2)}) collective-permute-start(bf16[16,2048]{1,0:T(8,128)(2,1)} %add_convert_fusion.2), channel_id=1, source_target_pairs={{0,2},{1,3},{2,0},{3,1},{4,6},{5,7},{6,4},{7,5},{8,10},{9,11},{10,... | collective-permute-start | bytes 196616 | tf_op jit(solution)/shard_map/ppermute | solution.py:32
  61.0 3.4 %collective-permute-start.4 = (bf16[16,2048]{1,0:T(8,128)(2,1)}, bf16[16,2048]{1,0:T(8,128)(2,1)}, u32[]{:S(2)}, u32[]{:S(2)}) collective-permute-start(bf16[16,2048]{1,0:T(8,128)(2,1)} %add_convert_fusion.1), channel_id=1, source_target_pairs={{0,1},{1,0},{2,3},{3,2},{4,5},{5,4},{6,7},{7,6},{8,9},{9,8},{10,11... | collective-permute-start | bytes 196616 | tf_op jit(solution)/shard_map/ppermute | solution.py:32
  64.4 6.2 %copy-start.14 = (s32[128]{0:T(128)S(1)}, s32[128]{0:T(128)}, u32[]{:S(2)}) copy-start(s32[128]{0:T(128)} %copy-done.13) | copy-start | bytes 1540
  64.4 6.2 %copy-start.17 = (pred[128]{0:T(512)(128)(4,1)S(1)}, pred[128]{0:T(512)(128)(4,1)}, u32[]{:S(2)}) copy-start(pred[128]{0:T(512)(128)(4,1)} %copy-done.16) | copy-start | bytes 388
  70.0 1.8 %collective-permute-start.7 = (bf16[16,512]{1,0:T(8,128)(2,1)S(1)}, bf16[16,512]{1,0:T(8,128)(2,1)S(1)}, u32[]{:S(2)}, u32[]{:S(2)}) collective-permute-start(bf16[16,512]{1,0:T(8,128)(2,1)S(1)} %convolution_convert_fusion.4), channel_id=1, source_target_pairs={{0,1},{1,0},{2,3},{3,2},{4,5},{5,4},{6,7},{7,6},{8,9},{9,8},{10,11... | collective-permute-start | bytes 49160 | tf_op jit(solution)/shard_map/ppermute | solution.py:32
  78.4 3.3 %copy-start.1 = (f32[1024,2048]{1,0:T(8,128)}, f32[1024,2048]{1,0:T(8,128)S(1)}, u32[]{:S(2)}) copy-start(f32[1024,2048]{1,0:T(8,128)S(1)} %get-tuple-element.26) | copy-start | bytes 25165828
  85.7 10.5 %collective-permute-start.6 = (f32[2,8,128]{2,1,0:T(8,128)}, f32[2,8,128]{2,1,0:T(8,128)S(1)}, u32[]{:S(2)}, u32[]{:S(2)}) collective-permute-start(f32[2,8,128]{2,1,0:T(8,128)} %fusion.31), channel_id=1, source_target_pairs={{0,1},{1,0},{2,3},{3,2},{4,5},{5,4},{6,7},{7,6},{8,9},{9,8},{10,11... | collective-permute-start | bytes 24584 | tf_op jit(solution)/shard_map/ppermute | solution.py:32
  86.4 15.9 %collective-permute-start.9 = (bf16[8,128,128]{1,2,0:T(8,128)(2,1)}, bf16[8,128,128]{1,2,0:T(8,128)(2,1)}, u32[]{:S(2)}, u32[]{:S(2)}) collective-permute-start(bf16[8,128,128]{1,2,0:T(8,128)(2,1)} %pad_maximum_fusion.3), channel_id=1, source_target_pairs={{0,1},{1,0},{2,3},{3,2},{4,5},{5,4},{6,7},{7,6},{8,9},{9,8},{10,11... | collective-permute-start | bytes 786440 | tf_op jit(solution)/shard_map/ppermute | solution.py:32
  96.2 7.3 %slice-start = ((s8[8388608]{0:T(1024)(128)(4,1)}), s8[4194304]{0:T(1024)(128)(4,1)S(1)}, s32[]{:S(2)}) async-start(s8[8388608]{0:T(1024)(128)(4,1)} %bitcast.146), calls=%async_computation.2 | async-start | bytes 8388608
  96.2 7.3 %slice-start.1 = ((s8[8388608]{0:T(1024)(128)(4,1)}), s8[4194304]{0:T(1024)(128)(4,1)S(1)}, s32[]{:S(2)}) async-start(s8[8388608]{0:T(1024)(128)(4,1)} %bitcast.146), calls=%async_computation.3 | async-start | bytes 8388608
  101.0 1.3 copy-start.6
  101.0 2.4 %copy-start.8 = (bf16[8,128,128]{2,1,0:T(8,128)(2,1)S(1)}, bf16[8,128,128]{2,1,0:T(8,128)(2,1)}, u32[]{:S(2)}) copy-start(bf16[8,128,128]{2,1,0:T(8,128)(2,1)} %copy.60) | copy-start | bytes 786436
  103.5 6.4 %copy-start.7 = (bf16[8,128,128]{2,1,0:T(8,128)(2,1)S(1)}, bf16[8,128,128]{2,1,0:T(8,128)(2,1)}, u32[]{:S(2)}) copy-start(bf16[8,128,128]{2,1,0:T(8,128)(2,1)} %copy.58) | copy-start | bytes 786436
  107.9 1.9 %copy-start.4 = (bf16[1024,2048]{1,0:T(8,128)(2,1)}, bf16[1024,2048]{1,0:T(8,128)(2,1)S(1)}, u32[]{:S(2)}) copy-start(bf16[1024,2048]{1,0:T(8,128)(2,1)S(1)} %multiply_convert_fusion.1) | copy-start | bytes 12582916
  109.9 14.6 %copy-start.15 = (s32[128]{0:T(128)S(1)}, s32[128]{0:T(128)}, u32[]{:S(2)}) copy-start(s32[128]{0:T(128)} %copy-done.13) | copy-start | bytes 1540
  109.9 14.6 %copy-start.18 = (pred[128]{0:T(512)(128)(4,1)S(1)}, pred[128]{0:T(512)(128)(4,1)}, u32[]{:S(2)}) copy-start(pred[128]{0:T(512)(128)(4,1)} %copy-done.16) | copy-start | bytes 388
  112.4 40.0 %all-to-all-start.1 = ((bf16[32,64,256]{2,1,0:T(8,128)(2,1)}), bf16[32,64,256]{2,1,0:T(8,128)(2,1)}, u32[]{:S(2)}, u32[]{:S(2)}) async-start(bf16[32,64,256]{2,1,0:T(8,128)(2,1)} %pad_maximum_fusion), calls=%async_computation.1 | async-start | bytes 2097152 | tf_op jit(solution)/shard_map/all_to_all | solution.py:161
  129.6 30.8 %collective-permute-start.10 = (bf16[128,512]{1,0:T(8,128)(2,1)S(1)}, bf16[128,512]{1,0:T(8,128)(2,1)S(1)}, u32[]{:S(2)}, u32[]{:S(2)}) collective-permute-start(bf16[128,512]{1,0:T(8,128)(2,1)S(1)} %slice.155), channel_id=1, source_target_pairs={{0,1},{1,0},{2,3},{3,2},{4,5},{5,4},{6,7},{7,6},{8,9},{9,8},{10,11... | collective-permute-start | bytes 393224 | tf_op jit(solution)/shard_map/ppermute | solution.py:32
  153.7 7.3 %collective-permute-start.11 = (f32[16,256]{1,0:T(8,128)S(1)}, f32[16,256]{1,0:T(8,128)S(1)}, u32[]{:S(2)}, u32[]{:S(2)}) collective-permute-start(f32[16,256]{1,0:T(8,128)S(1)} %get-tuple-element.14), channel_id=1, source_target_pairs={{0,2},{1,3},{2,0},{3,1},{4,6},{5,7},{6,4},{7,5},{8,10},{9,11},{10,... | collective-permute-start | bytes 49160 | tf_op jit(solution)/shard_map/ppermute | solution.py:32
  157.9 3.7 %collective-permute-start.13 = (f32[16,256]{1,0:T(8,128)S(1)}, f32[16,256]{1,0:T(8,128)S(1)}, u32[]{:S(2)}, u32[]{:S(2)}) collective-permute-start(f32[16,256]{1,0:T(8,128)S(1)} %get-tuple-element.15), channel_id=1, source_target_pairs={{0,6},{1,7},{2,4},{3,5},{4,2},{5,3},{6,0},{7,1},{8,14},{9,15},{10,... | collective-permute-start | bytes 49160 | tf_op jit(solution)/shard_map/ppermute | solution.py:32
  158.9 4.6 %collective-permute-start.12 = (f32[16,256]{1,0:T(8,128)S(1)}, f32[16,256]{1,0:T(8,128)S(1)}, u32[]{:S(2)}, u32[]{:S(2)}) collective-permute-start(f32[16,256]{1,0:T(8,128)S(1)} %get-tuple-element.16), channel_id=1, source_target_pairs={{0,4},{1,5},{2,6},{3,7},{4,0},{5,1},{6,2},{7,3},{8,12},{9,13},{10,... | collective-permute-start | bytes 49160 | tf_op jit(solution)/shard_map/ppermute | solution.py:32

commit v2 on v1

v2 whole, which is shorter than its diff:
```python
import functools
import math

import jax
import jax.numpy as jnp
from jax import lax
from jax.experimental import pallas as pl
from jax.experimental.pallas import tpu as pltpu
from jax.sharding import Mesh, PartitionSpec as P

DH = 128
GROUP = 16
CAP = 16
EPS = 1e-06
LOW = -1e30
KEYS = 256
CTX = ("y", "hi", "x")
EXP = ("lo", "core")

bf16 = jnp.bfloat16
f32 = jnp.float32
SMEM = pl.BlockSpec(memory_space=pltpu.SMEM)
VMEM = pl.BlockSpec(memory_space=pltpu.VMEM)
HBM = pl.BlockSpec(memory_space=pl.ANY)


def product(left, right, left_dim=1, right_dim=0):
    return lax.dot_general(
        left, right, (((left_dim,), (right_dim,)), ((), ())), preferred_element_type=f32
    )


def params(mib):
    return pltpu.CompilerParams(vmem_limit_bytes=mib << 20)


def cost(flops, moved):
    return pl.CostEstimate(flops=flops, bytes_accessed=moved, transcendentals=0)


def shape(dims, dtype):
    return jax.ShapeDtypeStruct(dims, dtype)


def expert_kernel(
    place, ids, combine, gain, resid, out_grad, w_gate, w_up, w_down,
    give, keep, selector, resid16, grad16,
    resid_in, grad_in, gate_in, up_in, down_in, sems,
):
    copies = [
        pltpu.make_async_copy(source, target, sems.at[i])
        for i, (source, target) in enumerate(
            [(resid, resid_in), (out_grad, grad_in), (w_gate, gate_in), (w_up, up_in), (w_down, down_in)]
        )
    ]
    for copy in copies:
        copy.start()
    rows = ids.shape[1]
    hit = ids[...] == 0
    chosen_row = jnp.sum(jnp.where(hit, 1.0, 0.0), axis=0, keepdims=True)
    weight_row = jnp.sum(jnp.where(hit, combine[...], 0.0), axis=0, keepdims=True)
    before = lax.broadcasted_iota(jnp.int32, (rows, rows), 0)
    after = lax.broadcasted_iota(jnp.int32, (rows, rows), 1)
    upper = jnp.where(before <= after, 1.0, 0.0).astype(bf16)
    spread = jnp.broadcast_to(chosen_row, (CAP, rows)).astype(bf16)
    rank_row = product(spread, upper)
    slot = lax.broadcasted_iota(jnp.int32, (CAP, rows), 0).astype(f32) + 1.0
    picks = (rank_row == slot) & (chosen_row > 0.0)
    pick = jnp.where(picks, 1.0, 0.0).astype(bf16)
    selector[...] = pick
    weight16 = jnp.sum(jnp.where(picks, weight_row, 0.0), axis=1, keepdims=True)
    copies[0].wait()
    rows16 = product(pick, resid_in[...])
    resid16[...] = rows16.astype(bf16)
    rms16 = lax.rsqrt(jnp.mean(rows16 * rows16, axis=1, keepdims=True) + EPS)
    normed16 = (rows16 * rms16 * gain[...]).astype(bf16)
    copies[1].wait()
    taken = product(pick, grad_in[...])
    grad16[...] = taken.astype(bf16)
    scaled16 = (taken * weight16).astype(bf16)
    copies[2].wait()
    gate_pre = product(normed16, gate_in[...], 1, 1)
    copies[3].wait()
    up_pre = product(normed16, up_in[...], 1, 1)
    copies[4].wait()
    hidden = product(scaled16, down_in[...], 1, 1)
    sig = jax.nn.sigmoid(gate_pre)
    gate_grad = (hidden * up_pre * sig * (1.0 + gate_pre * (1.0 - sig))).astype(bf16)
    up_grad = (hidden * gate_pre * sig).astype(bf16)
    half = give.shape[1]
    first = product(gate_grad, gate_in[:, :half]) + product(up_grad, up_in[:, :half])
    second = product(gate_grad, gate_in[:, half:]) + product(up_grad, up_in[:, half:])
    low = place[1] == 0
    keep[...] = jnp.where(low, first, second)
    give[...] = jnp.where(low, second, first).astype(bf16)


def late_kernel(place, total, other, resid16, grad16, gain, w_out, rows16, late, out_in, sems):
    n = sems.shape[0]
    step = w_out.shape[0] // n
    copies = [
        pltpu.make_async_copy(
            w_out.at[pl.ds(i * step, step)], out_in.at[pl.ds(i * step, step)], sems.at[i]
        )
        for i in range(n)
    ]
    for copy in copies:
        copy.start()
    low = place[1] == 0
    first, second = total[...].astype(f32), other[...].astype(f32)
    left, right = jnp.where(low, first, second), jnp.where(low, second, first)
    gained = jnp.concatenate([left, right], axis=1) * gain[...]
    wide = resid16[...].astype(f32)
    rms = lax.rsqrt(jnp.mean(wide * wide, axis=1, keepdims=True) + EPS)
    inner = jnp.mean(gained * wide, axis=1, keepdims=True)
    done = (grad16[...].astype(f32) + rms * (gained - wide * rms * rms * inner)).astype(bf16)
    rows16[...] = done
    for i in range(n):
        copies[i].wait()
        part = product(done, out_in[i * step : (i + 1) * step], 1, 1)
        late[:, i * step : (i + 1) * step] = part.astype(bf16)


def base_kernel(w_out, out_grad, base, total):
    @pl.when(pl.program_id(0) == 0)
    def _():
        total[...] = jnp.zeros_like(total)

    total[...] += product(w_out[...], out_grad[...], 1, 1)

    @pl.when(pl.program_id(0) == pl.num_programs(0) - 1)
    def _():
        base[...] = total[...].astype(bf16)


def resid_kernel(selector, rows16, out_grad, resid_grad):
    pick = selector[...]
    chosen = product(pick, jnp.ones((CAP, 128), bf16), 0, 0)[:, :1] > 0.5
    moved = product(pick, rows16[...], 0, 0)
    resid_grad[...] = jnp.where(chosen, moved, out_grad[...].astype(f32)).astype(bf16)


def stack_heads(target, own, par):
    rows, heads = own.shape[0], own.shape[1] // DH
    for h in range(heads):
        target[h * rows : (h + 1) * rows] = own[:, h * DH : (h + 1) * DH]
        target[(h + heads) * rows : (h + heads + 1) * rows] = par[:, h * DH : (h + 1) * DH]


def forward_kernel(chunk, n_hi, n_x, place, spans, q_own, q_par, kv, weights, stats, q_all, held, top):
    phase, step = pl.program_id(0), pl.program_id(1)
    rows = q_own.shape[0]
    block = rows // 2
    columns = q_all.shape[0]
    factor = math.log2(math.e) / math.sqrt(DH)
    at = pl.ds(pl.multiple_of(step * KEYS, KEYS), KEYS)

    @pl.when((phase == 0) & (step == 0))
    def _():
        stack_heads(q_all, q_own, q_par)
        top[...] = jnp.full_like(top, 2.0 * LOW)

    @pl.when(phase == 0)
    def _():
        lane = lax.broadcasted_iota(jnp.int32, (chunk, rows), 1)
        below = lax.broadcasted_iota(jnp.int32, (chunk, rows), 0)
        here = place[0] * 2
        query_pos = jnp.where(
            lane < block, spans[here] * block + lane, spans[here + 1] * block + lane - block
        )
        per_ctx = block // chunk
        pieces = []
        for g in range(KEYS // chunk):
            held_by, i = step * (KEYS // block) + g // per_ctx, g % per_ctx
            plane, high = held_by // n_hi, held_by % n_hi
            ctx = (plane // n_x * n_hi + high) * n_x + plane % n_x
            offset = (2 * i + place[1]) * chunk
            span = spans[2 * ctx + (2 * i * chunk) // block]
            key_pos = span * block + offset % block + below
            pieces.append(jnp.where(key_pos <= query_pos, 0.0, LOW))
        bias = jnp.concatenate(pieces, axis=0)
        bias = jnp.concatenate([bias, bias], axis=1)
        key = kv[:, :DH]
        for c in range(0, columns, 2 * rows):
            score = product(key, q_all[c : c + 2 * rows], 1, 1) * factor + bias
            held[at, c : c + 2 * rows] = score
            top[:, c : c + 2 * rows] = jnp.maximum(
                top[:, c : c + 2 * rows], jnp.max(score, axis=0, keepdims=True)
            )

    @pl.when((phase == 1) & (step == 0))
    def _():
        stats[...] = jnp.zeros_like(stats)
        stats[DH : DH + 1] = top[...]

    @pl.when(phase == 1)
    def _():
        value = kv[:, DH:]
        for c in range(0, columns, 2 * rows):
            weight = jnp.exp2(held[at, c : c + 2 * rows] - top[:, c : c + 2 * rows])
            stats[DH + 1 : DH + 2, c : c + 2 * rows] += jnp.sum(weight, axis=0, keepdims=True)
            weight = weight.astype(bf16)
            weights[:, c : c + 2 * rows] = weight
            stats[:DH, c : c + 2 * rows] += product(value, weight, 0, 0)


def backward_kernel(
    q_own, q_par, base_own, base_par, late_own, late_par, selector, mine, theirs, kv, weights,
    kv_part, score_grad, q_all, grads, delta,
):
    rows, heads = q_own.shape[0], q_own.shape[1] // DH
    columns = q_all.shape[0]
    wide = heads * rows
    scale = 1.0 / math.sqrt(DH)

    @pl.when(pl.program_id(0) == 0)
    def _():
        stack_heads(q_all, q_own, q_par)
        pick = selector[...]
        chosen = jnp.sum(pick.astype(f32), axis=0, keepdims=True) > 0.5
        for side, (base, late) in enumerate([(base_own, late_own), (base_par, late_par)]):
            moved = product(late[...], pick, 0, 0)
            merged = jnp.where(chosen, moved, base[...].astype(f32))
            here, there = side * wide, (1 - side) * wide
            top, mass = mine[DH : DH + 1, here : here + wide], mine[DH + 1 : DH + 2, here : here + wide]
            far_top = theirs[DH : DH + 1, there : there + wide]
            far_mass = theirs[DH + 1 : DH + 2, there : there + wide]
            peak = jnp.maximum(top, far_top)
            near, far = jnp.exp2(top - peak), jnp.exp2(far_top - peak)
            inverse = 1.0 / (mass * near + far_mass * far)
            near, far = near * inverse, far * inverse
            out = mine[:DH, here : here + wide] * near + theirs[:DH, there : there + wide] * far
            for h in range(heads):
                part = merged[h * DH : (h + 1) * DH]
                c = slice(h * rows, (h + 1) * rows)
                to = slice(here + h * rows, here + (h + 1) * rows)
                delta[:, to] = near[:, c] * jnp.sum(part * out[:, c], axis=0, keepdims=True)
                grads[:, to] = (part * near[:, c]).astype(bf16)

    key, value = kv[:, :DH], kv[:, DH:]
    for c in range(0, columns, 2 * rows):
        prob_grad = product(value, grads[:, c : c + 2 * rows])
        weight = weights[:, c : c + 2 * rows].astype(f32)
        score_grad[:, c : c + 2 * rows] = (
            weight * (prob_grad - delta[:, c : c + 2 * rows])
        ).astype(bf16)
    kv_part[:, DH:] = product(weights[...], grads[...], 1, 1).astype(bf16)
    kv_part[:, :DH] = (product(score_grad[...], q_all[...]) * scale).astype(bf16)


def query_kernel(kv, score_grad, own, par, total):
    step = pl.program_id(0)

    @pl.when(step == 0)
    def _():
        total[...] = jnp.zeros_like(total)

    total[...] += product(kv[:, :DH], score_grad[...], 0, 0)

    @pl.when(step == pl.num_programs(0) - 1)
    def _():
        rows, heads = own.shape[0], own.shape[1] // DH
        scale = 1.0 / math.sqrt(DH)
        for h in range(heads):
            to = slice(h * DH, (h + 1) * DH)
            own[:, to] = total[:, h * rows : (h + 1) * rows].T * scale
            there = h + heads
            par[:, to] = (total[:, there * rows : (there + 1) * rows].T * scale).astype(bf16)


def across(array, axis, mask=1):
    count = lax.axis_size(axis)
    return lax.ppermute(array, axis, [(i, i ^ mask) for i in range(count)])


def on_device(
    resid, out_grad, norm_gain, expert_ids, combine, w_gate, w_up, w_down, w_out,
    queries, keys, values, span_order,
):
    rows, width = resid.shape
    heads = queries.shape[1] // DH
    hidden = w_gate.shape[1]
    n_y, n_x, n_hi, n_lo = (lax.axis_size(axis) for axis in ("y", "x", "hi", "lo"))
    exp, core, high = lax.axis_index(("lo", "core")), lax.axis_index("core"), lax.axis_index("hi")
    chunk = rows // (2 * n_lo)
    half = width // 2
    columns = 2 * heads * rows
    n_keys = n_y * n_x * n_hi * n_lo * chunk
    steps = n_keys // KEYS
    place = jnp.stack([lax.axis_index(CTX), core]).astype(jnp.int32)
    gain = norm_gain[None, :]

    kv_index = exp * heads // GROUP
    own_kv = jnp.concatenate(
        [
            lax.dynamic_slice_in_dim(keys, kv_index * DH, DH, 1),
            lax.dynamic_slice_in_dim(values, kv_index * DH, DH, 1),
        ],
        axis=1,
    ).reshape(n_lo, 2, chunk, 2 * DH)
    near_kv = jnp.where(core == 0, own_kv[:, 0], own_kv[:, 1]).reshape(n_lo * chunk, 2 * DH)
    far_kv = across(near_kv, "hi")
    plane_kv = jnp.where(
        high == 0, jnp.stack([near_kv, far_kv]), jnp.stack([far_kv, near_kv])
    )
    sent = jnp.broadcast_to(plane_kv[None], (n_y * n_x,) + plane_kv.shape)
    kv = lax.all_to_all(sent, ("y", "x"), 0, 0, tiled=True).reshape(-1, 2 * DH)
    q_par = across(queries, "core")

    give, keep, selector, resid16, grad16 = pl.pallas_call(
        expert_kernel,
        out_shape=(
            shape((CAP, half), bf16),
            shape((CAP, half), f32),
            shape((CAP, rows), bf16),
            shape((CAP, width), bf16),
            shape((CAP, width), bf16),
        ),
        in_specs=[SMEM, VMEM, VMEM, VMEM] + [HBM] * 5,
        out_specs=(VMEM,) * 5,
        scratch_shapes=[
            pltpu.VMEM((rows, width), bf16),
            pltpu.VMEM((rows, width), bf16),
            pltpu.VMEM((hidden, width), bf16),
            pltpu.VMEM((hidden, width), bf16),
            pltpu.VMEM((hidden, width), bf16),
            pltpu.SemaphoreType.DMA((5,)),
        ],
        compiler_params=params(24),
        cost_estimate=cost(10 * CAP * width * hidden, 8 << 20),
        name="expert",
    )(place, expert_ids.T, combine.T, gain, resid, out_grad, w_gate.T, w_up.T, w_down)

    pair = lax.optimization_barrier((keep + across(give, "core").astype(f32)).astype(bf16))
    r1, r2, r3 = across(pair, "lo", 1), across(pair, "lo", 2), across(pair, "lo", 3)
    total = (pair.astype(f32) + r1.astype(f32)) + (r2.astype(f32) + r3.astype(f32))
    total = lax.optimization_barrier(total.astype(bf16))
    other = across(total, "core")
    rows16, late_own = pl.pallas_call(
        late_kernel,
        out_shape=(shape((CAP, width), bf16), shape((CAP, heads * DH), bf16)),
        in_specs=[SMEM] + [VMEM] * 5 + [HBM],
        out_specs=(VMEM, VMEM),
        scratch_shapes=[
            pltpu.VMEM((heads * DH, width), bf16),
            pltpu.SemaphoreType.DMA((2,)),
        ],
        compiler_params=params(24),
        cost_estimate=cost(2 * CAP * width * heads * DH, 5 << 20),
        name="late",
    )(place, total, other, resid16, grad16, gain, w_out)
    late_par = across(late_own, "core")

    cut = 4
    base_own = pl.pallas_call(
        base_kernel,
        grid=(cut,),
        out_shape=shape((heads * DH, rows), bf16),
        in_specs=[
            pl.BlockSpec((heads * DH, width // cut), lambda i: (0, i)),
            pl.BlockSpec((rows, width // cut), lambda i: (0, i)),
        ],
        out_specs=pl.BlockSpec((heads * DH, rows), lambda i: (0, 0)),
        scratch_shapes=[pltpu.VMEM((heads * DH, rows), f32)],
        compiler_params=params(24),
        cost_estimate=cost(2 * rows * width * heads * DH, 5 << 20),
        name="base",
    )(w_out, out_grad)
    base_par = across(base_own, "core")
    resid_grad = pl.pallas_call(
        resid_kernel,
        grid=(cut,),
        out_shape=shape((rows, width), bf16),
        in_specs=[
            pl.BlockSpec((CAP, rows), lambda i: (0, 0)),
            pl.BlockSpec((CAP, width // cut), lambda i: (0, i)),
            pl.BlockSpec((rows, width // cut), lambda i: (0, i)),
        ],
        out_specs=pl.BlockSpec((rows, width // cut), lambda i: (0, i)),
        compiler_params=params(24),
        cost_estimate=cost(2 * rows * width * CAP, 2 << 20),
        name="resid",
    )(selector, rows16, out_grad)

    whole = lambda *_: (0, 0)
    query_spec = pl.BlockSpec((rows, heads * DH), whole)
    pair_flops = 2 * n_keys * columns * DH
    weights, mine = pl.pallas_call(
        functools.partial(forward_kernel, chunk, n_hi, n_x),
        grid=(2, steps),
        out_shape=(shape((n_keys, columns), bf16), shape((DH + 8, columns), f32)),
        in_specs=[
            SMEM,
            SMEM,
            query_spec,
            query_spec,
            pl.BlockSpec((KEYS, 2 * DH), lambda p, j: (j, 0)),
        ],
        out_specs=(
            pl.BlockSpec((KEYS, columns), lambda p, j: (j * p, 0)),
            pl.BlockSpec((DH + 8, columns), whole),
        ),
        scratch_shapes=[
            pltpu.VMEM((columns, DH), bf16),
            pltpu.VMEM((n_keys, columns), f32),
            pltpu.VMEM((1, columns), f32),
        ],
        compiler_params=params(24),
        cost_estimate=cost(2 * pair_flops, 6 << 20),
        name="forward",
    )(place, span_order, queries, q_par, kv)
    theirs = across(mine, "core")
    kv_part, score_grad = pl.pallas_call(
        backward_kernel,
        grid=(steps,),
        out_shape=(shape((n_keys, 2 * DH), bf16), shape((n_keys, columns), bf16)),
        in_specs=[
            query_spec,
            query_spec,
            pl.BlockSpec((heads * DH, rows), whole),
            pl.BlockSpec((heads * DH, rows), whole),
            pl.BlockSpec((CAP, heads * DH), whole),
            pl.BlockSpec((CAP, heads * DH), whole),
            pl.BlockSpec((CAP, rows), whole),
            pl.BlockSpec((DH + 8, columns), whole),
            pl.BlockSpec((DH + 8, columns), whole),
            pl.BlockSpec((KEYS, 2 * DH), lambda j: (j, 0)),
            pl.BlockSpec((KEYS, columns), lambda j: (j, 0)),
        ],
        out_specs=(
            pl.BlockSpec((KEYS, 2 * DH), lambda j: (j, 0)),
            pl.BlockSpec((KEYS, columns), lambda j: (j, 0)),
        ),
        scratch_shapes=[
            pltpu.VMEM((columns, DH), bf16),
            pltpu.VMEM((DH, columns), bf16),
            pltpu.VMEM((1, columns), f32),
        ],
        compiler_params=params(24),
        cost_estimate=cost(3 * pair_flops, 10 << 20),
        name="backward",
    )(
        queries, q_par, base_own, base_par, late_own, late_par, selector, mine, theirs, kv, weights,
    )
    got = lax.all_to_all(
        kv_part.reshape(n_y * n_x, n_hi * n_lo * chunk, 2 * DH), ("y", "x"), 0, 0, tiled=True
    )
    query_spec = pl.BlockSpec((rows, heads * DH), whole)
    query_own, query_give = pl.pallas_call(
        query_kernel,
        grid=(steps,),
        out_shape=(shape((rows, heads * DH), f32), shape((rows, heads * DH), bf16)),
        in_specs=[
            pl.BlockSpec((KEYS, 2 * DH), lambda j: (j, 0)),
            pl.BlockSpec((KEYS, columns), lambda j: (j, 0)),
        ],
        out_specs=(query_spec, query_spec),
        scratch_shapes=[pltpu.VMEM((DH, columns), f32)],
        compiler_params=params(24),
        cost_estimate=cost(pair_flops, 6 << 20),
        name="query",
    )(kv, score_grad)
    query_grad = (query_own + across(query_give, "core").astype(f32)).astype(bf16)

    owned = jnp.sum(got.astype(f32), axis=0).astype(bf16)
    owned = owned.reshape(n_hi * n_lo, chunk, 2 * DH)
    parts = lax.all_to_all(owned, ("hi", "lo"), 0, 0, tiled=True).astype(f32)
    parts = parts.reshape(n_hi, 2, n_lo // 2, chunk, 2, DH)
    summed = jnp.sum(parts, axis=(0, 2)).transpose(2, 1, 0, 3).reshape(2, chunk, 2 * DH)
    summed = summed.astype(bf16)
    key_grad, value_grad = summed[0], summed[1]
    return (resid_grad, query_grad, key_grad, value_grad)


def solution(mesh):
    fine = Mesh(mesh.devices.reshape(4, 2, 4, 4, 2), ("y", "hi", "x", "lo", "core"))
    return jax.shard_map(
        on_device,
        mesh=fine,
        in_specs=(
            P(CTX, None),
            P(CTX, None),
            P(),
            P(CTX, None),
            P(CTX, None),
            P(None, EXP),
            P(None, EXP),
            P(EXP, None),
            P(EXP, None),
            P(CTX, EXP),
            P(CTX, None),
            P(CTX, None),
            P(),
        ),
        out_specs=(
            P(CTX, None),
            P(CTX, EXP),
            P(CTX + EXP, None),
            P(CTX + EXP, None),
        ),
        check_vma=False,
    )
```

time: 167 us -> 107 us (0.64)
  matrix products: 36.7 us -> 0 us
  Pallas kernels: 0 us -> 28.1 us
  waiting for transfers between devices: 44.7 us -> 22 us
  other arithmetic: 24.3 us -> 3.75 us
  local copies, waits for them, and re-layouts: 20.5 us -> 15.9 us
  starting transfers between devices: 37.3 us -> 35.2 us
    dot_general x17 -> x0, matrix products: 36.7 us -> none  [the longest x7 21.1 us: contract_last(): lax.dot_general(left, right, (((1,), (1,)), ((), ())), preferred_element_...]
    pallas_call x0 -> x7, Pallas kernels: none -> 28.1 us  [the longest x1 6.4 us: on_device(): pl.pallas_call(functools.partial(forward_kernel, chunk, n_hi, n_x), grid=...]
    ppermute x14 -> x11, waiting for transfers between devices: 22 us -> 4.9 us  [across(): return lax.ppermute(array, axis, [(i, i ^ mask) for i in range(count)])]
    reshape x3 -> x1, local copies, waits for them, and re-layouts: 10.4 us -> 0.02 us  [on_device(): parts = parts.reshape(n_hi, 2, n_lo // 2, chunk, 2, DH)]
    unnamed x50 -> x33, local copies, waits for them, and re-layouts: 3.79 us -> 13.9 us
    convert_element_type x6 -> x2, other arithmetic: 8.07 us -> 0.7 us  [the longest x1 0.68 us: on_device(): (query_own + across(query_give, 'core').astype(f32)).astype(bf16)]
    concatenate x7 -> x0, other arithmetic: 6.03 us -> none  [the longest x2 2.37 us: by_head(): both = jnp.concatenate([own, par], axis=1)]
    all_to_all x2 -> x3, waiting for transfers between devices: 22.7 us -> 17.1 us  [the longest x1 10.8 us: on_device(): lax.all_to_all(kv_part.reshape(n_y * n_x, n_hi * n_lo * chunk, 2 * DH), (...]
  transfers between devices with their start and end apart: 16 -> 14, of which waited for: 5 -> 6; matrix products, arithmetic and copies ran while one was open for 33% -> 3% of each run, Pallas kernels for 0% -> 21%
where the time goes in v2:
time: 107 us; the launch traced here: 106 us
  starting transfers between devices  35.2 us (33%)
  Pallas kernels  28.1 us (26%)
  waiting for transfers between devices  22 us (21%)
  local copies, waits for them, and re-layouts  15.9 us (15%)
  other arithmetic  3.75 us (4%)
    unnamed x33, local copies, waits for them, and re-layouts  13.9 us
    ppermute x11, starting transfers between devices, across(): return lax.ppermute(array, axis, [(i, i ^ mask) for i in range(count)])  11.7 us
    all_to_all x1, waiting for transfers between devices, on_device(): lax.all_to_all(kv_part.reshape(n_y * n_x, n_hi * n_lo * chunk, 2 * DH), (...  10.8 us
    all_to_all x1, starting transfers between devices, on_device(): parts = lax.all_to_all(owned, ('hi', 'lo'), 0, 0, tiled=True).astype(f32)  9.09 us
    all_to_all x1, starting transfers between devices, on_device(): lax.all_to_all(kv_part.reshape(n_y * n_x, n_hi * n_lo * chunk, 2 * DH), (...  7.27 us
    all_to_all x1, starting transfers between devices, on_device(): kv = lax.all_to_all(sent, ('y', 'x'), 0, 0, tiled=True).reshape(-1, 2 * DH)  7.17 us
    pallas_call x1, Pallas kernels, on_device(): pl.pallas_call(functools.partial(forward_kernel, chunk, n_hi, n_x), grid=...  6.4 us
    all_to_all x1, waiting for transfers between devices, on_device(): parts = lax.all_to_all(owned, ('hi', 'lo'), 0, 0, tiled=True).astype(f32)  6.23 us
  transfers between devices with their start and end apart: 14, of which 6 were waited for; matrix products, arithmetic and copies ran while one was open for 3% of the time, Pallas kernels for 21%

profile of v2, /device:TPU:32, one launch (start us, length us, event | category | flops | bytes accessed | tf_op | source)
XLA Modules:
  0.0 105.8 jit_solution(1370280638922769673)
XLA Ops:
  0.6 0.0 copy-start.8
  0.6 0.0 copy-start.2
  0.7 0.9 constant_dynamic-slice_fusion
  1.6 6.4 %collective-permute-start.5 = (bf16[64,256]{1,0:T(8,128)(2,1)S(1)}, bf16[64,256]{1,0:T(8,128)(2,1)S(1)}, u32[]{:S(2)}, u32[]{:S(2)}) collective-permute-start(bf16[64,256]{1,0:T(8,128)(2,1)S(1)} %bitcast.37), channel_id=1, source_target_pairs={{0,32},{32,0},{1,33},{33,1},{2,34},{34,2},{3,35},{35,3},{4,36},{36... | collective-permute-start | bytes 98312 | tf_op jit(solution)/shard_map/ppermute | solution.py:273
  8.0 1.9 %collective-permute-done.5 = bf16[64,256]{1,0:T(8,128)(2,1)S(1)} collective-permute-done((bf16[64,256]{1,0:T(8,128)(2,1)S(1)}, bf16[64,256]{1,0:T(8,128)(2,1)S(1)}, u32[]{:S(2)}, u32[]{:S(2)}) %collective-permute-start.5) | collective-permute-done | bytes 32800 | tf_op jit(solution)/shard_map/ppermute | solution.py:273
  9.9 1.1 %broadcast_in_dim.10 = bf16[16,2,64,256]{3,2,1,0:T(8,128)(2,1)} broadcast(bf16[2,64,256]{2,1,0:T(8,128)(2,1)S(1)} %maximum_select_fusion), dimensions={1,2,3} | broadcast | bytes 1114112 | tf_op jit(solution)/shard_map/broadcast_in_dim | solution.py:306
  11.0 7.2 %all-to-all-start = ((bf16[16,2,64,256]{3,2,1,0:T(8,128)(2,1)}), bf16[16,2,64,256]{3,2,1,0:T(8,128)(2,1)S(1)}, u32[]{:S(2)}, u32[]{:S(2)}) async-start(bf16[16,2,64,256]{3,2,1,0:T(8,128)(2,1)} %broadcast_in_dim.10), calls=%async_computation | async-start | bytes 2097152 | tf_op jit(solution)/shard_map/all_to_all | solution.py:307
  18.2 0.1 pad_add_fusion.place
  18.3 0.0 copy-done.8
  18.3 0.0 copy-done.2
  18.3 1.4 %copy-done.5 = bf16[4096,192]{0,1:T(8,128)(2,1)S(1)} copy-done((bf16[4096,192]{0,1:T(8,128)(2,1)S(1)}, bf16[4096,192]{0,1:T(8,128)(2,1)}, u32[]{:S(2)}) %copy-start.5) | copy-done | bytes 1572888
  19.7 1.4 %copy-done.6 = bf16[4096,192]{0,1:T(8,128)(2,1)S(1)} copy-done((bf16[4096,192]{0,1:T(8,128)(2,1)S(1)}, bf16[4096,192]{0,1:T(8,128)(2,1)}, u32[]{:S(2)}) %copy-start.6) | copy-done | bytes 1572888
  21.1 1.4 %copy-done.7 = bf16[192,4096]{1,0:T(8,128)(2,1)S(1)} copy-done((bf16[192,4096]{1,0:T(8,128)(2,1)S(1)}, bf16[192,4096]{1,0:T(8,128)(2,1)}, u32[]{:S(2)}) %copy-start.7) | copy-done | bytes 1572888
  22.5 0.7 copy-done.10
  23.2 0.7 copy-done.12
  23.9 0.7 copy-done.13
  24.6 5.6 %expert.1 = (bf16[16,2048]{1,0:T(8,128)(2,1)S(1)}, f32[16,2048]{1,0:T(8,128)S(1)}, bf16[16,128]{1,0:T(8,128)(2,1)S(1)}, bf16[16,4096]{1,0:T(8,128)(2,1)S(1)}, bf16[16,4096]{1,0:T(8,128)(2,1)S(1)}) custom-call(s32[2]{0:T(128)S(1)} %pad_add_fusion.place, s32[8,128]{1,0:T(8,128)S(1)} %bitcast.34, f32[8,128]{1,0:T(8,128)S(1)} %bitcast.35, ...), custom_call_target="tpu_custom_call" | custom-call | flops 125829120 | bytes 8388608 | tf_op jit(solution)/shard_map/expert/pallas_call | solution.py:310
  30.2 0.1 collective-permute-start
  30.3 0.0 copy-done.9
  30.3 0.5 collective-permute-start.6
  30.8 0.7 collective-permute-done
  31.5 1.1 %collective-permute-start.1 = (bf16[16,2048]{1,0:T(8,128)(2,1)S(1)}, bf16[16,2048]{1,0:T(8,128)(2,1)S(1)}, u32[]{:S(2)}, u32[]{:S(2)}) collective-permute-start(bf16[16,2048]{1,0:T(8,128)(2,1)S(1)} %add_convert_fusion.2), channel_id=1, source_target_pairs={{0,2},{2,0},{4,6},{6,4},{1,3},{3,1},{5,7},{7,5},{8,10},{10,8},{12,... | collective-permute-start | bytes 196616 | tf_op jit(solution)/shard_map/ppermute | solution.py:273
  32.6 2.1 %collective-permute-start.2 = (bf16[16,2048]{1,0:T(8,128)(2,1)S(1)}, bf16[16,2048]{1,0:T(8,128)(2,1)S(1)}, u32[]{:S(2)}, u32[]{:S(2)}) collective-permute-start(bf16[16,2048]{1,0:T(8,128)(2,1)S(1)} %add_convert_fusion.2), channel_id=1, source_target_pairs={{0,4},{2,6},{4,0},{6,2},{1,5},{3,7},{5,1},{7,3},{8,12},{10,14},{12... | collective-permute-start | bytes 196616 | tf_op jit(solution)/shard_map/ppermute | solution.py:273
  34.7 0.4 collective-permute-start.3
  35.1 0.0 collective-permute-done.6.q_par
  35.1 0.0 all-to-all-done
  35.1 0.0 copy-done.14
  35.1 0.0 copy-start.11
  35.1 6.4 %forward.1 = (bf16[2048,1024]{1,0:T(8,128)(2,1)S(1)}, f32[136,1024]{1,0:T(8,128)S(1)}) custom-call(s32[2]{0:T(128)S(1)} %pad_add_fusion.place, s32[64]{0:T(128)S(1)} %copy-done.14, bf16[128,512]{1,0:T(8,128)(2,1)S(1)} %copy-done.9, bf16[128,512]{1,0:T(8,128)(2,1)S(1)} %collective-permute-done.6.q_par, bf16[2048,256]{1,0:T(8,128)(2,1)S(1)} %bitcast.27), custom_call_target="tpu_custom_call" | custom-call | flops 1073741824 | bytes 6291456 | tf_op jit(solution)/shard_map/forward/pallas_call | solution.py:388
  41.5 0.1 collective-permute-start.9
  41.6 0.0 copy-start
  41.7 2.2 %copy-done = bf16[512,4096]{1,0:T(8,128)(2,1)S(1)} copy-done((bf16[512,4096]{1,0:T(8,128)(2,1)S(1)}, bf16[512,4096]{1,0:T(8,128)(2,1)}, u32[]{:S(2)}) %copy-start) | copy-done | bytes 4194328
  43.8 2.2 %base.1.base_own = bf16[512,128]{1,0:T(8,128)(2,1)S(1)} custom-call(bf16[512,4096]{1,0:T(8,128)(2,1)S(1)} %copy-done, bf16[128,4096]{1,0:T(8,128)(2,1)S(1)} %copy-done.2), custom_call_target="tpu_custom_call" | custom-call | flops 536870912 | bytes 5242880 | tf_op jit(solution)/shard_map/base/pallas_call | solution.py:355
  46.0 0.6 collective-permute-start.7
  46.6 0.0 collective-permute-done.1
  46.6 0.0 collective-permute-done.2
  46.6 0.0 collective-permute-done.3
  46.6 0.9 add_convert_fusion.1.total
  47.5 0.1 collective-permute-start.4
  47.6 1.2 %collective-permute-done.4.other = bf16[16,2048]{1,0:T(8,128)(2,1)S(1)} collective-permute-done((bf16[16,2048]{1,0:T(8,128)(2,1)S(1)}, bf16[16,2048]{1,0:T(8,128)(2,1)S(1)}, u32[]{:S(2)}, u32[]{:S(2)}) %collective-permute-start.4) | collective-permute-done | bytes 65568 | tf_op jit(solution)/shard_map/ppermute | solution.py:273
  48.8 0.0 copy-done.11
  48.8 0.0 copy-done.1
  48.8 3.4 %late.1 = (bf16[16,4096]{1,0:T(8,128)(2,1)S(1)}, bf16[16,512]{1,0:T(8,128)(2,1)S(1)}) custom-call(s32[2]{0:T(128)S(1)} %pad_add_fusion.place, bf16[16,2048]{1,0:T(8,128)(2,1)S(1)} %add_convert_fusion.1.total, bf16[16,2048]{1,0:T(8,128)(2,1)S(1)} %collective-permute-done.4.other, bf16[16,4096]{1,0:T(8,128)(2,1)S(1)} %get-tuple-element.20.resid16, ...), custom_call_target="tpu_custom_call" | custom-call | flops 67108864 | bytes 5242880 | tf_op jit(solution)/shard_map/late/pallas_call | solution.py:339
  52.3 0.2 collective-permute-start.8
  52.5 0.0 collective-permute-done.7.base_par
  52.5 1.0 collective-permute-done.8.late_par
  53.6 0.0 collective-permute-done.9.theirs
  53.6 5.8 %backward.1 = (bf16[2048,256]{1,0:T(8,128)(2,1)}, bf16[2048,1024]{1,0:T(8,128)(2,1)S(1)}) custom-call(bf16[128,512]{1,0:T(8,128)(2,1)S(1)} %copy-done.9, bf16[128,512]{1,0:T(8,128)(2,1)S(1)} %collective-permute-done.6.q_par, bf16[512,128]{1,0:T(8,128)(2,1)S(1)} %base.1.base_own, bf16[512,128]{1,0:T(8,128)(2,1)S(1)} %collective-permute-done.7.base_par, ...), custom_call_target="tpu_custom_call" | custom-call | flops 1610612736 | bytes 10485760 | tf_op jit(solution)/shard_map/backward/pallas_call | solution.py:413
  59.4 2.0 %copy-done.3 = bf16[2048,1024]{1,0:T(8,128)(2,1)} copy-done((bf16[2048,1024]{1,0:T(8,128)(2,1)}, bf16[2048,1024]{1,0:T(8,128)(2,1)S(1)}, u32[]{:S(2)}) %copy-start.3) | copy-done | bytes 4194328
  61.3 7.3 %all-to-all-start.1 = ((bf16[16,128,256]{2,1,0:T(8,128)(2,1)}), bf16[16,128,256]{2,1,0:T(8,128)(2,1)}, u32[]{:S(2)}, u32[]{:S(2)}) async-start(bf16[16,128,256]{2,1,0:T(8,128)(2,1)} %bitcast.12), calls=%async_computation.1 | async-start | bytes 2097152 | tf_op jit(solution)/shard_map/all_to_all | solution.py:445
  68.6 0.0 copy-start.4
  68.6 2.2 %copy-done.4 = bf16[2048,1024]{1,0:T(8,128)(2,1)S(1)} copy-done((bf16[2048,1024]{1,0:T(8,128)(2,1)S(1)}, bf16[2048,1024]{1,0:T(8,128)(2,1)}, u32[]{:S(2)}) %copy-start.4) | copy-done | bytes 4194328
  70.8 2.3 %query.1 = (f32[128,512]{1,0:T(8,128)S(1)}, bf16[128,512]{1,0:T(8,128)(2,1)S(1)}) custom-call(bf16[2048,256]{1,0:T(8,128)(2,1)S(1)} %bitcast.29, bf16[2048,1024]{1,0:T(8,128)(2,1)S(1)} %copy-done.4), custom_call_target="tpu_custom_call" | custom-call | flops 536870912 | bytes 6291456 | tf_op jit(solution)/shard_map/query/pallas_call | solution.py:449
  73.1 0.1 collective-permute-start.10
  73.2 2.4 %resid.3 = bf16[128,4096]{1,0:T(8,128)(2,1)} custom-call(bf16[16,128]{1,0:T(8,128)(2,1)S(1)} %get-tuple-element.17.selector, bf16[16,4096]{1,0:T(8,128)(2,1)S(1)} %get-tuple-element.22.rows16, bf16[128,4096]{1,0:T(8,128)(2,1)S(1)} %copy-done.2), custom_call_target="tpu_custom_call" | custom-call | flops 16777216 | bytes 2097152 | tf_op jit(solution)/shard_map/resid/pallas_call | solution.py:370
  75.6 10.8 %all-to-all-done.1 = bf16[16,128,256]{2,1,0:T(8,128)(2,1)} async-done(((bf16[16,128,256]{2,1,0:T(8,128)(2,1)}), bf16[16,128,256]{2,1,0:T(8,128)(2,1)}, u32[]{:S(2)}, u32[]{:S(2)}) %all-to-all-start.1) | async-done | bytes 1048608 | tf_op jit(solution)/shard_map/all_to_all | solution.py:445
  86.5 2.0 %reduce_sum.21 = bf16[128,256]{1,0:T(8,128)(2,1)} reduce(bf16[16,128,256]{2,1,0:T(8,128)(2,1)} %all-to-all-done.1, bf16[]{:T(256)} %constant.47.clone.1), dimensions={0}, to_apply=%region_0.1 | reduce | flops 491520 | bytes 1114114 | tf_op jit(solution)/shard_map/reduce_sum | solution.py:465
  88.5 9.1 %all-to-all-start.2 = ((bf16[8,16,256]{2,1,0:T(8,128)(2,1)}), bf16[8,16,256]{2,1,0:T(8,128)(2,1)S(1)}, u32[]{:S(2)}, u32[]{:S(2)}) async-start(bf16[8,16,256]{2,1,0:T(8,128)(2,1)} %bitcast.13), calls=%async_computation.2 | async-start | bytes 131072 | tf_op jit(solution)/shard_map/all_to_all | solution.py:467
  97.6 0.0 collective-permute-done.10
  97.6 0.7 add_convert_fusion
  98.3 6.2 %all-to-all-done.2 = bf16[8,16,256]{2,1,0:T(8,128)(2,1)S(1)} async-done(((bf16[8,16,256]{2,1,0:T(8,128)(2,1)}), bf16[8,16,256]{2,1,0:T(8,128)(2,1)S(1)}, u32[]{:S(2)}, u32[]{:S(2)}) %all-to-all-start.2) | async-done | bytes 65568 | tf_op jit(solution)/shard_map/all_to_all | solution.py:467
  104.5 0.1 reduce.1
  104.6 0.6 copy.27
  105.2 0.6 copy.28
  (19 shorter events, 0.1 us)
Async XLA Ops:
  0.6 17.6 %copy-start.8 = (bf16[128,4096]{1,0:T(8,128)(2,1)S(1)}, bf16[128,4096]{1,0:T(8,128)(2,1)}, u32[]{:S(2)}) copy-start(bf16[128,4096]{1,0:T(8,128)(2,1)} %resid.2) | copy-start | bytes 3145732
  0.6 17.6 %copy-start.2 = (bf16[128,4096]{1,0:T(8,128)(2,1)S(1)}, bf16[128,4096]{1,0:T(8,128)(2,1)}, u32[]{:S(2)}) copy-start(bf16[128,4096]{1,0:T(8,128)(2,1)} %out_grad.5) | copy-start | bytes 3145732
  1.6 8.3 %collective-permute-start.5 = (bf16[64,256]{1,0:T(8,128)(2,1)S(1)}, bf16[64,256]{1,0:T(8,128)(2,1)S(1)}, u32[]{:S(2)}, u32[]{:S(2)}) collective-permute-start(bf16[64,256]{1,0:T(8,128)(2,1)S(1)} %bitcast.37), channel_id=1, source_target_pairs={{0,32},{32,0},{1,33},{33,1},{2,34},{34,2},{3,35},{35,3},{4,36},{36... | collective-permute-start | bytes 98312 | tf_op jit(solution)/shard_map/ppermute | solution.py:273
  11.0 19.3 %copy-start.9 = (bf16[128,512]{1,0:T(8,128)(2,1)S(1)}, bf16[128,512]{1,0:T(8,128)(2,1)}, u32[]{:S(2)}) copy-start(bf16[128,512]{1,0:T(8,128)(2,1)} %q_own.3) | copy-start | bytes 393220
  11.0 24.1 %copy-start.14 = (s32[64]{0:T(128)S(1)}, s32[64]{0:T(128)}, u32[]{:S(2)}) copy-start(s32[64]{0:T(128)} %spans.1) | copy-start | bytes 772
  11.0 24.1 %all-to-all-start = ((bf16[16,2,64,256]{3,2,1,0:T(8,128)(2,1)}), bf16[16,2,64,256]{3,2,1,0:T(8,128)(2,1)S(1)}, u32[]{:S(2)}, u32[]{:S(2)}) async-start(bf16[16,2,64,256]{3,2,1,0:T(8,128)(2,1)} %broadcast_in_dim.10), calls=%async_computation | async-start | bytes 2097152 | tf_op jit(solution)/shard_map/all_to_all | solution.py:307
  18.3 1.4 %copy-start.5 = (bf16[4096,192]{0,1:T(8,128)(2,1)S(1)}, bf16[4096,192]{0,1:T(8,128)(2,1)}, u32[]{:S(2)}) copy-start(bf16[4096,192]{0,1:T(8,128)(2,1)} %param.18) | copy-start | bytes 4718596
  19.7 1.4 %copy-start.6 = (bf16[4096,192]{0,1:T(8,128)(2,1)S(1)}, bf16[4096,192]{0,1:T(8,128)(2,1)}, u32[]{:S(2)}) copy-start(bf16[4096,192]{0,1:T(8,128)(2,1)} %param.19) | copy-start | bytes 4718596
  21.1 1.4 %copy-start.7 = (bf16[192,4096]{1,0:T(8,128)(2,1)S(1)}, bf16[192,4096]{1,0:T(8,128)(2,1)}, u32[]{:S(2)}) copy-start(bf16[192,4096]{1,0:T(8,128)(2,1)} %w_down.1) | copy-start | bytes 4718596
  22.5 0.7 copy-start.10
  23.2 0.7 copy-start.12
  23.9 0.7 copy-start.13
  30.2 1.3 %collective-permute-start = (bf16[16,2048]{1,0:T(8,128)(2,1)S(1)}, bf16[16,2048]{1,0:T(8,128)(2,1)S(1)}, u32[]{:S(2)}, u32[]{:S(2)}) collective-permute-start(bf16[16,2048]{1,0:T(8,128)(2,1)S(1)} %get-tuple-element.19), channel_id=1, source_target_pairs={{0,1},{1,0},{2,3},{3,2},{4,5},{5,4},{6,7},{7,6},{8,9},{9,8},{10,11... | collective-permute-start | bytes 196616 | tf_op jit(solution)/shard_map/ppermute | solution.py:273
  30.3 4.8 %collective-permute-start.6 = (bf16[128,512]{1,0:T(8,128)(2,1)S(1)}, bf16[128,512]{1,0:T(8,128)(2,1)S(1)}, u32[]{:S(2)}, u32[]{:S(2)}) collective-permute-start(bf16[128,512]{1,0:T(8,128)(2,1)S(1)} %copy-done.9), channel_id=1, source_target_pairs={{0,1},{1,0},{2,3},{3,2},{4,5},{5,4},{6,7},{7,6},{8,9},{9,8},{10,11... | collective-permute-start | bytes 393224 | tf_op jit(solution)/shard_map/ppermute | solution.py:273
  31.5 15.1 %collective-permute-start.1 = (bf16[16,2048]{1,0:T(8,128)(2,1)S(1)}, bf16[16,2048]{1,0:T(8,128)(2,1)S(1)}, u32[]{:S(2)}, u32[]{:S(2)}) collective-permute-start(bf16[16,2048]{1,0:T(8,128)(2,1)S(1)} %add_convert_fusion.2), channel_id=1, source_target_pairs={{0,2},{2,0},{4,6},{6,4},{1,3},{3,1},{5,7},{7,5},{8,10},{10,8},{12,... | collective-permute-start | bytes 196616 | tf_op jit(solution)/shard_map/ppermute | solution.py:273
  32.6 14.0 %collective-permute-start.2 = (bf16[16,2048]{1,0:T(8,128)(2,1)S(1)}, bf16[16,2048]{1,0:T(8,128)(2,1)S(1)}, u32[]{:S(2)}, u32[]{:S(2)}) collective-permute-start(bf16[16,2048]{1,0:T(8,128)(2,1)S(1)} %add_convert_fusion.2), channel_id=1, source_target_pairs={{0,4},{2,6},{4,0},{6,2},{1,5},{3,7},{5,1},{7,3},{8,12},{10,14},{12... | collective-permute-start | bytes 196616 | tf_op jit(solution)/shard_map/ppermute | solution.py:273
  34.7 11.9 %collective-permute-start.3 = (bf16[16,2048]{1,0:T(8,128)(2,1)S(1)}, bf16[16,2048]{1,0:T(8,128)(2,1)}, u32[]{:S(2)}, u32[]{:S(2)}) collective-permute-start(bf16[16,2048]{1,0:T(8,128)(2,1)S(1)} %add_convert_fusion.2), channel_id=1, source_target_pairs={{0,6},{2,4},{4,2},{6,0},{1,7},{3,5},{5,3},{7,1},{8,14},{10,12},{12... | collective-permute-start | bytes 196616 | tf_op jit(solution)/shard_map/ppermute | solution.py:273
  35.1 13.7 %copy-start.11 = (f32[4096]{0:T(1024)S(1)}, f32[4096]{0:T(1024)}, u32[]{:S(2)}) copy-start(f32[4096]{0:T(1024)} %param.15) | copy-start | bytes 49156
  41.5 12.0 %collective-permute-start.9 = (f32[136,1024]{1,0:T(8,128)S(1)}, f32[136,1024]{1,0:T(8,128)S(1)}, u32[]{:S(2)}, u32[]{:S(2)}) collective-permute-start(f32[136,1024]{1,0:T(8,128)S(1)} %get-tuple-element.24.mine), channel_id=1, source_target_pairs={{0,1},{1,0},{2,3},{3,2},{4,5},{5,4},{6,7},{7,6},{8,9},{9,8},{10,11... | collective-permute-start | bytes 1671176 | tf_op jit(solution)/shard_map/ppermute | solution.py:273
  41.6 2.2 %copy-start = (bf16[512,4096]{1,0:T(8,128)(2,1)S(1)}, bf16[512,4096]{1,0:T(8,128)(2,1)}, u32[]{:S(2)}) copy-start(bf16[512,4096]{1,0:T(8,128)(2,1)} %w_out.3) | copy-start | bytes 12582916
  43.8 5.0 %copy-start.1 = (bf16[512,4096]{1,0:T(8,128)(2,1)S(1)}, bf16[512,4096]{1,0:T(8,128)(2,1)}, u32[]{:S(2)}) copy-start(bf16[512,4096]{1,0:T(8,128)(2,1)} %w_out.3) | copy-start | bytes 12582916
  46.0 6.5 %collective-permute-start.7 = (bf16[512,128]{1,0:T(8,128)(2,1)S(1)}, bf16[512,128]{1,0:T(8,128)(2,1)S(1)}, u32[]{:S(2)}, u32[]{:S(2)}) collective-permute-start(bf16[512,128]{1,0:T(8,128)(2,1)S(1)} %base.1.base_own), channel_id=1, source_target_pairs={{0,1},{1,0},{2,3},{3,2},{4,5},{5,4},{6,7},{7,6},{8,9},{9,8},{10,11... | collective-permute-start | bytes 393224 | tf_op jit(solution)/shard_map/ppermute | solution.py:273
  47.5 1.3 %collective-permute-start.4 = (bf16[16,2048]{1,0:T(8,128)(2,1)S(1)}, bf16[16,2048]{1,0:T(8,128)(2,1)S(1)}, u32[]{:S(2)}, u32[]{:S(2)}) collective-permute-start(bf16[16,2048]{1,0:T(8,128)(2,1)S(1)} %add_convert_fusion.1.total), channel_id=1, source_target_pairs={{0,1},{1,0},{2,3},{3,2},{4,5},{5,4},{6,7},{7,6},{8,9},{9,8},{10,11... | collective-permute-start | bytes 196616 | tf_op jit(solution)/shard_map/ppermute | solution.py:273
  52.3 1.3 %collective-permute-start.8 = (bf16[16,512]{1,0:T(8,128)(2,1)S(1)}, bf16[16,512]{1,0:T(8,128)(2,1)S(1)}, u32[]{:S(2)}, u32[]{:S(2)}) collective-permute-start(bf16[16,512]{1,0:T(8,128)(2,1)S(1)} %get-tuple-element.23.late_own), channel_id=1, source_target_pairs={{0,1},{1,0},{2,3},{3,2},{4,5},{5,4},{6,7},{7,6},{8,9},{9,8},{10,11... | collective-permute-start | bytes 49160 | tf_op jit(solution)/shard_map/ppermute | solution.py:273
  59.4 2.0 %copy-start.3 = (bf16[2048,1024]{1,0:T(8,128)(2,1)}, bf16[2048,1024]{1,0:T(8,128)(2,1)S(1)}, u32[]{:S(2)}) copy-start(bf16[2048,1024]{1,0:T(8,128)(2,1)S(1)} %get-tuple-element.26.score_grad) | copy-start | bytes 12582916
  61.3 25.1 %all-to-all-start.1 = ((bf16[16,128,256]{2,1,0:T(8,128)(2,1)}), bf16[16,128,256]{2,1,0:T(8,128)(2,1)}, u32[]{:S(2)}, u32[]{:S(2)}) async-start(bf16[16,128,256]{2,1,0:T(8,128)(2,1)} %bitcast.12), calls=%async_computation.1 | async-start | bytes 2097152 | tf_op jit(solution)/shard_map/all_to_all | solution.py:445
  68.6 2.2 %copy-start.4 = (bf16[2048,1024]{1,0:T(8,128)(2,1)S(1)}, bf16[2048,1024]{1,0:T(8,128)(2,1)}, u32[]{:S(2)}) copy-start(bf16[2048,1024]{1,0:T(8,128)(2,1)} %copy-done.3) | copy-start | bytes 12582916
  73.1 24.4 %collective-permute-start.10 = (bf16[128,512]{1,0:T(8,128)(2,1)S(1)}, bf16[128,512]{1,0:T(8,128)(2,1)S(1)}, u32[]{:S(2)}, u32[]{:S(2)}) collective-permute-start(bf16[128,512]{1,0:T(8,128)(2,1)S(1)} %get-tuple-element.28), channel_id=1, source_target_pairs={{0,1},{1,0},{2,3},{3,2},{4,5},{5,4},{6,7},{7,6},{8,9},{9,8},{10,11... | collective-permute-start | bytes 393224 | tf_op jit(solution)/shard_map/ppermute | solution.py:273
  88.5 16.0 %all-to-all-start.2 = ((bf16[8,16,256]{2,1,0:T(8,128)(2,1)}), bf16[8,16,256]{2,1,0:T(8,128)(2,1)S(1)}, u32[]{:S(2)}, u32[]{:S(2)}) async-start(bf16[8,16,256]{2,1,0:T(8,128)(2,1)} %bitcast.13), calls=%async_computation.2 | async-start | bytes 131072 | tf_op jit(solution)/shard_map/all_to_all | solution.py:467

commit v3 on v2

v3 whole, which is shorter than its diff:
```python
import functools
import math

import jax
import jax.numpy as jnp
from jax import lax
from jax.experimental import pallas as pl
from jax.experimental.pallas import tpu as pltpu
from jax.sharding import Mesh, PartitionSpec as P

DH = 128
GROUP = 16
CAP = 16
EPS = 1e-06
LOW = -1e30
KEYS = 256
CTX = ("y", "hi", "x")
EXP = ("lh", "lb", "core")
CLIQUE = ("lb", "core")
PLANE = ("y", "x")

bf16 = jnp.bfloat16
f32 = jnp.float32
SMEM = pl.BlockSpec(memory_space=pltpu.SMEM)
VMEM = pl.BlockSpec(memory_space=pltpu.VMEM)
HBM = pl.BlockSpec(memory_space=pltpu.HBM)


def product(left, right, left_dim=1, right_dim=0):
    return lax.dot_general(
        left, right, (((left_dim,), (right_dim,)), ((), ())), preferred_element_type=f32
    )


def params(mib):
    return pltpu.CompilerParams(vmem_limit_bytes=mib << 20)


def cost(flops, moved):
    return pl.CostEstimate(flops=flops, bytes_accessed=moved, transcendentals=0)


def stay(array):
    return pltpu.with_memory_space_constraint(array, pltpu.HBM)


def shape(dims, dtype):
    return jax.ShapeDtypeStruct(dims, dtype)


def expert_kernel(
    place, ids_far, combine_far, gain_far, resid, out_grad, w_gate, w_up, w_down, w_out,
    give, keep, selector, resid16, grad16, gain, grad_in, out_in,
    ids, combine, resid_in, gate_in, up_in, down_in, sems,
):
    copies = [
        pltpu.make_async_copy(source, target, sems.at[i])
        for i, (source, target) in enumerate(
            [
                (resid, resid_in), (out_grad, grad_in), (w_gate, gate_in), (w_up, up_in),
                (w_down, down_in), (ids_far, ids), (combine_far, combine), (gain_far, gain),
                (w_out, out_in),
            ]
        )
    ]
    for copy in copies[5:8] + copies[:5] + copies[8:]:
        copy.start()
    for copy in copies[5:8]:
        copy.wait()
    rows = ids.shape[1]
    hit = ids[...] == 0
    chosen_row = jnp.sum(jnp.where(hit, 1.0, 0.0), axis=0, keepdims=True)
    weight_row = jnp.sum(jnp.where(hit, combine[...], 0.0), axis=0, keepdims=True)
    before = lax.broadcasted_iota(jnp.int32, (rows, rows), 0)
    after = lax.broadcasted_iota(jnp.int32, (rows, rows), 1)
    upper = jnp.where(before <= after, 1.0, 0.0).astype(bf16)
    spread = jnp.broadcast_to(chosen_row, (CAP, rows)).astype(bf16)
    rank_row = product(spread, upper)
    slot = lax.broadcasted_iota(jnp.int32, (CAP, rows), 0).astype(f32) + 1.0
    picks = (rank_row == slot) & (chosen_row > 0.0)
    pick = jnp.where(picks, 1.0, 0.0).astype(bf16)
    selector[...] = pick
    weight16 = jnp.sum(jnp.where(picks, weight_row, 0.0), axis=1, keepdims=True)
    copies[0].wait()
    rows16 = product(pick, resid_in[...])
    resid16[...] = rows16.astype(bf16)
    rms16 = lax.rsqrt(jnp.mean(rows16 * rows16, axis=1, keepdims=True) + EPS)
    normed16 = (rows16 * rms16 * gain[...]).astype(bf16)
    copies[1].wait()
    taken = product(pick, grad_in[...])
    grad16[...] = taken.astype(bf16)
    scaled16 = (taken * weight16).astype(bf16)
    copies[2].wait()
    gate_pre = product(normed16, gate_in[...], 1, 1)
    copies[3].wait()
    up_pre = product(normed16, up_in[...], 1, 1)
    copies[4].wait()
    hidden = product(scaled16, down_in[...], 1, 1)
    sig = jax.nn.sigmoid(gate_pre)
    gate_grad = (hidden * up_pre * sig * (1.0 + gate_pre * (1.0 - sig))).astype(bf16)
    up_grad = (hidden * gate_pre * sig).astype(bf16)
    half = give.shape[1]
    first = product(gate_grad, gate_in[:, :half]) + product(up_grad, up_in[:, :half])
    second = product(gate_grad, gate_in[:, half:]) + product(up_grad, up_in[:, half:])
    low = lax.rem(place[1], 2) == 0
    keep[...] = jnp.where(low, first, second)
    give[...] = jnp.where(low, second, first).astype(bf16)
    copies[8].wait()


def late_kernel(
    place, total, other, resid16, grad16, gain, selector, out_grad, w_out,
    resid_grad, attn_grad, merged, sem,
):
    low = lax.rem(place[1], 2) == 0
    first, second = total[...].astype(f32), other[...].astype(f32)
    left, right = jnp.where(low, first, second), jnp.where(low, second, first)
    gained = jnp.concatenate([left, right], axis=1) * gain[...]
    wide = resid16[...].astype(f32)
    rms = lax.rsqrt(jnp.mean(wide * wide, axis=1, keepdims=True) + EPS)
    inner = jnp.mean(gained * wide, axis=1, keepdims=True)
    done = (grad16[...].astype(f32) + rms * (gained - wide * rms * rms * inner)).astype(bf16)
    pick = selector[...]
    chosen = product(pick, jnp.ones((CAP, 128), bf16), 0, 0)[:, :1] > 0.5
    moved = product(pick, done, 0, 0).astype(bf16)
    merged[...] = jnp.where(chosen, moved, out_grad[...])
    copy = pltpu.make_async_copy(merged, resid_grad, sem.at[0])
    copy.start()
    attn_grad[...] = product(w_out[...], merged[...], 1, 1).astype(bf16)
    copy.wait()


def stack_heads(target, groups):
    rows, heads = groups[0].shape[0], groups[0].shape[1] // DH
    for g, group in enumerate(groups):
        for h in range(heads):
            at = (g * heads + h) * rows
            target[at : at + rows] = group[:, h * DH : (h + 1) * DH]


def forward_kernel(
    chunk, sizes, place, spans, q0, q1, q2, q3, kv, weights, out, stats, q_all, held, top
):
    phase, step = pl.program_id(0), pl.program_id(1)
    rows = q0.shape[0]
    block = rows // 2
    columns = q_all.shape[0]
    n_hi, n_x, n_lh = sizes
    factor = math.log2(math.e) / math.sqrt(DH)
    at = pl.ds(pl.multiple_of(step * KEYS, KEYS), KEYS)

    @pl.when((phase == 0) & (step == 0))
    def _():
        stack_heads(q_all, [q0, q1, q2, q3])
        top[...] = jnp.full_like(top, 2.0 * LOW)

    @pl.when(phase == 0)
    def _():
        lane = lax.broadcasted_iota(jnp.int32, (chunk, rows), 1)
        below = lax.broadcasted_iota(jnp.int32, (chunk, rows), 0)
        here = place[0] * 2
        query_pos = jnp.where(
            lane < block, spans[here] * block + lane, spans[here + 1] * block + lane - block
        )
        pieces = []
        for g in range(KEYS // chunk):
            held_by, i = step * (KEYS // chunk // n_lh) + g // n_lh, g % n_lh
            plane, high = held_by // n_hi, held_by % n_hi
            ctx = (plane // n_x * n_hi + high) * n_x + plane % n_x
            key_pos = spans[2 * ctx + i] * block + place[1] * chunk + below
            pieces.append(jnp.where(key_pos <= query_pos, 0.0, LOW))
        bias = jnp.concatenate(pieces, axis=0)
        bias = jnp.concatenate([bias, bias], axis=1)
        key = kv[:, :DH]
        for c in range(0, columns, 2 * rows):
            score = product(key, q_all[c : c + 2 * rows], 1, 1) * factor + bias
            held[at, c : c + 2 * rows] = score
            top[:, c : c + 2 * rows] = jnp.maximum(
                top[:, c : c + 2 * rows], jnp.max(score, axis=0, keepdims=True)
            )

    @pl.when((phase == 1) & (step == 0))
    def _():
        out[...] = jnp.zeros_like(out)
        stats[...] = jnp.zeros_like(stats)
        stats[0:1] = top[...]

    @pl.when(phase == 1)
    def _():
        value = kv[:, DH:]
        for c in range(0, columns, 2 * rows):
            weight = jnp.exp2(held[at, c : c + 2 * rows] - top[:, c : c + 2 * rows])
            stats[1:2, c : c + 2 * rows] += jnp.sum(weight, axis=0, keepdims=True)
            weight = weight.astype(bf16)
            weights[:, c : c + 2 * rows] = weight
            out[:, c : c + 2 * rows] += product(value, weight, 0, 0)


def merge_kernel(grad0, grad1, grad2, grad3, out, stats, grads, merged):
    rows, heads = grad0.shape[1], grad0.shape[0] // DH
    merged[...] = stats[...]
    for g, grad in enumerate([grad0, grad1, grad2, grad3]):
        for h in range(heads):
            to = slice((g * heads + h) * rows, (g * heads + h + 1) * rows)
            part = grad[h * DH : (h + 1) * DH]
            grads[:, to] = part
            merged[2:3, to] = jnp.sum(part.astype(f32) * out[:, to], axis=0, keepdims=True)


def backward_kernel(
    q0, q1, q2, q3, grads_in, stats0, stats1, stats2, stats3, kv, weights,
    kv_part, own, part1, part2, part3,
    q_all, grads, delta, score_grad, total,
):
    rows, heads = q0.shape[0], q0.shape[1] // DH
    columns = q_all.shape[0]
    wide = heads * rows
    scale = 1.0 / math.sqrt(DH)
    step = pl.program_id(0)

    @pl.when(step == 0)
    def _():
        stack_heads(q_all, [q0, q1, q2, q3])
        total[...] = jnp.zeros_like(total)
        every = [stats0, stats1, stats2, stats3]
        for g in range(len(every)):
            views = [
                stats[:, (g ^ m) * wide : (g ^ m) * wide + wide] for m, stats in enumerate(every)
            ]
            peak = functools.reduce(jnp.maximum, [view[0:1] for view in views])
            gains = [jnp.exp2(view[0:1] - peak) for view in views]
            mass = sum(view[1:2] * up for view, up in zip(views, gains))
            dots = sum(view[2:3] * up for view, up in zip(views, gains))
            inverse = 1.0 / mass
            near = gains[0] * inverse
            to = slice(g * wide, (g + 1) * wide)
            delta[:, to] = near * dots * inverse
            grads[:, to] = (grads_in[:, to].astype(f32) * near).astype(bf16)

    key, value = kv[:, :DH], kv[:, DH:]
    for c in range(0, columns, 2 * rows):
        prob_grad = product(value, grads[:, c : c + 2 * rows])
        weight = weights[:, c : c + 2 * rows].astype(f32)
        score_grad[:, c : c + 2 * rows] = (
            weight * (prob_grad - delta[:, c : c + 2 * rows])
        ).astype(bf16)
    kv_part[:, DH:] = product(weights[...], grads[...], 1, 1).astype(bf16)
    kv_part[:, :DH] = (product(score_grad[...], q_all[...]) * scale).astype(bf16)
    total[...] += product(key, score_grad[...], 0, 0)

    @pl.when(step == pl.num_programs(0) - 1)
    def _():
        for g, part in enumerate([own, part1, part2, part3]):
            for h in range(heads):
                at = (g * heads + h) * rows
                moved = total[:, at : at + rows].T * scale
                part[:, h * DH : (h + 1) * DH] = moved.astype(part.dtype)


def final_kernel(parts, key_grad, value_grad):
    n_lh = key_grad.shape[1] // DH
    for k in range(n_lh):
        summed = sum(
            parts[i].astype(f32) for i in range(k, parts.shape[0], n_lh)
        ).astype(bf16)
        key_grad[:, k * DH : (k + 1) * DH] = summed[:, :DH]
        value_grad[:, k * DH : (k + 1) * DH] = summed[:, DH:]


def across(array, axis, mask=1):
    count = lax.axis_size(axis)
    return lax.ppermute(array, axis, [(i, i ^ mask) for i in range(count)])


def shared(array):
    return [array] + [across(array, CLIQUE, mask) for mask in (1, 2, 3)]


def on_device(
    resid, out_grad, norm_gain, expert_ids, combine, w_gate, w_up, w_down, w_out,
    queries, keys, values, span_order,
):
    rows, width = resid.shape
    heads = queries.shape[1] // DH
    hidden = w_gate.shape[1]
    n_y, n_x, n_hi, n_lh, n_lb = (lax.axis_size(axis) for axis in ("y", "x", "hi", "lh", "lb"))
    core, high, share = lax.axis_index("core"), lax.axis_index("hi"), lax.axis_index(CLIQUE)
    n_share = 2 * n_lb
    chunk = rows // (n_lh * n_share)
    half = width // 2
    columns = n_share * heads * rows
    n_keys = n_y * n_x * n_hi * n_lh * chunk
    steps = n_keys // KEYS
    place = jnp.stack([lax.axis_index(CTX), share]).astype(jnp.int32)

    def chunks_of(array):
        split = array.reshape(n_lh, n_share, chunk, n_lh * DH)
        start = (0, share, 0, lax.axis_index("lh") * DH)
        return lax.dynamic_slice(split, start, (n_lh, 1, chunk, DH))[:, 0]

    own_kv = jnp.concatenate([chunks_of(keys), chunks_of(values)], axis=2)
    far_kv = across(own_kv, "hi")
    plane_kv = jnp.where(high == 0, jnp.stack([own_kv, far_kv]), jnp.stack([far_kv, own_kv]))
    sent = jnp.broadcast_to(plane_kv[None], (n_y * n_x,) + plane_kv.shape)

    give, keep, selector, resid16, grad16, gain, grad_near, out_near = pl.pallas_call(
        expert_kernel,
        out_shape=(
            shape((CAP, half), bf16),
            shape((CAP, half), f32),
            shape((CAP, rows), bf16),
            shape((CAP, width), bf16),
            shape((CAP, width), bf16),
            shape((1, width), f32),
            shape((rows, width), bf16),
            shape(w_out.shape, bf16),
        ),
        in_specs=[SMEM] + [HBM] * 9,
        out_specs=(VMEM,) * 8,
        scratch_shapes=[
            pltpu.VMEM(expert_ids.shape[::-1], jnp.int32),
            pltpu.VMEM(expert_ids.shape[::-1], f32),
            pltpu.VMEM((rows, width), bf16),
            pltpu.VMEM((hidden, width), bf16),
            pltpu.VMEM((hidden, width), bf16),
            pltpu.VMEM((hidden, width), bf16),
            pltpu.SemaphoreType.DMA((9,)),
        ],
        compiler_params=params(24),
        cost_estimate=cost(10 * CAP * width * hidden, 8 << 20),
        name="expert",
    )(
        place,
        *map(
            stay,
            (expert_ids.T, combine.T, norm_gain[None, :], resid, out_grad)
            + (w_gate.T, w_up.T, w_down, w_out),
        ),
    )

    pair = lax.optimization_barrier((keep + across(give, "core").astype(f32)).astype(bf16))
    sent, pair = lax.optimization_barrier((sent, pair))
    kv = lax.all_to_all(sent, PLANE, 0, 0, tiled=True).reshape(-1, 2 * DH)
    r1, r2, r3 = [across(pair, ("lh", "lb"), mask) for mask in (1, 2, 3)]
    total = (pair.astype(f32) + r1.astype(f32)) + (r2.astype(f32) + r3.astype(f32))
    total = lax.optimization_barrier(total.astype(bf16))
    other = across(total, "core")
    resid_grad, attn_grad = pl.pallas_call(
        late_kernel,
        out_shape=(shape((rows, width), bf16), shape((heads * DH, rows), bf16)),
        in_specs=[SMEM] + [VMEM] * 8,
        out_specs=(HBM, VMEM),
        scratch_shapes=[pltpu.VMEM((rows, width), bf16), pltpu.SemaphoreType.DMA((1,))],
        compiler_params=params(16),
        cost_estimate=cost(2 * rows * width * heads * DH, 1 << 20),
        name="late",
    )(place, total, other, resid16, grad16, gain, selector, grad_near, out_near)

    whole = lambda *_: (0, 0)
    query_spec = pl.BlockSpec((rows, heads * DH), whole)
    wide_spec = pl.BlockSpec((DH, columns), whole)
    stats_spec = pl.BlockSpec((8, columns), whole)
    query_all = shared(queries)
    pair_flops = 2 * n_keys * columns * DH
    weights, out, stats = pl.pallas_call(
        functools.partial(forward_kernel, chunk, (n_hi, n_x, n_lh)),
        grid=(2, steps),
        out_shape=(
            shape((n_keys, columns), bf16),
            shape((DH, columns), f32),
            shape((8, columns), f32),
        ),
        in_specs=[SMEM, SMEM]
        + [query_spec] * n_share
        + [pl.BlockSpec((KEYS, 2 * DH), lambda p, j: (j, 0))],
        out_specs=(
            pl.BlockSpec((KEYS, columns), lambda p, j: (j * p, 0)),
            wide_spec,
            stats_spec,
        ),
        scratch_shapes=[
            pltpu.VMEM((columns, DH), bf16),
            pltpu.VMEM((n_keys, columns), f32),
            pltpu.VMEM((1, columns), f32),
        ],
        compiler_params=params(24),
        cost_estimate=cost(2 * pair_flops, 6 << 20),
        name="forward",
    )(place, span_order, *query_all, kv)
    grads, stats = pl.pallas_call(
        merge_kernel,
        out_shape=(shape((DH, columns), bf16), shape((8, columns), f32)),
        in_specs=[VMEM] * (n_share + 2),
        out_specs=(VMEM, VMEM),
        compiler_params=params(12),
        cost_estimate=cost(2 * DH * columns, 3 << 20),
        name="merge",
    )(*shared(attn_grad), out, stats)
    kv_part, query_own, *query_give = pl.pallas_call(
        backward_kernel,
        grid=(steps,),
        out_shape=(shape((n_keys, 2 * DH), bf16), shape((rows, heads * DH), f32))
        + (shape((rows, heads * DH), bf16),) * (n_share - 1),
        in_specs=[query_spec] * n_share
        + [wide_spec]
        + [stats_spec] * n_share
        + [
            pl.BlockSpec((KEYS, 2 * DH), lambda j: (j, 0)),
            pl.BlockSpec((KEYS, columns), lambda j: (j, 0)),
        ],
        out_specs=(pl.BlockSpec((KEYS, 2 * DH), lambda j: (j, 0)),) + (query_spec,) * n_share,
        scratch_shapes=[
            pltpu.VMEM((columns, DH), bf16),
            pltpu.VMEM((DH, columns), bf16),
            pltpu.VMEM((1, columns), f32),
            pltpu.VMEM((KEYS, columns), bf16),
            pltpu.VMEM((DH, columns), f32),
        ],
        compiler_params=params(24),
        cost_estimate=cost(4 * pair_flops, 8 << 20),
        name="backward",
    )(*query_all, grads, *shared(stats), kv, weights)
    got = lax.all_to_all(
        kv_part.reshape(n_y * n_x, n_hi * n_lh * chunk, 2 * DH), PLANE, 0, 0, tiled=True
    )
    query_parts = [
        across(part, CLIQUE, mask).astype(f32) for mask, part in enumerate(query_give, 1)
    ]
    query_grad = (query_own + sum(query_parts)).astype(bf16)

    owned = jnp.sum(got.astype(f32), axis=0).astype(bf16)
    owned = owned.reshape(n_hi * n_lh, chunk, 2 * DH)
    parts = lax.all_to_all(owned, ("hi", "lh"), 0, 0, tiled=True)
    key_grad, value_grad = pl.pallas_call(
        final_kernel,
        out_shape=(shape((chunk, n_lh * DH), bf16),) * 2,
        in_specs=[VMEM],
        out_specs=(VMEM, VMEM),
        compiler_params=params(8),
        name="final",
    )(parts)
    return (resid_grad, query_grad, key_grad, value_grad)


def solution(mesh):
    fine = Mesh(mesh.devices.reshape(4, 2, 4, 2, 2, 2), CTX + EXP)
    return jax.shard_map(
        on_device,
        mesh=fine,
        in_specs=(
            P(CTX, None),
            P(CTX, None),
            P(),
            P(CTX, None),
            P(CTX, None),
            P(None, EXP),
            P(None, EXP),
            P(EXP, None),
            P(EXP, None),
            P(CTX, EXP),
            P(CTX, None),
            P(CTX, None),
            P(),
        ),
        out_specs=(
            P(CTX, None),
            P(CTX, EXP),
            P(CTX + EXP, None),
            P(CTX + EXP, None),
        ),
        check_vma=False,
    )
```

time: 107 us -> 88.6 us (0.83)
  local copies, waits for them, and re-layouts: 15.9 us -> 5.74 us
  Pallas kernels: 28.1 us -> 20.7 us
  waiting for transfers between devices: 22 us -> 27.3 us
  starting transfers between devices: 35.2 us -> 32.1 us
  other arithmetic: 3.75 us -> 1.55 us
    unnamed x33 -> x8, local copies, waits for them, and re-layouts: 13.9 us -> 4.15 us
    all_to_all x3, starting transfers between devices: 23.5 us -> 13.9 us  [the longest x1 7.03 us: on_device(): kv = lax.all_to_all(sent, PLANE, 0, 0, tiled=True).reshape(-1, 2 * DH)]
    pallas_call x5 -> x4, Pallas kernels: 16.7 us -> 8.24 us  [the longest x1 5.14 us: on_device(): pl.pallas_call(functools.partial(forward_kernel, chunk, (n_hi, n_x, n_lh)...]
    ppermute x11 -> x18, starting transfers between devices: 11.7 us -> 18.2 us  [across(): return lax.ppermute(array, axis, [(i, i ^ mask) for i in range(count)])]
    all_to_all x3, waiting for transfers between devices: 17.1 us -> 21.6 us  [the longest x1 9.86 us: on_device(): lax.all_to_all(kv_part.reshape(n_y * n_x, n_hi * n_lh * chunk, 2 * DH), P...]
    reduce_sum x1, other arithmetic: 2 us -> 0.68 us  [on_device(): owned = jnp.sum(got.astype(f32), axis=0).astype(bf16)]
    ppermute x11 -> x18, waiting for transfers between devices: 4.9 us -> 5.68 us  [across(): return lax.ppermute(array, axis, [(i, i ^ mask) for i in range(count)])]
  transfers between devices with their start and end apart: 14 -> 21, of which waited for: 6 -> 7; matrix products, arithmetic and copies ran while one was open for 3% -> 2% of each run, Pallas kernels for 21% -> 16%
where the time goes in v3:
time: 88.6 us; the launch traced here: 88.2 us
  starting transfers between devices  32.1 us (36%)
  waiting for transfers between devices  27.3 us (31%)
  Pallas kernels  20.7 us (23%)
  local copies, waits for them, and re-layouts  5.74 us (6%)
  other arithmetic  1.55 us (2%)
    ppermute x18, starting transfers between devices, across(): return lax.ppermute(array, axis, [(i, i ^ mask) for i in range(count)])  18.2 us
    all_to_all x1, waiting for transfers between devices, on_device(): lax.all_to_all(kv_part.reshape(n_y * n_x, n_hi * n_lh * chunk, 2 * DH), P...  9.86 us
    all_to_all x1, waiting for transfers between devices, on_device(): parts = lax.all_to_all(owned, ('hi', 'lh'), 0, 0, tiled=True)  7.08 us
    all_to_all x1, starting transfers between devices, on_device(): kv = lax.all_to_all(sent, PLANE, 0, 0, tiled=True).reshape(-1, 2 * DH)  7.03 us
    pallas_call x1, Pallas kernels, on_device(): pl.pallas_call(expert_kernel, out_shape=(shape((CAP, half), bf16), shape(...  6.4 us
    pallas_call x1, Pallas kernels, on_device(): pl.pallas_call(backward_kernel, grid=(steps,), out_shape=(shape((n_keys,...  6.02 us
    ppermute x18, waiting for transfers between devices, across(): return lax.ppermute(array, axis, [(i, i ^ mask) for i in range(count)])  5.68 us
    pallas_call x1, Pallas kernels, on_device(): pl.pallas_call(functools.partial(forward_kernel, chunk, (n_hi, n_x, n_lh)...  5.14 us
  transfers between devices with their start and end apart: 21, of which 7 were waited for; matrix products, arithmetic and copies ran while one was open for 2% of the time, Pallas kernels for 16%

profile of v3, /device:TPU:32, one launch (start us, length us, event | category | flops | bytes accessed | tf_op | source)
XLA Modules:
  0.0 88.2 jit_solution(1843336269308505564)
XLA Ops:
  0.6 0.7 dynamic-slice_bitcast_fusion
  1.4 6.4 %collective-permute-start = (bf16[2,16,256]{2,1,0:T(8,128)(2,1)S(1)}, bf16[2,16,256]{2,1,0:T(8,128)(2,1)S(1)}, u32[]{:S(2)}, u32[]{:S(2)}) collective-permute-start(bf16[2,16,256]{2,1,0:T(8,128)(2,1)S(1)} %get-tuple-element.53), channel_id=1, source_target_pairs={{0,32},{32,0},{1,33},{33,1},{2,34},{34,2},{3,35},{35,3},{4,36},{36... | collective-permute-start | bytes 49160 | tf_op jit(solution)/shard_map/ppermute | solution.py:272
  7.7 0.1 pad_add_fusion.place
  7.8 0.0 copy-start.2
  7.8 6.4 %expert.1 = (bf16[16,2048]{1,0:T(8,128)(2,1)S(1)}, f32[16,2048]{1,0:T(8,128)S(1)}, bf16[16,128]{1,0:T(8,128)(2,1)S(1)}, bf16[16,4096]{1,0:T(8,128)(2,1)S(1)}, bf...) custom-call(s32[2]{0:T(128)S(1)} %pad_add_fusion.place, ...), custom_call_target="tpu_custom_call" | custom-call | flops 125829120 | bytes 8388608 | tf_op jit(solution)/shard_map/expert/pallas_call | solution.py:306
  14.2 0.0 copy-start
  14.2 1.9 %copy-done = bf16[512,4096]{1,0:T(8,128)(2,1)} copy-done((bf16[512,4096]{1,0:T(8,128)(2,1)}, bf16[512,4096]{1,0:T(8,128)(2,1)S(1)}, u32[]{:S(2)}) %copy-start) | copy-done | bytes 4194328
  16.2 0.0 copy-start.3
  16.2 0.0 collective-permute-start.1
  16.2 0.0 collective-permute-done
  16.2 1.2 %collective-permute-done.1 = bf16[16,2048]{1,0:T(8,128)(2,1)S(1)} collective-permute-done((bf16[16,2048]{1,0:T(8,128)(2,1)S(1)}, bf16[16,2048]{1,0:T(8,128)(2,1)S(1)}, u32[]{:S(2)}, u32[]{:S(2)}) %collective-permute-start.1) | collective-permute-done | bytes 65568 | tf_op jit(solution)/shard_map/ppermute | solution.py:272
  17.5 0.9 broadcast_in_dim.4
  18.3 1.0 %collective-permute-start.4 = (bf16[16,2048]{1,0:T(8,128)(2,1)S(1)}, bf16[16,2048]{1,0:T(8,128)(2,1)S(1)}, u32[]{:S(2)}, u32[]{:S(2)}) collective-permute-start(bf16[16,2048]{1,0:T(8,128)(2,1)S(1)} %add_convert_fusion.2), channel_id=1, source_target_pairs={{0,6},{2,4},{4,2},{6,0},{1,7},{3,5},{5,3},{7,1},{8,14},{10,12},{12... | collective-permute-start | bytes 196616 | tf_op jit(solution)/shard_map/ppermute | solution.py:272
  19.3 2.4 %collective-permute-start.3 = (bf16[16,2048]{1,0:T(8,128)(2,1)S(1)}, bf16[16,2048]{1,0:T(8,128)(2,1)S(1)}, u32[]{:S(2)}, u32[]{:S(2)}) collective-permute-start(bf16[16,2048]{1,0:T(8,128)(2,1)S(1)} %add_convert_fusion.2), channel_id=1, source_target_pairs={{0,4},{2,6},{4,0},{6,2},{1,5},{3,7},{5,1},{7,3},{8,12},{10,14},{12... | collective-permute-start | bytes 196616 | tf_op jit(solution)/shard_map/ppermute | solution.py:272
  21.7 0.1 collective-permute-start.2
  21.8 0.0 copy-done.2
  21.8 0.8 collective-permute-start.8
  22.6 7.0 %all-to-all-start = ((bf16[16,2,2,16,256]{4,3,2,1,0:T(8,128)(2,1)}), bf16[16,2,2,16,256]{4,3,2,1,0:T(8,128)(2,1)S(1)}, u32[]{:S(2)}, u32[]{:S(2)}) async-start(bf16[16,2,2,16,256]{4,3,2,1,0:T(8,128)(2,1)} %broadcast_in_dim.4), calls=%async_computation | async-start | bytes 1048576 | tf_op jit(solution)/shard_map/all_to_all | solution.py:343
  29.7 0.0 collective-permute-done.4
  29.7 0.0 collective-permute-done.3
  29.7 0.0 collective-permute-done.2
  29.8 1.0 %collective-permute-start.5 = (bf16[16,2048]{1,0:T(8,128)(2,1)S(1)}, bf16[16,2048]{1,0:T(8,128)(2,1)S(1)}, u32[]{:S(2)}, u32[]{:S(2)}) collective-permute-start(bf16[16,2048]{1,0:T(8,128)(2,1)S(1)} %add_convert_fusion.1.total), channel_id=1, source_target_pairs={{0,1},{1,0},{2,3},{3,2},{4,5},{5,4},{6,7},{7,6},{8,9},{9,8},{10,11... | collective-permute-start | bytes 196616 | tf_op jit(solution)/shard_map/ppermute | solution.py:272
  30.8 0.3 collective-permute-start.7
  31.0 0.1 collective-permute-start.6
  31.2 0.5 collective-permute-done.5.other
  31.7 0.0 copy-start.1
  31.7 2.2 %copy-done.1 = bf16[512,4096]{1,0:T(8,128)(2,1)S(1)} copy-done((bf16[512,4096]{1,0:T(8,128)(2,1)S(1)}, bf16[512,4096]{1,0:T(8,128)(2,1)}, u32[]{:S(2)}) %copy-start.1) | copy-done | bytes 4194328
  33.9 2.3 %late.1 = (bf16[128,4096]{1,0:T(8,128)(2,1)}, bf16[512,128]{1,0:T(8,128)(2,1)S(1)}) custom-call(s32[2]{0:T(128)S(1)} %pad_add_fusion.place, bf16[16,2048]{1,0:T(8,128)(2,1)S(1)} %add_convert_fusion.1.total, bf16[16,2048]{1,0:T(8,128)(2,1)S(1)} %collective-permute-done.5.other, bf16[16,4096]{1,0:T(8,128)(2,1)S(1)} %get-tuple-element.31.resid16, ...), custom_call_target="tpu_custom_call" | custom-call | flops 536870912 | bytes 1048576 | tf_op jit(solution)/shard_map/late/pallas_call | solution.py:348
  36.1 1.3 %collective-permute-start.11 = (bf16[512,128]{1,0:T(8,128)(2,1)S(1)}, bf16[512,128]{1,0:T(8,128)(2,1)S(1)}, u32[]{:S(2)}, u32[]{:S(2)}) collective-permute-start(bf16[512,128]{1,0:T(8,128)(2,1)S(1)} %get-tuple-element.38.grad0), channel_id=1, source_target_pairs={{0,3},{1,2},{2,1},{3,0},{4,7},{5,6},{6,5},{7,4},{8,11},{9,10},{10,... | collective-permute-start | bytes 393224 | tf_op jit(solution)/shard_map/ppermute | solution.py:272
  37.5 0.7 collective-permute-start.10
  38.2 0.0 collective-permute-done.8.q3
  38.2 0.0 collective-permute-start.9
  38.2 0.0 collective-permute-done.7.q2
  38.2 0.0 collective-permute-done.6.q1
  38.2 4.7 %all-to-all-done = bf16[16,2,2,16,256]{4,3,2,1,0:T(8,128)(2,1)S(1)} async-done(((bf16[16,2,2,16,256]{4,3,2,1,0:T(8,128)(2,1)}), bf16[16,2,2,16,256]{4,3,2,1,0:T(8,128)(2,1)S(1)}, u32[]{:S(2)}, u32[]{:S(2)}) %all-to-all-start) | async-done | bytes 524320 | tf_op jit(solution)/shard_map/all_to_all | solution.py:343
  42.9 0.0 copy-done.3
  42.9 5.1 %forward.1 = (bf16[1024,2048]{1,0:T(8,128)(2,1)S(1)}, f32[128,2048]{1,0:T(8,128)S(1)}, f32[8,2048]{1,0:T(8,128)S(1)}) custom-call(s32[2]{0:T(128)S(1)} %pad_add_fusion.place, s32[64]{0:T(128)S(1)} %copy-done.3, bf16[128,512]{1,0:T(8,128)(2,1)S(1)} %copy-done.2, bf16[128,512]{1,0:T(8,128)(2,1)S(1)} %collective-permute-done.6.q1, ...), custom_call_target="tpu_custom_call" | custom-call | flops 1073741824 | bytes 6291456 | tf_op jit(solution)/shard_map/forward/pallas_call | solution.py:365
  48.1 0.0 collective-permute-done.11.grad3
  48.1 0.0 collective-permute-done.10.grad2
  48.1 0.0 collective-permute-done.9.grad1
  48.1 0.2 merge.1
  48.3 0.3 collective-permute-start.14
  48.6 1.7 %collective-permute-start.13 = (f32[8,2048]{1,0:T(8,128)S(1)}, f32[8,2048]{1,0:T(8,128)S(1)}, u32[]{:S(2)}, u32[]{:S(2)}) collective-permute-start(f32[8,2048]{1,0:T(8,128)S(1)} %get-tuple-element.43.stats0), channel_id=1, source_target_pairs={{0,2},{1,3},{2,0},{3,1},{4,6},{5,7},{6,4},{7,5},{8,10},{9,11},{10,... | collective-permute-start | bytes 196616 | tf_op jit(solution)/shard_map/ppermute | solution.py:272
  50.3 0.2 collective-permute-start.12
  50.4 2.3 %collective-permute-done.14.stats3 = f32[8,2048]{1,0:T(8,128)S(1)} collective-permute-done((f32[8,2048]{1,0:T(8,128)S(1)}, f32[8,2048]{1,0:T(8,128)S(1)}, u32[]{:S(2)}, u32[]{:S(2)}) %collective-permute-start.14) | collective-permute-done | bytes 65568 | tf_op jit(solution)/shard_map/ppermute | solution.py:272
  52.7 1.6 %collective-permute-done.13.stats2 = f32[8,2048]{1,0:T(8,128)S(1)} collective-permute-done((f32[8,2048]{1,0:T(8,128)S(1)}, f32[8,2048]{1,0:T(8,128)S(1)}, u32[]{:S(2)}, u32[]{:S(2)}) %collective-permute-start.13) | collective-permute-done | bytes 65568 | tf_op jit(solution)/shard_map/ppermute | solution.py:272
  54.4 0.0 collective-permute-done.12.stats1
  54.4 6.0 %backward.1 = (bf16[1024,256]{1,0:T(8,128)(2,1)}, f32[128,512]{1,0:T(8,128)S(1)}, bf16[128,512]{1,0:T(8,128)(2,1)S(1)}, bf16[128,512]{1,0:T(8,128)(2,1)S(1)}, bf16[128,512]{1,0:T(8,128)(2,1)S(1)}) custom-call(bf16[128,512]{1,0:T(8,128)(2,1)S(1)} %copy-done.2, bf16[128,512]{1,0:T(8,128)(2,1)S(1)} %collective-permute-done.6.q1, ...), custom_call_target="tpu_custom_call" | custom-call | flops 2147483648 | bytes 8388608 | tf_op jit(solution)/shard_map/backward/pallas_call | solution.py:399
  60.4 3.6 %all-to-all-start.1 = ((bf16[16,64,256]{2,1,0:T(8,128)(2,1)}), bf16[16,64,256]{2,1,0:T(8,128)(2,1)S(1)}, u32[]{:S(2)}, u32[]{:S(2)}) async-start(bf16[16,64,256]{2,1,0:T(8,128)(2,1)} %bitcast.14), calls=%async_computation.1 | async-start | bytes 1048576 | tf_op jit(solution)/shard_map/all_to_all | solution.py:423
  64.0 0.1 collective-permute-start.15
  64.1 0.7 collective-permute-start.16
  64.7 1.2 %collective-permute-start.17 = (bf16[128,512]{1,0:T(8,128)(2,1)S(1)}, bf16[128,512]{1,0:T(8,128)(2,1)S(1)}, u32[]{:S(2)}, u32[]{:S(2)}) collective-permute-start(bf16[128,512]{1,0:T(8,128)(2,1)S(1)} %get-tuple-element.48), channel_id=1, source_target_pairs={{0,3},{1,2},{2,1},{3,0},{4,7},{5,6},{6,5},{7,4},{8,11},{9,10},{10,... | collective-permute-start | bytes 393224 | tf_op jit(solution)/shard_map/ppermute | solution.py:272
  65.9 9.9 %all-to-all-done.1 = bf16[16,64,256]{2,1,0:T(8,128)(2,1)S(1)} async-done(((bf16[16,64,256]{2,1,0:T(8,128)(2,1)}), bf16[16,64,256]{2,1,0:T(8,128)(2,1)S(1)}, u32[]{:S(2)}, u32[]{:S(2)}) %all-to-all-start.1) | async-done | bytes 524320 | tf_op jit(solution)/shard_map/all_to_all | solution.py:423
  75.8 0.7 reduce_sum.12
  76.5 3.3 %all-to-all-start.2 = ((bf16[4,16,256]{2,1,0:T(8,128)(2,1)}), bf16[4,16,256]{2,1,0:T(8,128)(2,1)S(1)}, u32[]{:S(2)}, u32[]{:S(2)}) async-start(bf16[4,16,256]{2,1,0:T(8,128)(2,1)} %bitcast.15), calls=%async_computation.2 | async-start | bytes 65536 | tf_op jit(solution)/shard_map/all_to_all | solution.py:433
  79.8 0.0 collective-permute-done.15
  79.8 0.0 collective-permute-done.16
  79.8 0.0 collective-permute-done.17
  79.8 0.7 add_convert_fusion
  80.5 7.1 %all-to-all-done.2.parts = bf16[4,16,256]{2,1,0:T(8,128)(2,1)S(1)} async-done(((bf16[4,16,256]{2,1,0:T(8,128)(2,1)}), bf16[4,16,256]{2,1,0:T(8,128)(2,1)S(1)}, u32[]{:S(2)}, u32[]{:S(2)}) %all-to-all-start.2) | async-done | bytes 32800 | tf_op jit(solution)/shard_map/all_to_all | solution.py:433
  87.6 0.6 final.1
  (4 shorter events, 0.1 us)
Async XLA Ops:
  1.4 14.8 %collective-permute-start = (bf16[2,16,256]{2,1,0:T(8,128)(2,1)S(1)}, bf16[2,16,256]{2,1,0:T(8,128)(2,1)S(1)}, u32[]{:S(2)}, u32[]{:S(2)}) collective-permute-start(bf16[2,16,256]{2,1,0:T(8,128)(2,1)S(1)} %get-tuple-element.53), channel_id=1, source_target_pairs={{0,32},{32,0},{1,33},{33,1},{2,34},{34,2},{3,35},{35,3},{4,36},{36... | collective-permute-start | bytes 49160 | tf_op jit(solution)/shard_map/ppermute | solution.py:272
  7.8 14.0 %copy-start.2 = (bf16[128,512]{1,0:T(8,128)(2,1)S(1)}, bf16[128,512]{1,0:T(8,128)(2,1)}, u32[]{:S(2)}) copy-start(bf16[128,512]{1,0:T(8,128)(2,1)} %q0.3) | copy-start | bytes 393220
  14.2 2.0 %copy-start = (bf16[512,4096]{1,0:T(8,128)(2,1)}, bf16[512,4096]{1,0:T(8,128)(2,1)S(1)}, u32[]{:S(2)}) copy-start(bf16[512,4096]{1,0:T(8,128)(2,1)S(1)} %get-tuple-element.36.w_out) | copy-start | bytes 12582916
  16.2 26.7 %copy-start.3 = (s32[64]{0:T(128)S(1)}, s32[64]{0:T(128)}, u32[]{:S(2)}) copy-start(s32[64]{0:T(128)} %spans.1) | copy-start | bytes 772
  16.2 1.3 %collective-permute-start.1 = (bf16[16,2048]{1,0:T(8,128)(2,1)S(1)}, bf16[16,2048]{1,0:T(8,128)(2,1)S(1)}, u32[]{:S(2)}, u32[]{:S(2)}) collective-permute-start(bf16[16,2048]{1,0:T(8,128)(2,1)S(1)} %get-tuple-element.29), channel_id=1, source_target_pairs={{0,1},{1,0},{2,3},{3,2},{4,5},{5,4},{6,7},{7,6},{8,9},{9,8},{10,11... | collective-permute-start | bytes 196616 | tf_op jit(solution)/shard_map/ppermute | solution.py:272
  18.3 11.4 %collective-permute-start.4 = (bf16[16,2048]{1,0:T(8,128)(2,1)S(1)}, bf16[16,2048]{1,0:T(8,128)(2,1)S(1)}, u32[]{:S(2)}, u32[]{:S(2)}) collective-permute-start(bf16[16,2048]{1,0:T(8,128)(2,1)S(1)} %add_convert_fusion.2), channel_id=1, source_target_pairs={{0,6},{2,4},{4,2},{6,0},{1,7},{3,5},{5,3},{7,1},{8,14},{10,12},{12... | collective-permute-start | bytes 196616 | tf_op jit(solution)/shard_map/ppermute | solution.py:272
  19.3 10.4 %collective-permute-start.3 = (bf16[16,2048]{1,0:T(8,128)(2,1)S(1)}, bf16[16,2048]{1,0:T(8,128)(2,1)S(1)}, u32[]{:S(2)}, u32[]{:S(2)}) collective-permute-start(bf16[16,2048]{1,0:T(8,128)(2,1)S(1)} %add_convert_fusion.2), channel_id=1, source_target_pairs={{0,4},{2,6},{4,0},{6,2},{1,5},{3,7},{5,1},{7,3},{8,12},{10,14},{12... | collective-permute-start | bytes 196616 | tf_op jit(solution)/shard_map/ppermute | solution.py:272
  21.7 8.0 %collective-permute-start.2 = (bf16[16,2048]{1,0:T(8,128)(2,1)S(1)}, bf16[16,2048]{1,0:T(8,128)(2,1)S(1)}, u32[]{:S(2)}, u32[]{:S(2)}) collective-permute-start(bf16[16,2048]{1,0:T(8,128)(2,1)S(1)} %add_convert_fusion.2), channel_id=1, source_target_pairs={{0,2},{2,0},{4,6},{6,4},{1,3},{3,1},{5,7},{7,5},{8,10},{10,8},{12,... | collective-permute-start | bytes 196616 | tf_op jit(solution)/shard_map/ppermute | solution.py:272
  21.8 16.4 %collective-permute-start.8 = (bf16[128,512]{1,0:T(8,128)(2,1)S(1)}, bf16[128,512]{1,0:T(8,128)(2,1)S(1)}, u32[]{:S(2)}, u32[]{:S(2)}) collective-permute-start(bf16[128,512]{1,0:T(8,128)(2,1)S(1)} %copy-done.2), channel_id=1, source_target_pairs={{0,3},{1,2},{2,1},{3,0},{4,7},{5,6},{6,5},{7,4},{8,11},{9,10},{10,... | collective-permute-start | bytes 393224 | tf_op jit(solution)/shard_map/ppermute | solution.py:272
  22.6 20.3 %all-to-all-start = ((bf16[16,2,2,16,256]{4,3,2,1,0:T(8,128)(2,1)}), bf16[16,2,2,16,256]{4,3,2,1,0:T(8,128)(2,1)S(1)}, u32[]{:S(2)}, u32[]{:S(2)}) async-start(bf16[16,2,2,16,256]{4,3,2,1,0:T(8,128)(2,1)} %broadcast_in_dim.4), calls=%async_computation | async-start | bytes 1048576 | tf_op jit(solution)/shard_map/all_to_all | solution.py:343
  29.8 1.9 %collective-permute-start.5 = (bf16[16,2048]{1,0:T(8,128)(2,1)S(1)}, bf16[16,2048]{1,0:T(8,128)(2,1)S(1)}, u32[]{:S(2)}, u32[]{:S(2)}) collective-permute-start(bf16[16,2048]{1,0:T(8,128)(2,1)S(1)} %add_convert_fusion.1.total), channel_id=1, source_target_pairs={{0,1},{1,0},{2,3},{3,2},{4,5},{5,4},{6,7},{7,6},{8,9},{9,8},{10,11... | collective-permute-start | bytes 196616 | tf_op jit(solution)/shard_map/ppermute | solution.py:272
  30.8 7.5 %collective-permute-start.7 = (bf16[128,512]{1,0:T(8,128)(2,1)S(1)}, bf16[128,512]{1,0:T(8,128)(2,1)S(1)}, u32[]{:S(2)}, u32[]{:S(2)}) collective-permute-start(bf16[128,512]{1,0:T(8,128)(2,1)S(1)} %copy-done.2), channel_id=1, source_target_pairs={{0,2},{1,3},{2,0},{3,1},{4,6},{5,7},{6,4},{7,5},{8,10},{9,11},{10,... | collective-permute-start | bytes 393224 | tf_op jit(solution)/shard_map/ppermute | solution.py:272
  31.0 7.2 %collective-permute-start.6 = (bf16[128,512]{1,0:T(8,128)(2,1)S(1)}, bf16[128,512]{1,0:T(8,128)(2,1)S(1)}, u32[]{:S(2)}, u32[]{:S(2)}) collective-permute-start(bf16[128,512]{1,0:T(8,128)(2,1)S(1)} %copy-done.2), channel_id=1, source_target_pairs={{0,1},{1,0},{2,3},{3,2},{4,5},{5,4},{6,7},{7,6},{8,9},{9,8},{10,11... | collective-permute-start | bytes 393224 | tf_op jit(solution)/shard_map/ppermute | solution.py:272
  31.7 2.2 %copy-start.1 = (bf16[512,4096]{1,0:T(8,128)(2,1)S(1)}, bf16[512,4096]{1,0:T(8,128)(2,1)}, u32[]{:S(2)}) copy-start(bf16[512,4096]{1,0:T(8,128)(2,1)} %copy-done) | copy-start | bytes 12582916
  36.1 11.9 %collective-permute-start.11 = (bf16[512,128]{1,0:T(8,128)(2,1)S(1)}, bf16[512,128]{1,0:T(8,128)(2,1)S(1)}, u32[]{:S(2)}, u32[]{:S(2)}) collective-permute-start(bf16[512,128]{1,0:T(8,128)(2,1)S(1)} %get-tuple-element.38.grad0), channel_id=1, source_target_pairs={{0,3},{1,2},{2,1},{3,0},{4,7},{5,6},{6,5},{7,4},{8,11},{9,10},{10,... | collective-permute-start | bytes 393224 | tf_op jit(solution)/shard_map/ppermute | solution.py:272
  37.5 10.6 %collective-permute-start.10 = (bf16[512,128]{1,0:T(8,128)(2,1)S(1)}, bf16[512,128]{1,0:T(8,128)(2,1)S(1)}, u32[]{:S(2)}, u32[]{:S(2)}) collective-permute-start(bf16[512,128]{1,0:T(8,128)(2,1)S(1)} %get-tuple-element.38.grad0), channel_id=1, source_target_pairs={{0,2},{1,3},{2,0},{3,1},{4,6},{5,7},{6,4},{7,5},{8,10},{9,11},{10,... | collective-permute-start | bytes 393224 | tf_op jit(solution)/shard_map/ppermute | solution.py:272
  38.2 9.9 %collective-permute-start.9 = (bf16[512,128]{1,0:T(8,128)(2,1)S(1)}, bf16[512,128]{1,0:T(8,128)(2,1)S(1)}, u32[]{:S(2)}, u32[]{:S(2)}) collective-permute-start(bf16[512,128]{1,0:T(8,128)(2,1)S(1)} %get-tuple-element.38.grad0), channel_id=1, source_target_pairs={{0,1},{1,0},{2,3},{3,2},{4,5},{5,4},{6,7},{7,6},{8,9},{9,8},{10,11... | collective-permute-start | bytes 393224 | tf_op jit(solution)/shard_map/ppermute | solution.py:272
  48.3 4.4 %collective-permute-start.14 = (f32[8,2048]{1,0:T(8,128)S(1)}, f32[8,2048]{1,0:T(8,128)S(1)}, u32[]{:S(2)}, u32[]{:S(2)}) collective-permute-start(f32[8,2048]{1,0:T(8,128)S(1)} %get-tuple-element.43.stats0), channel_id=1, source_target_pairs={{0,3},{1,2},{2,1},{3,0},{4,7},{5,6},{6,5},{7,4},{8,11},{9,10},{10,... | collective-permute-start | bytes 196616 | tf_op jit(solution)/shard_map/ppermute | solution.py:272
  48.6 5.8 %collective-permute-start.13 = (f32[8,2048]{1,0:T(8,128)S(1)}, f32[8,2048]{1,0:T(8,128)S(1)}, u32[]{:S(2)}, u32[]{:S(2)}) collective-permute-start(f32[8,2048]{1,0:T(8,128)S(1)} %get-tuple-element.43.stats0), channel_id=1, source_target_pairs={{0,2},{1,3},{2,0},{3,1},{4,6},{5,7},{6,4},{7,5},{8,10},{9,11},{10,... | collective-permute-start | bytes 196616 | tf_op jit(solution)/shard_map/ppermute | solution.py:272
  50.3 4.1 %collective-permute-start.12 = (f32[8,2048]{1,0:T(8,128)S(1)}, f32[8,2048]{1,0:T(8,128)S(1)}, u32[]{:S(2)}, u32[]{:S(2)}) collective-permute-start(f32[8,2048]{1,0:T(8,128)S(1)} %get-tuple-element.43.stats0), channel_id=1, source_target_pairs={{0,1},{1,0},{2,3},{3,2},{4,5},{5,4},{6,7},{7,6},{8,9},{9,8},{10,11... | collective-permute-start | bytes 196616 | tf_op jit(solution)/shard_map/ppermute | solution.py:272
  60.4 15.4 %all-to-all-start.1 = ((bf16[16,64,256]{2,1,0:T(8,128)(2,1)}), bf16[16,64,256]{2,1,0:T(8,128)(2,1)S(1)}, u32[]{:S(2)}, u32[]{:S(2)}) async-start(bf16[16,64,256]{2,1,0:T(8,128)(2,1)} %bitcast.14), calls=%async_computation.1 | async-start | bytes 1048576 | tf_op jit(solution)/shard_map/all_to_all | solution.py:423
  64.0 15.8 %collective-permute-start.15 = (bf16[128,512]{1,0:T(8,128)(2,1)S(1)}, bf16[128,512]{1,0:T(8,128)(2,1)S(1)}, u32[]{:S(2)}, u32[]{:S(2)}) collective-permute-start(bf16[128,512]{1,0:T(8,128)(2,1)S(1)} %get-tuple-element.46), channel_id=1, source_target_pairs={{0,1},{1,0},{2,3},{3,2},{4,5},{5,4},{6,7},{7,6},{8,9},{9,8},{10,11... | collective-permute-start | bytes 393224 | tf_op jit(solution)/shard_map/ppermute | solution.py:272
  64.1 15.7 %collective-permute-start.16 = (bf16[128,512]{1,0:T(8,128)(2,1)S(1)}, bf16[128,512]{1,0:T(8,128)(2,1)S(1)}, u32[]{:S(2)}, u32[]{:S(2)}) collective-permute-start(bf16[128,512]{1,0:T(8,128)(2,1)S(1)} %get-tuple-element.47), channel_id=1, source_target_pairs={{0,2},{1,3},{2,0},{3,1},{4,6},{5,7},{6,4},{7,5},{8,10},{9,11},{10,... | collective-permute-start | bytes 393224 | tf_op jit(solution)/shard_map/ppermute | solution.py:272
  64.7 15.0 %collective-permute-start.17 = (bf16[128,512]{1,0:T(8,128)(2,1)S(1)}, bf16[128,512]{1,0:T(8,128)(2,1)S(1)}, u32[]{:S(2)}, u32[]{:S(2)}) collective-permute-start(bf16[128,512]{1,0:T(8,128)(2,1)S(1)} %get-tuple-element.48), channel_id=1, source_target_pairs={{0,3},{1,2},{2,1},{3,0},{4,7},{5,6},{6,5},{7,4},{8,11},{9,10},{10,... | collective-permute-start | bytes 393224 | tf_op jit(solution)/shard_map/ppermute | solution.py:272
  76.5 11.1 %all-to-all-start.2 = ((bf16[4,16,256]{2,1,0:T(8,128)(2,1)}), bf16[4,16,256]{2,1,0:T(8,128)(2,1)S(1)}, u32[]{:S(2)}, u32[]{:S(2)}) async-start(bf16[4,16,256]{2,1,0:T(8,128)(2,1)} %bitcast.15), calls=%async_computation.2 | async-start | bytes 65536 | tf_op jit(solution)/shard_map/all_to_all | solution.py:433

commit v4 on v3

v4 whole, which is shorter than its diff:
```python
import functools
import itertools
import math

import jax
import jax.numpy as jnp
from jax import lax
from jax.experimental import pallas as pl
from jax.experimental.pallas import tpu as pltpu
from jax.sharding import Mesh, PartitionSpec as P

DH = 128
GROUP = 16
CAP = 16
EPS = 1e-06
LOW = -1e30
AHEAD = 4
CTX = ("y", "hi", "x")
EXP = ("lh", "lb", "core")
CLIQUE = ("lb", "core")
PLANE = ("y", "x")
RING = (0, 1, 2, 3)

bf16 = jnp.bfloat16
f32 = jnp.float32
SMEM = pl.BlockSpec(memory_space=pltpu.SMEM)
VMEM = pl.BlockSpec(memory_space=pltpu.VMEM)
HBM = pl.BlockSpec(memory_space=pltpu.HBM)


def product(left, right, left_dim=1, right_dim=0):
    return lax.dot_general(
        left, right, (((left_dim,), (right_dim,)), ((), ())), preferred_element_type=f32
    )


def params(mib):
    return pltpu.CompilerParams(vmem_limit_bytes=mib << 20)


def cost(flops, moved):
    return pl.CostEstimate(flops=flops, bytes_accessed=moved, transcendentals=0)


def stay(array):
    return pltpu.with_memory_space_constraint(array, pltpu.HBM)


def shape(dims, dtype):
    return jax.ShapeDtypeStruct(dims, dtype)


def expert_kernel(
    flags, ids_far, combine_far, gain_far, resid, out_grad, w_gate, w_up, w_down,
    give, keep, selector, resid16, grad16, gain,
    ids, combine, resid_in, grad_in, wide_in, down_in, sems,
):
    hidden_rows = w_down.shape[0]
    cuts = (sems.shape[0] - 5) // 3
    step = w_down.shape[1] // cuts
    heads = [
        pltpu.make_async_copy(source, target, sems.at[i])
        for i, (source, target) in enumerate(
            [
                (ids_far, ids),
                (combine_far, combine),
                (gain_far, gain),
                (resid, resid_in),
                (out_grad, grad_in),
            ]
        )
    ]
    spans = [pl.ds(i * step, step) for i in range(cuts)]
    bodies = [
        [
            pltpu.make_async_copy(
                source.at[:, span], target.at[pl.ds(row, hidden_rows), span], sems.at[5 + 3 * i + j]
            )
            for j, (source, target, row) in enumerate(
                [(w_gate, wide_in, 0), (w_up, wide_in, hidden_rows), (w_down, down_in, 0)]
            )
        ]
        for i, span in enumerate(spans)
    ]
    for copy in heads:
        copy.start()
    for body in bodies[:AHEAD]:
        for copy in body:
            copy.start()
    for copy in heads[:3]:
        copy.wait()
    rows = ids.shape[1]
    hit = ids[...] == 0
    chosen_row = jnp.sum(jnp.where(hit, 1.0, 0.0), axis=0, keepdims=True)
    weight_row = jnp.sum(jnp.where(hit, combine[...], 0.0), axis=0, keepdims=True)
    before = lax.broadcasted_iota(jnp.int32, (rows, rows), 0)
    after = lax.broadcasted_iota(jnp.int32, (rows, rows), 1)
    upper = jnp.where(before <= after, 1.0, 0.0).astype(bf16)
    spread = jnp.broadcast_to(chosen_row, (CAP, rows)).astype(bf16)
    rank_row = product(spread, upper)
    slot = lax.broadcasted_iota(jnp.int32, (CAP, rows), 0).astype(f32) + 1.0
    picks = (rank_row == slot) & (chosen_row > 0.0)
    pick = jnp.where(picks, 1.0, 0.0).astype(bf16)
    selector[...] = pick
    weight16 = jnp.sum(jnp.where(picks, weight_row, 0.0), axis=1, keepdims=True)
    heads[3].wait()
    rows16 = product(pick, resid_in[...])
    resid16[...] = rows16.astype(bf16)
    rms16 = lax.rsqrt(jnp.mean(rows16 * rows16, axis=1, keepdims=True) + EPS)
    normed16 = (rows16 * rms16 * gain[...]).astype(bf16)
    heads[4].wait()
    taken = product(pick, grad_in[...])
    grad16[...] = taken.astype(bf16)
    scaled16 = (taken * weight16).astype(bf16)
    pre = hidden = 0.0
    for i, span in enumerate(spans):
        for copy in bodies[i]:
            copy.wait()
        if i + AHEAD < cuts:
            for copy in bodies[i + AHEAD]:
                copy.start()
        at = slice(i * step, (i + 1) * step)
        pre += product(normed16[:, at], wide_in[:, span], 1, 1)
        hidden += product(scaled16[:, at], down_in[:, span], 1, 1)
    pre, hidden = pre.T, hidden.T
    gate_pre, up_pre = pre[:hidden_rows], pre[hidden_rows:]
    sig = jax.nn.sigmoid(gate_pre)
    gate_grad = hidden * up_pre * sig * (1.0 + gate_pre * (1.0 - sig))
    up_grad = hidden * gate_pre * sig
    both = jnp.concatenate([gate_grad, up_grad], axis=0).astype(bf16)
    half = give.shape[1]
    first = product(both, wide_in[:, :half], 0, 0)
    second = product(both, wide_in[:, half:], 0, 0)
    low = flags[0:1, 0:1] == 0.0
    keep[...] = jnp.where(low, first, second)
    give[...] = jnp.where(low, second, first).astype(bf16)


def late_kernel(
    flags, summed, other, resid16, grad16, gain, selector, out_grad, w_out,
    resid_grad, attn_grad, merged, grad_in, out_in, sems,
):
    cuts = sems.shape[0] - 2
    step = w_out.shape[1] // cuts
    arrive = pltpu.make_async_copy(out_grad, grad_in, sems.at[cuts])
    arrive.start()
    spans = [pl.ds(i * step, step) for i in range(cuts)]
    copies = [
        pltpu.make_async_copy(w_out.at[:, span], out_in.at[:, span], sems.at[i])
        for i, span in enumerate(spans)
    ]
    for copy in copies[:AHEAD]:
        copy.start()
    low = flags[0:1, 0:1] == 0.0
    first, second = summed[...].astype(f32), other[...].astype(f32)
    left, right = jnp.where(low, first, second), jnp.where(low, second, first)
    gained = jnp.concatenate([left, right], axis=1) * gain[...]
    wide = resid16[...].astype(f32)
    rms = lax.rsqrt(jnp.mean(wide * wide, axis=1, keepdims=True) + EPS)
    inner = jnp.mean(gained * wide, axis=1, keepdims=True)
    done = (grad16[...].astype(f32) + rms * (gained - wide * rms * rms * inner)).astype(bf16)
    pick = selector[...]
    chosen = product(pick, jnp.ones((CAP, 128), bf16), 0, 0)[:, :1] > 0.5
    moved = product(pick, done, 0, 0).astype(bf16)
    arrive.wait()
    merged[...] = jnp.where(chosen, moved, grad_in[...])
    leave = pltpu.make_async_copy(merged, resid_grad, sems.at[cuts + 1])
    leave.start()
    total = 0.0
    for i, span in enumerate(spans):
        copies[i].wait()
        if i + AHEAD < cuts:
            copies[i + AHEAD].start()
        total += product(out_in[:, span], merged[:, span], 1, 1)
    attn_grad[...] = total.astype(bf16)
    leave.wait()


def stack_heads(target, groups):
    rows, heads = groups[0].shape[0], groups[0].shape[1] // DH
    for g, group in enumerate(groups):
        for h in range(heads):
            at = (g * heads + h) * rows
            target[at : at + rows] = group[:, h * DH : (h + 1) * DH]


def forward_kernel(
    chunk, order, place, spans, q0, q1, q2, q3, kv, weights, out, stats, q_all, held, top
):
    phase = pl.program_id(0)
    rows = q0.shape[0]
    block = rows // 2
    columns = q_all.shape[0]
    factor = math.log2(math.e) / math.sqrt(DH)

    @pl.when(phase == 0)
    def _():
        stack_heads(q_all, [q0, q1, q2, q3])
        top[...] = jnp.full_like(top, 2.0 * LOW)

    @pl.when(phase == 0)
    def _():
        lane = lax.broadcasted_iota(jnp.int32, (chunk, rows), 1)
        below = lax.broadcasted_iota(jnp.int32, (chunk, rows), 0)
        here = place[0] * 2
        query_pos = jnp.where(
            lane < block, spans[here] * block + lane, spans[here + 1] * block + lane - block
        )
        pieces = []
        for ctx, i in order:
            key_pos = spans[2 * ctx + i] * block + place[1] * chunk + below
            pieces.append(jnp.where(key_pos <= query_pos, 0.0, LOW))
        bias = jnp.concatenate(pieces, axis=0)
        bias = jnp.concatenate([bias, bias], axis=1)
        key = kv[:, :DH]
        for c in range(0, columns, 2 * rows):
            score = product(key, q_all[c : c + 2 * rows], 1, 1) * factor + bias
            held[:, c : c + 2 * rows] = score
            top[:, c : c + 2 * rows] = jnp.maximum(
                top[:, c : c + 2 * rows], jnp.max(score, axis=0, keepdims=True)
            )

    @pl.when(phase == 1)
    def _():
        out[...] = jnp.zeros_like(out)
        stats[...] = jnp.zeros_like(stats)
        stats[0:1] = top[...]

    @pl.when(phase == 1)
    def _():
        value = kv[:, DH:]
        for c in range(0, columns, 2 * rows):
            weight = jnp.exp2(held[:, c : c + 2 * rows] - top[:, c : c + 2 * rows])
            stats[1:2, c : c + 2 * rows] += jnp.sum(weight, axis=0, keepdims=True)
            weight = weight.astype(bf16)
            weights[:, c : c + 2 * rows] = weight
            out[:, c : c + 2 * rows] += product(value, weight, 0, 0)


def merge_kernel(grad0, grad1, grad2, grad3, out, stats, grads, packed):
    rows, heads = grad0.shape[1], grad0.shape[0] // DH
    wide = packed.shape[1] // 3
    for g, grad in enumerate([grad0, grad1, grad2, grad3]):
        for h in range(heads):
            at = (g * heads + h) * rows
            to = slice(at, at + rows)
            part = grad[h * DH : (h + 1) * DH]
            grads[:, to] = part
            row, column = at // wide, at % wide
            for k, value in enumerate(
                [stats[0:1, to], stats[1:2, to], jnp.sum(part.astype(f32) * out[:, to], axis=0, keepdims=True)]
            ):
                packed[row : row + 1, k * wide + column : k * wide + column + rows] = value


def backward_kernel(
    order, q0, q1, q2, q3, grads_in, stats0, stats1, stats2, stats3, kv, weights,
    kv_part, own, part1, part2, part3,
    q_all, grads, delta, score_grad,
):
    rows, heads = q0.shape[0], q0.shape[1] // DH
    columns = q_all.shape[0]
    wide = heads * rows
    scale = 1.0 / math.sqrt(DH)
    stack_heads(q_all, [q0, q1, q2, q3])
    every = [stats0, stats1, stats2, stats3]
    lanes = stats0.shape[1] // 3
    each = wide // lanes
    for g in range(len(every)):
        views = [stats[(g ^ m) * each : (g ^ m) * each + each] for m, stats in enumerate(every)]
        tops = [view[:, :lanes] for view in views]
        peak = functools.reduce(jnp.maximum, tops)
        gains = [jnp.exp2(top - peak) for top in tops]
        mass = sum(view[:, lanes : 2 * lanes] * up for view, up in zip(views, gains))
        dots = sum(view[:, 2 * lanes :] * up for view, up in zip(views, gains))
        inverse = 1.0 / mass
        near = gains[0] * inverse
        middle = near * dots * inverse
        for r in range(each):
            to = slice(g * wide + r * lanes, g * wide + (r + 1) * lanes)
            delta[:, to] = middle[r : r + 1]
            grads[:, to] = (grads_in[:, to].astype(f32) * near[r : r + 1]).astype(bf16)

    key, value = kv[:, :DH], kv[:, DH:]
    for c in range(0, columns, 2 * rows):
        at = slice(c, c + 2 * rows)
        prob_grad = product(value, grads[:, at])
        score_grad[:, at] = (weights[:, at].astype(f32) * (prob_grad - delta[:, at])).astype(bf16)
    value_part = product(weights[...], grads[...], 1, 1).astype(bf16)
    key_part = (product(score_grad[...], q_all[...]) * scale).astype(bf16)
    group = key.shape[0] // len(order)
    for g, to in enumerate(order):
        at, to = slice(g * group, (g + 1) * group), slice(to * group, (to + 1) * group)
        kv_part[to, :DH] = key_part[at]
        kv_part[to, DH:] = value_part[at]
    for g, part in enumerate([own, part1, part2, part3]):
        total = product(key, score_grad[:, g * wide : (g + 1) * wide], 0, 0)
        for h in range(heads):
            moved = total[:, h * rows : (h + 1) * rows].T * scale
            part[:, h * DH : (h + 1) * DH] = moved.astype(part.dtype)


def final_kernel(flags, own, lower, upper, both, key_grad, value_grad):
    same = own[...].astype(f32) + upper[...].astype(f32)
    rest = lower[...].astype(f32) + both[...].astype(f32)
    low = flags[1:2, 0:1] == 0.0
    first, second = jnp.where(low, same, rest), jnp.where(low, rest, same)
    for k, summed in enumerate([first, second]):
        key_grad[:, k * DH : (k + 1) * DH] = summed[:, :DH].astype(bf16)
        value_grad[:, k * DH : (k + 1) * DH] = summed[:, DH:].astype(bf16)


def across(array, axis, mask=1):
    count = lax.axis_size(axis)
    return lax.ppermute(array, axis, [(i, i ^ mask) for i in range(count)])


def shared(array):
    return [array] + [across(array, CLIQUE, mask) for mask in (1, 2, 3)]


def on_device(
    resid, out_grad, norm_gain, expert_ids, combine, w_gate, w_up, w_down, w_out,
    queries, keys, values, span_order,
):
    rows, width = resid.shape
    heads = queries.shape[1] // DH
    hidden = w_gate.shape[1]
    n_y, n_x, n_hi, n_lh, n_lb = (lax.axis_size(axis) for axis in ("y", "x", "hi", "lh", "lb"))
    core, high, share = lax.axis_index("core"), lax.axis_index("hi"), lax.axis_index(CLIQUE)
    n_share = 2 * n_lb
    chunk = rows // (n_lh * n_share)
    half = width // 2
    columns = n_share * heads * rows
    n_keys = n_y * n_x * n_hi * n_lh * chunk
    place = jnp.stack([lax.axis_index(CTX), share]).astype(jnp.int32)
    group = lax.axis_index("lh")
    flags = jnp.where(lax.broadcasted_iota(jnp.int32, (8, 128), 0) == 0, core, group).astype(f32)

    def chunks_of(array, head):
        split = array.reshape(n_lh, n_share, chunk, n_lh * DH)
        start = (0, share, 0, head * DH)
        return lax.dynamic_slice(split, start, (n_lh, 1, chunk, DH))[:, 0]

    def both_of(head):
        return jnp.concatenate([chunks_of(keys, head), chunks_of(values, head)], axis=2)

    give, keep, selector, resid16, grad16, gain = pl.pallas_call(
        expert_kernel,
        out_shape=(
            shape((CAP, half), bf16),
            shape((CAP, half), f32),
            shape((CAP, rows), bf16),
            shape((CAP, width), bf16),
            shape((CAP, width), bf16),
            shape((1, width), f32),
        ),
        in_specs=[VMEM] + [HBM] * 8,
        out_specs=(VMEM,) * 6,
        scratch_shapes=[
            pltpu.VMEM(expert_ids.shape[::-1], jnp.int32),
            pltpu.VMEM(expert_ids.shape[::-1], f32),
            pltpu.VMEM((rows, width), bf16),
            pltpu.VMEM((rows, width), bf16),
            pltpu.VMEM((2 * hidden, width), bf16),
            pltpu.VMEM((hidden, width), bf16),
            pltpu.SemaphoreType.DMA((17,)),
        ],
        compiler_params=params(24),
        cost_estimate=cost(10 * CAP * width * hidden, 8 << 20),
        name="expert",
    )(
        flags,
        *map(
            stay,
            (expert_ids.T, combine.T, norm_gain[None, :], resid, out_grad)
            + (w_gate.T, w_up.T, w_down),
        ),
    )

    own_kv = both_of(group)
    leaving, give = lax.optimization_barrier((both_of(1 - group), give))
    far_kv = across(leaving, ("hi", "lh"), 3)
    plane_kv = jnp.where(high == 0, jnp.stack([own_kv, far_kv]), jnp.stack([far_kv, own_kv]))
    sent = jnp.broadcast_to(plane_kv[None], (n_y * n_x,) + plane_kv.shape)

    pair = lax.optimization_barrier((keep + across(give, "core").astype(f32)).astype(bf16))
    kv = lax.all_to_all(sent, PLANE, 0, 0, tiled=True).reshape(-1, 2 * DH)
    r1, r2, r3 = [across(pair, ("lh", "lb"), mask) for mask in (1, 2, 3)]
    total = (pair.astype(f32) + r1.astype(f32)) + (r2.astype(f32) + r3.astype(f32))
    total = lax.optimization_barrier(total.astype(bf16))
    other = across(total, "core")
    resid_grad, attn_grad = pl.pallas_call(
        late_kernel,
        out_shape=(shape((rows, width), bf16), shape((heads * DH, rows), bf16)),
        in_specs=[VMEM] * 7 + [HBM] * 2,
        out_specs=(HBM, VMEM),
        scratch_shapes=[
            pltpu.VMEM((rows, width), bf16),
            pltpu.VMEM((rows, width), bf16),
            pltpu.VMEM(w_out.shape, bf16),
            pltpu.SemaphoreType.DMA((4,)),
        ],
        compiler_params=params(16),
        cost_estimate=cost(1 << 20, 1 << 16),
        name="late",
    )(flags, total, other, resid16, grad16, gain, selector, stay(out_grad), stay(w_out))

    query_all = shared(queries)
    tour = list(itertools.product(RING, RING))
    places = [y * n_x + x for y, x in tour]
    held = [
        ((y * n_hi + hi) * n_x + x, i) for y, x in tour for hi in range(n_hi) for i in range(n_lh)
    ]
    whole = lambda *_: (0, 0)
    pair_flops = 2 * n_keys * columns * DH
    weights, out, stats = pl.pallas_call(
        functools.partial(forward_kernel, chunk, held),
        grid=(2,),
        out_shape=(
            shape((n_keys, columns), bf16),
            shape((DH, columns), f32),
            shape((8, columns), f32),
        ),
        in_specs=[SMEM, SMEM] + [pl.BlockSpec((rows, heads * DH), whole)] * n_share
        + [pl.BlockSpec((n_keys, 2 * DH), whole)],
        out_specs=(
            pl.BlockSpec((n_keys, columns), whole),
            pl.BlockSpec((DH, columns), whole),
            pl.BlockSpec((8, columns), whole),
        ),
        scratch_shapes=[
            pltpu.VMEM((columns, DH), bf16),
            pltpu.VMEM((n_keys, columns), f32),
            pltpu.VMEM((1, columns), f32),
        ],
        compiler_params=params(24),
        cost_estimate=cost(2 * pair_flops, 6 << 20),
        name="forward",
    )(place, span_order, *query_all, kv)
    grads, packed = pl.pallas_call(
        merge_kernel,
        out_shape=(shape((DH, columns), bf16), shape((8, 3 * columns // 8), f32)),
        in_specs=[VMEM] * (n_share + 2),
        out_specs=(VMEM, VMEM),
        compiler_params=params(12),
        cost_estimate=cost(2 * DH * columns, 3 << 20),
        name="merge",
    )(*shared(attn_grad), out, stats)
    kv_part, query_own, *query_give = pl.pallas_call(
        functools.partial(backward_kernel, places),
        out_shape=(shape((n_keys, 2 * DH), bf16), shape((rows, heads * DH), f32))
        + (shape((rows, heads * DH), bf16),) * (n_share - 1),
        in_specs=[VMEM] * (2 * n_share + 3),
        out_specs=(VMEM,) * (n_share + 1),
        scratch_shapes=[
            pltpu.VMEM((columns, DH), bf16),
            pltpu.VMEM((DH, columns), bf16),
            pltpu.VMEM((1, columns), f32),
            pltpu.VMEM((n_keys, columns), bf16),
        ],
        compiler_params=params(16),
        cost_estimate=cost(4 * pair_flops, 8 << 20),
        name="backward",
    )(*query_all, grads, *shared(packed), kv, weights)
    got = lax.all_to_all(
        kv_part.reshape(n_y * n_x, n_hi * n_lh * chunk, 2 * DH), PLANE, 0, 0, tiled=True
    )
    query_parts = [
        across(part, CLIQUE, mask).astype(f32) for mask, part in enumerate(query_give, 1)
    ]
    query_grad = (query_own + sum(query_parts)).astype(bf16)

    owned = jnp.sum(got.astype(f32), axis=0).astype(bf16)
    owned = owned.reshape(n_hi * n_lh, chunk, 2 * DH)
    here = 2 * high + group
    parts = [lax.dynamic_index_in_dim(owned, here, 0, keepdims=False)] + [
        across(lax.dynamic_index_in_dim(owned, here ^ mask, 0, keepdims=False), ("hi", "lh"), mask)
        for mask in (1, 2, 3)
    ]
    key_grad, value_grad = pl.pallas_call(
        final_kernel,
        out_shape=(shape((chunk, n_lh * DH), bf16),) * 2,
        in_specs=[VMEM] * 5,
        out_specs=(VMEM, VMEM),
        compiler_params=params(8),
        name="final",
    )(flags, *parts)
    return (resid_grad, query_grad, key_grad, value_grad)


def solution(mesh):
    fine = Mesh(mesh.devices.reshape(4, 2, 4, 2, 2, 2), CTX + EXP)
    return jax.shard_map(
        on_device,
        mesh=fine,
        in_specs=(
            P(CTX, None),
            P(CTX, None),
            P(),
            P(CTX, None),
            P(CTX, None),
            P(None, EXP),
            P(None, EXP),
            P(EXP, None),
            P(EXP, None),
            P(CTX, EXP),
            P(CTX, None),
            P(CTX, None),
            P(),
        ),
        out_specs=(
            P(CTX, None),
            P(CTX, EXP),
            P(CTX + EXP, None),
            P(CTX + EXP, None),
        ),
        check_vma=False,
    )
```

time: 88.6 us -> 79.1 us (0.89)
  waiting for transfers between devices: 27.3 us -> 18.1 us
  starting transfers between devices: 32.1 us -> 38.9 us
  local copies, waits for them, and re-layouts: 5.74 us -> 1.73 us
  Pallas kernels: 20.7 us -> 18.3 us
    all_to_all x1 -> x0, waiting for transfers between devices: 7.08 us -> none  [on_device(): parts = lax.all_to_all(owned, ('hi', 'lh'), 0, 0, tiled=True)]
    ppermute x18 -> x21, starting transfers between devices: 18.2 us -> 24.7 us  [across(): return lax.ppermute(array, axis, [(i, i ^ mask) for i in range(count)])]
    unnamed x8 -> x4, local copies, waits for them, and re-layouts: 4.15 us -> 0.01 us
    all_to_all x1, starting transfers between devices: 3.57 us -> 7.21 us  [on_device(): lax.all_to_all(kv_part.reshape(n_y * n_x, n_hi * n_lh * chunk, 2 * DH), P...]
    all_to_all x1 -> x0, starting transfers between devices: 3.26 us -> none  [on_device(): parts = lax.all_to_all(owned, ('hi', 'lh'), 0, 0, tiled=True)]
    all_to_all x1, waiting for transfers between devices: 4.69 us -> 2.11 us  [on_device(): kv = lax.all_to_all(sent, PLANE, 0, 0, tiled=True).reshape(-1, 2 * DH)]
    pallas_call x2, Pallas kernels: 11.2 us -> 8.61 us  [the longest x1 5.03 us: on_device(): pl.pallas_call(functools.partial(backward_kernel, places), out_shape=(sha...]
    pallas_call x1, Pallas kernels: 2.28 us -> 4.15 us  [on_device(): pl.pallas_call(late_kernel, out_shape=(shape((rows, width), bf16), shape(...]
  transfers between devices with their start and end apart: 21 -> 23, of which waited for: 7 -> 8; matrix products, arithmetic and copies ran while one was open for 2% -> 2% of each run, Pallas kernels for 16% -> 10%
where the time goes in v4:
time: 79.1 us; the launch traced here: 78.8 us
  starting transfers between devices  38.9 us (49%)
  Pallas kernels  18.3 us (23%)
  waiting for transfers between devices  18.1 us (23%)
  local copies, waits for them, and re-layouts  1.73 us (2%)
  other arithmetic  0.95 us (1%)
  between operations  0.81 us (1%)
    ppermute x21, starting transfers between devices, across(): return lax.ppermute(array, axis, [(i, i ^ mask) for i in range(count)])  24.7 us
    all_to_all x1, waiting for transfers between devices, on_device(): lax.all_to_all(kv_part.reshape(n_y * n_x, n_hi * n_lh * chunk, 2 * DH), P...  9.86 us
    all_to_all x1, starting transfers between devices, on_device(): lax.all_to_all(kv_part.reshape(n_y * n_x, n_hi * n_lh * chunk, 2 * DH), P...  7.21 us
    all_to_all x1, starting transfers between devices, on_device(): kv = lax.all_to_all(sent, PLANE, 0, 0, tiled=True).reshape(-1, 2 * DH)  7.03 us
    ppermute x21, waiting for transfers between devices, across(): return lax.ppermute(array, axis, [(i, i ^ mask) for i in range(count)])  6.08 us
    pallas_call x1, Pallas kernels, on_device(): pl.pallas_call(functools.partial(backward_kernel, places), out_shape=(sha...  5.03 us
    pallas_call x1, Pallas kernels, on_device(): pl.pallas_call(expert_kernel, out_shape=(shape((CAP, half), bf16), shape(...  4.73 us
    pallas_call x1, Pallas kernels, on_device(): pl.pallas_call(late_kernel, out_shape=(shape((rows, width), bf16), shape(...  4.15 us
  transfers between devices with their start and end apart: 23, of which 8 were waited for; matrix products, arithmetic and copies ran while one was open for 2% of the time, Pallas kernels for 10%

profile of v4, /device:TPU:32, one launch (start us, length us, event | category | flops | bytes accessed | tf_op | source)
XLA Modules:
  0.0 78.8 jit_solution(14009767275801365195)
XLA Ops:
  0.7 0.8 dynamic-slice_bitcast_fusion.4
  1.4 0.1 iota.7.flags
  1.5 0.0 copy-start
  1.5 4.7 %expert.1 = (bf16[16,2048]{1,0:T(8,128)(2,1)S(1)}, f32[16,2048]{1,0:T(8,128)S(1)}, bf16[16,128]{1,0:T(8,128)(2,1)S(1)}, bf16[16,4096]{1,0:T(8,128)(2,1)S(1)}, bf...) custom-call(f32[8,128]{1,0:T(8,128)S(1)} %iota.7.flags, s32[8,128]{1,0:T(8,128)} %bitcast.38, f32[8,128]{1,0:T(8,128)} %bitcast.39, ...), custom_call_target="tpu_custom_call" | custom-call | flops 125829120 | bytes 8388608 | tf_op jit(solution)/shard_map/expert/pallas_call | solution.py:348
  6.2 0.1 collective-permute-start
  6.3 0.0 copy-done
  6.4 0.5 collective-permute-start.5
  6.8 5.4 %collective-permute-start.11 = (bf16[2,16,256]{2,1,0:T(8,128)(2,1)S(1)}, bf16[2,16,256]{2,1,0:T(8,128)(2,1)S(1)}, u32[]{:S(2)}, u32[]{:S(2)}) collective-permute-start(bf16[2,16,256]{2,1,0:T(8,128)(2,1)S(1)} %pad_maximum_fusion), channel_id=1, source_target_pairs={{0,36},{4,32},{32,4},{36,0},{1,37},{5,33},{33,5},{37,1},{2,38},{6,... | collective-permute-start | bytes 49160 | tf_op jit(solution)/shard_map/ppermute | solution.py:315
  12.2 0.0 collective-permute-done
  12.3 1.1 %collective-permute-start.3 = (bf16[16,2048]{1,0:T(8,128)(2,1)S(1)}, bf16[16,2048]{1,0:T(8,128)(2,1)S(1)}, u32[]{:S(2)}, u32[]{:S(2)}) collective-permute-start(bf16[16,2048]{1,0:T(8,128)(2,1)S(1)} %add_convert_fusion.2), channel_id=1, source_target_pairs={{0,6},{2,4},{4,2},{6,0},{1,7},{3,5},{5,3},{7,1},{8,14},{10,12},{12... | collective-permute-start | bytes 196616 | tf_op jit(solution)/shard_map/ppermute | solution.py:315
  13.4 2.4 %collective-permute-start.2 = (bf16[16,2048]{1,0:T(8,128)(2,1)S(1)}, bf16[16,2048]{1,0:T(8,128)(2,1)S(1)}, u32[]{:S(2)}, u32[]{:S(2)}) collective-permute-start(bf16[16,2048]{1,0:T(8,128)(2,1)S(1)} %add_convert_fusion.2), channel_id=1, source_target_pairs={{0,4},{2,6},{4,0},{6,2},{1,5},{3,7},{5,1},{7,3},{8,12},{10,14},{12... | collective-permute-start | bytes 196616 | tf_op jit(solution)/shard_map/ppermute | solution.py:315
  15.7 0.1 collective-permute-start.1
  15.8 0.0 collective-permute-done.11
  15.9 0.9 %broadcast_in_dim.20 = bf16[16,2,2,16,256]{4,3,2,1,0:T(8,128)(2,1)} broadcast(bf16[2,2,16,256]{3,2,1,0:T(8,128)(2,1)S(1)} %maximum_select_fusion), dimensions={1,2,3,4} | broadcast | bytes 557056 | tf_op jit(solution)/shard_map/broadcast_in_dim | solution.py:385
  16.7 7.0 %all-to-all-start = ((bf16[16,2,2,16,256]{4,3,2,1,0:T(8,128)(2,1)}), bf16[16,2,2,16,256]{4,3,2,1,0:T(8,128)(2,1)S(1)}, u32[]{:S(2)}, u32[]{:S(2)}) async-start(bf16[16,2,2,16,256]{4,3,2,1,0:T(8,128)(2,1)} %broadcast_in_dim.20), calls=%async_computation | async-start | bytes 1048576 | tf_op jit(solution)/shard_map/all_to_all | solution.py:388
  23.8 0.0 collective-permute-done.3
  23.8 0.0 collective-permute-done.2
  23.8 0.0 collective-permute-done.1
  23.8 0.1 collective-permute-start.4
  23.9 2.0 %collective-permute-start.6 = (bf16[128,512]{1,0:T(8,128)(2,1)S(1)}, bf16[128,512]{1,0:T(8,128)(2,1)S(1)}, u32[]{:S(2)}, u32[]{:S(2)}) collective-permute-start(bf16[128,512]{1,0:T(8,128)(2,1)S(1)} %copy-done), channel_id=1, source_target_pairs={{0,2},{1,3},{2,0},{3,1},{4,6},{5,7},{6,4},{7,5},{8,10},{9,11},{10,... | collective-permute-start | bytes 393224 | tf_op jit(solution)/shard_map/ppermute | solution.py:315
  25.9 0.1 collective-permute-start.7
  26.0 0.0 collective-permute-done.4.other
  26.0 0.0 copy-start.1
  26.0 4.2 %late.1 = (bf16[128,4096]{1,0:T(8,128)(2,1)}, bf16[512,128]{1,0:T(8,128)(2,1)S(1)}) custom-call(f32[8,128]{1,0:T(8,128)S(1)} %iota.7.flags, bf16[16,2048]{1,0:T(8,128)(2,1)S(1)} %add_convert_fusion.1.summed, bf16[16,2048]{1,0:T(8,128)(2,1)S(1)} %collective-permute-done.4.other, bf16[16,4096]{1,0:T(8,128)(2,1)S(1)} %get-tuple-element.29.resid16, ...), custom_call_target="tpu_custom_call" | custom-call | flops 1048576 | bytes 65536 | tf_op jit(solution)/shard_map/late/pallas_call | solution.py:393
  30.2 0.3 collective-permute-start.8
  30.4 1.9 %collective-permute-start.9 = (bf16[512,128]{1,0:T(8,128)(2,1)S(1)}, bf16[512,128]{1,0:T(8,128)(2,1)S(1)}, u32[]{:S(2)}, u32[]{:S(2)}) collective-permute-start(bf16[512,128]{1,0:T(8,128)(2,1)S(1)} %get-tuple-element.34.grad0), channel_id=1, source_target_pairs={{0,2},{1,3},{2,0},{3,1},{4,6},{5,7},{6,4},{7,5},{8,10},{9,11},{10,... | collective-permute-start | bytes 393224 | tf_op jit(solution)/shard_map/ppermute | solution.py:315
  32.3 0.0 collective-permute-done.5.q1
  32.3 0.0 collective-permute-start.10
  32.4 0.1 pad_add_fusion.place
  32.4 0.0 collective-permute-done.6.q2
  32.4 0.1 collective-permute-done.7.q3
  32.5 2.1 %all-to-all-done = bf16[16,2,2,16,256]{4,3,2,1,0:T(8,128)(2,1)S(1)} async-done(((bf16[16,2,2,16,256]{4,3,2,1,0:T(8,128)(2,1)}), bf16[16,2,2,16,256]{4,3,2,1,0:T(8,128)(2,1)S(1)}, u32[]{:S(2)}, u32[]{:S(2)}) %all-to-all-start) | async-done | bytes 524320 | tf_op jit(solution)/shard_map/all_to_all | solution.py:388
  34.6 0.0 copy-done.1
  34.6 3.6 %forward.1 = (bf16[1024,2048]{1,0:T(8,128)(2,1)S(1)}, f32[128,2048]{1,0:T(8,128)S(1)}, f32[8,2048]{1,0:T(8,128)S(1)}) custom-call(s32[2]{0:T(128)S(1)} %pad_add_fusion.place, s32[64]{0:T(128)S(1)} %copy-done.1, bf16[128,512]{1,0:T(8,128)(2,1)S(1)} %copy-done, bf16[128,512]{1,0:T(8,128)(2,1)S(1)} %collective-permute-done.5.q1, ...), custom_call_target="tpu_custom_call" | custom-call | flops 1073741824 | bytes 6291456 | tf_op jit(solution)/shard_map/forward/pallas_call | solution.py:417
  38.2 0.0 collective-permute-done.8.grad1
  38.2 0.0 collective-permute-done.9.grad2
  38.2 0.1 collective-permute-done.10.grad3
  38.4 0.2 merge.1
  38.6 0.5 collective-permute-start.12
  39.1 1.7 %collective-permute-start.13 = (f32[8,768]{1,0:T(8,128)S(1)}, f32[8,768]{1,0:T(8,128)S(1)}, u32[]{:S(2)}, u32[]{:S(2)}) collective-permute-start(f32[8,768]{1,0:T(8,128)S(1)} %get-tuple-element.39.stats0), channel_id=1, source_target_pairs={{0,2},{1,3},{2,0},{3,1},{4,6},{5,7},{6,4},{7,5},{8,10},{9,11},{10,... | collective-permute-start | bytes 73736 | tf_op jit(solution)/shard_map/ppermute | solution.py:315
  40.8 0.0 collective-permute-start.14
  40.8 0.0 collective-permute-done.12.stats1
  40.8 2.1 %collective-permute-done.13.stats2 = f32[8,768]{1,0:T(8,128)S(1)} collective-permute-done((f32[8,768]{1,0:T(8,128)S(1)}, f32[8,768]{1,0:T(8,128)S(1)}, u32[]{:S(2)}, u32[]{:S(2)}) %collective-permute-start.13) | collective-permute-done | bytes 24608 | tf_op jit(solution)/shard_map/ppermute | solution.py:315
  42.9 1.4 %collective-permute-done.14.stats3 = f32[8,768]{1,0:T(8,128)S(1)} collective-permute-done((f32[8,768]{1,0:T(8,128)S(1)}, f32[8,768]{1,0:T(8,128)S(1)}, u32[]{:S(2)}, u32[]{:S(2)}) %collective-permute-start.14) | collective-permute-done | bytes 24608 | tf_op jit(solution)/shard_map/ppermute | solution.py:315
  44.3 5.0 %backward.1 = (bf16[1024,256]{1,0:T(8,128)(2,1)}, f32[128,512]{1,0:T(8,128)S(1)}, bf16[128,512]{1,0:T(8,128)(2,1)S(1)}, bf16[128,512]{1,0:T(8,128)(2,1)S(1)}, bf16[128,512]{1,0:T(8,128)(2,1)S(1)}) custom-call(bf16[128,512]{1,0:T(8,128)(2,1)S(1)} %copy-done, bf16[128,512]{1,0:T(8,128)(2,1)S(1)} %collective-permute-done.5.q1, ...), custom_call_target="tpu_custom_call" | custom-call | flops 2147483648 | bytes 8388608 | tf_op jit(solution)/shard_map/backward/pallas_call | solution.py:450
  49.4 7.2 %all-to-all-start.1 = ((bf16[16,64,256]{2,1,0:T(8,128)(2,1)}), bf16[16,64,256]{2,1,0:T(8,128)(2,1)S(1)}, u32[]{:S(2)}, u32[]{:S(2)}) async-start(bf16[16,64,256]{2,1,0:T(8,128)(2,1)} %bitcast.16), calls=%async_computation.1 | async-start | bytes 1048576 | tf_op jit(solution)/shard_map/all_to_all | solution.py:466
  56.6 0.1 collective-permute-start.17
  56.7 1.4 %collective-permute-start.16 = (bf16[128,512]{1,0:T(8,128)(2,1)S(1)}, bf16[128,512]{1,0:T(8,128)(2,1)S(1)}, u32[]{:S(2)}, u32[]{:S(2)}) collective-permute-start(bf16[128,512]{1,0:T(8,128)(2,1)S(1)} %get-tuple-element.43), channel_id=1, source_target_pairs={{0,2},{1,3},{2,0},{3,1},{4,6},{5,7},{6,4},{7,5},{8,10},{9,11},{10,... | collective-permute-start | bytes 393224 | tf_op jit(solution)/shard_map/ppermute | solution.py:315
  58.1 0.4 collective-permute-start.15
  58.5 9.9 %all-to-all-done.1 = bf16[16,64,256]{2,1,0:T(8,128)(2,1)S(1)} async-done(((bf16[16,64,256]{2,1,0:T(8,128)(2,1)}), bf16[16,64,256]{2,1,0:T(8,128)(2,1)S(1)}, u32[]{:S(2)}, u32[]{:S(2)}) %all-to-all-start.1) | async-done | bytes 524320 | tf_op jit(solution)/shard_map/all_to_all | solution.py:466
  68.4 0.1 reduce_sum.12
  68.5 0.8 %collective-permute-start.18 = (bf16[16,256]{1,0:T(8,128)(2,1)S(1)}, bf16[16,256]{1,0:T(8,128)(2,1)S(1)}, u32[]{:S(2)}, u32[]{:S(2)}) collective-permute-start(bf16[16,256]{1,0:T(8,128)(2,1)S(1)} %get-tuple-element.54), channel_id=1, source_target_pairs={{0,4},{4,0},{32,36},{36,32},{1,5},{5,1},{33,37},{37,33},{2,6},{6,2... | collective-permute-start | bytes 24584 | tf_op jit(solution)/shard_map/ppermute | solution.py:315
  69.3 3.0 %collective-permute-start.19 = (bf16[16,256]{1,0:T(8,128)(2,1)S(1)}, bf16[16,256]{1,0:T(8,128)(2,1)S(1)}, u32[]{:S(2)}, u32[]{:S(2)}) collective-permute-start(bf16[16,256]{1,0:T(8,128)(2,1)S(1)} %get-tuple-element.53), channel_id=1, source_target_pairs={{0,32},{4,36},{32,0},{36,4},{1,33},{5,37},{33,1},{37,5},{2,34},{6,... | collective-permute-start | bytes 24584 | tf_op jit(solution)/shard_map/ppermute | solution.py:315
  72.4 0.0 collective-permute-done.17
  72.4 2.7 %collective-permute-start.20 = (bf16[16,256]{1,0:T(8,128)(2,1)S(1)}, bf16[16,256]{1,0:T(8,128)(2,1)S(1)}, u32[]{:S(2)}, u32[]{:S(2)}) collective-permute-start(bf16[16,256]{1,0:T(8,128)(2,1)S(1)} %get-tuple-element.52), channel_id=1, source_target_pairs={{0,36},{4,32},{32,4},{36,0},{1,37},{5,33},{33,5},{37,1},{2,38},{6,... | collective-permute-start | bytes 24584 | tf_op jit(solution)/shard_map/ppermute | solution.py:315
  75.1 0.0 collective-permute-done.16
  75.1 0.0 collective-permute-done.15
  75.1 0.7 add_convert_fusion
  75.8 0.0 collective-permute-done.18.lower
  75.8 1.1 %collective-permute-done.19.upper = bf16[16,256]{1,0:T(8,128)(2,1)S(1)} collective-permute-done((bf16[16,256]{1,0:T(8,128)(2,1)S(1)}, bf16[16,256]{1,0:T(8,128)(2,1)S(1)}, u32[]{:S(2)}, u32[]{:S(2)}) %collective-permute-start.19) | collective-permute-done | bytes 8224 | tf_op jit(solution)/shard_map/ppermute | solution.py:315
  76.9 1.3 %collective-permute-done.20.both = bf16[16,256]{1,0:T(8,128)(2,1)S(1)} collective-permute-done((bf16[16,256]{1,0:T(8,128)(2,1)S(1)}, bf16[16,256]{1,0:T(8,128)(2,1)S(1)}, u32[]{:S(2)}, u32[]{:S(2)}) %collective-permute-start.20) | collective-permute-done | bytes 8224 | tf_op jit(solution)/shard_map/ppermute | solution.py:315
  78.1 0.6 final.1
  (7 shorter events, 0.1 us)
Async XLA Ops:
  1.5 4.8 %copy-start = (bf16[128,512]{1,0:T(8,128)(2,1)S(1)}, bf16[128,512]{1,0:T(8,128)(2,1)}, u32[]{:S(2)}) copy-start(bf16[128,512]{1,0:T(8,128)(2,1)} %q0.3) | copy-start | bytes 393220
  6.2 6.0 %collective-permute-start = (bf16[16,2048]{1,0:T(8,128)(2,1)S(1)}, bf16[16,2048]{1,0:T(8,128)(2,1)S(1)}, u32[]{:S(2)}, u32[]{:S(2)}) collective-permute-start(bf16[16,2048]{1,0:T(8,128)(2,1)S(1)} %get-tuple-element.28), channel_id=1, source_target_pairs={{0,1},{1,0},{2,3},{3,2},{4,5},{5,4},{6,7},{7,6},{8,9},{9,8},{10,11... | collective-permute-start | bytes 196616 | tf_op jit(solution)/shard_map/ppermute | solution.py:315
  6.4 26.0 %collective-permute-start.5 = (bf16[128,512]{1,0:T(8,128)(2,1)S(1)}, bf16[128,512]{1,0:T(8,128)(2,1)S(1)}, u32[]{:S(2)}, u32[]{:S(2)}) collective-permute-start(bf16[128,512]{1,0:T(8,128)(2,1)S(1)} %copy-done), channel_id=1, source_target_pairs={{0,1},{1,0},{2,3},{3,2},{4,5},{5,4},{6,7},{7,6},{8,9},{9,8},{10,11... | collective-permute-start | bytes 393224 | tf_op jit(solution)/shard_map/ppermute | solution.py:315
  6.8 9.0 %collective-permute-start.11 = (bf16[2,16,256]{2,1,0:T(8,128)(2,1)S(1)}, bf16[2,16,256]{2,1,0:T(8,128)(2,1)S(1)}, u32[]{:S(2)}, u32[]{:S(2)}) collective-permute-start(bf16[2,16,256]{2,1,0:T(8,128)(2,1)S(1)} %pad_maximum_fusion), channel_id=1, source_target_pairs={{0,36},{4,32},{32,4},{36,0},{1,37},{5,33},{33,5},{37,1},{2,38},{6,... | collective-permute-start | bytes 49160 | tf_op jit(solution)/shard_map/ppermute | solution.py:315
  12.3 11.5 %collective-permute-start.3 = (bf16[16,2048]{1,0:T(8,128)(2,1)S(1)}, bf16[16,2048]{1,0:T(8,128)(2,1)S(1)}, u32[]{:S(2)}, u32[]{:S(2)}) collective-permute-start(bf16[16,2048]{1,0:T(8,128)(2,1)S(1)} %add_convert_fusion.2), channel_id=1, source_target_pairs={{0,6},{2,4},{4,2},{6,0},{1,7},{3,5},{5,3},{7,1},{8,14},{10,12},{12... | collective-permute-start | bytes 196616 | tf_op jit(solution)/shard_map/ppermute | solution.py:315
  13.4 10.4 %collective-permute-start.2 = (bf16[16,2048]{1,0:T(8,128)(2,1)S(1)}, bf16[16,2048]{1,0:T(8,128)(2,1)S(1)}, u32[]{:S(2)}, u32[]{:S(2)}) collective-permute-start(bf16[16,2048]{1,0:T(8,128)(2,1)S(1)} %add_convert_fusion.2), channel_id=1, source_target_pairs={{0,4},{2,6},{4,0},{6,2},{1,5},{3,7},{5,1},{7,3},{8,12},{10,14},{12... | collective-permute-start | bytes 196616 | tf_op jit(solution)/shard_map/ppermute | solution.py:315
  15.7 8.1 %collective-permute-start.1 = (bf16[16,2048]{1,0:T(8,128)(2,1)S(1)}, bf16[16,2048]{1,0:T(8,128)(2,1)S(1)}, u32[]{:S(2)}, u32[]{:S(2)}) collective-permute-start(bf16[16,2048]{1,0:T(8,128)(2,1)S(1)} %add_convert_fusion.2), channel_id=1, source_target_pairs={{0,2},{2,0},{4,6},{6,4},{1,3},{3,1},{5,7},{7,5},{8,10},{10,8},{12,... | collective-permute-start | bytes 196616 | tf_op jit(solution)/shard_map/ppermute | solution.py:315
  16.7 17.9 %all-to-all-start = ((bf16[16,2,2,16,256]{4,3,2,1,0:T(8,128)(2,1)}), bf16[16,2,2,16,256]{4,3,2,1,0:T(8,128)(2,1)S(1)}, u32[]{:S(2)}, u32[]{:S(2)}) async-start(bf16[16,2,2,16,256]{4,3,2,1,0:T(8,128)(2,1)} %broadcast_in_dim.20), calls=%async_computation | async-start | bytes 1048576 | tf_op jit(solution)/shard_map/all_to_all | solution.py:388
  23.8 2.2 %collective-permute-start.4 = (bf16[16,2048]{1,0:T(8,128)(2,1)S(1)}, bf16[16,2048]{1,0:T(8,128)(2,1)S(1)}, u32[]{:S(2)}, u32[]{:S(2)}) collective-permute-start(bf16[16,2048]{1,0:T(8,128)(2,1)S(1)} %add_convert_fusion.1.summed), channel_id=1, source_target_pairs={{0,1},{1,0},{2,3},{3,2},{4,5},{5,4},{6,7},{7,6},{8,9},{9,8},{10,11... | collective-permute-start | bytes 196616 | tf_op jit(solution)/shard_map/ppermute | solution.py:315
  23.9 8.5 %collective-permute-start.6 = (bf16[128,512]{1,0:T(8,128)(2,1)S(1)}, bf16[128,512]{1,0:T(8,128)(2,1)S(1)}, u32[]{:S(2)}, u32[]{:S(2)}) collective-permute-start(bf16[128,512]{1,0:T(8,128)(2,1)S(1)} %copy-done), channel_id=1, source_target_pairs={{0,2},{1,3},{2,0},{3,1},{4,6},{5,7},{6,4},{7,5},{8,10},{9,11},{10,... | collective-permute-start | bytes 393224 | tf_op jit(solution)/shard_map/ppermute | solution.py:315
  25.9 6.6 %collective-permute-start.7 = (bf16[128,512]{1,0:T(8,128)(2,1)S(1)}, bf16[128,512]{1,0:T(8,128)(2,1)S(1)}, u32[]{:S(2)}, u32[]{:S(2)}) collective-permute-start(bf16[128,512]{1,0:T(8,128)(2,1)S(1)} %copy-done), channel_id=1, source_target_pairs={{0,3},{1,2},{2,1},{3,0},{4,7},{5,6},{6,5},{7,4},{8,11},{9,10},{10,... | collective-permute-start | bytes 393224 | tf_op jit(solution)/shard_map/ppermute | solution.py:315
  26.0 8.6 %copy-start.1 = (s32[64]{0:T(128)S(1)}, s32[64]{0:T(128)}, u32[]{:S(2)}) copy-start(s32[64]{0:T(128)} %spans.1) | copy-start | bytes 772
  30.2 8.1 %collective-permute-start.8 = (bf16[512,128]{1,0:T(8,128)(2,1)S(1)}, bf16[512,128]{1,0:T(8,128)(2,1)S(1)}, u32[]{:S(2)}, u32[]{:S(2)}) collective-permute-start(bf16[512,128]{1,0:T(8,128)(2,1)S(1)} %get-tuple-element.34.grad0), channel_id=1, source_target_pairs={{0,1},{1,0},{2,3},{3,2},{4,5},{5,4},{6,7},{7,6},{8,9},{9,8},{10,11... | collective-permute-start | bytes 393224 | tf_op jit(solution)/shard_map/ppermute | solution.py:315
  30.4 7.8 %collective-permute-start.9 = (bf16[512,128]{1,0:T(8,128)(2,1)S(1)}, bf16[512,128]{1,0:T(8,128)(2,1)S(1)}, u32[]{:S(2)}, u32[]{:S(2)}) collective-permute-start(bf16[512,128]{1,0:T(8,128)(2,1)S(1)} %get-tuple-element.34.grad0), channel_id=1, source_target_pairs={{0,2},{1,3},{2,0},{3,1},{4,6},{5,7},{6,4},{7,5},{8,10},{9,11},{10,... | collective-permute-start | bytes 393224 | tf_op jit(solution)/shard_map/ppermute | solution.py:315
  32.3 6.0 %collective-permute-start.10 = (bf16[512,128]{1,0:T(8,128)(2,1)S(1)}, bf16[512,128]{1,0:T(8,128)(2,1)S(1)}, u32[]{:S(2)}, u32[]{:S(2)}) collective-permute-start(bf16[512,128]{1,0:T(8,128)(2,1)S(1)} %get-tuple-element.34.grad0), channel_id=1, source_target_pairs={{0,3},{1,2},{2,1},{3,0},{4,7},{5,6},{6,5},{7,4},{8,11},{9,10},{10,... | collective-permute-start | bytes 393224 | tf_op jit(solution)/shard_map/ppermute | solution.py:315
  38.6 2.2 %collective-permute-start.12 = (f32[8,768]{1,0:T(8,128)S(1)}, f32[8,768]{1,0:T(8,128)S(1)}, u32[]{:S(2)}, u32[]{:S(2)}) collective-permute-start(f32[8,768]{1,0:T(8,128)S(1)} %get-tuple-element.39.stats0), channel_id=1, source_target_pairs={{0,1},{1,0},{2,3},{3,2},{4,5},{5,4},{6,7},{7,6},{8,9},{9,8},{10,11... | collective-permute-start | bytes 73736 | tf_op jit(solution)/shard_map/ppermute | solution.py:315
  39.1 3.8 %collective-permute-start.13 = (f32[8,768]{1,0:T(8,128)S(1)}, f32[8,768]{1,0:T(8,128)S(1)}, u32[]{:S(2)}, u32[]{:S(2)}) collective-permute-start(f32[8,768]{1,0:T(8,128)S(1)} %get-tuple-element.39.stats0), channel_id=1, source_target_pairs={{0,2},{1,3},{2,0},{3,1},{4,6},{5,7},{6,4},{7,5},{8,10},{9,11},{10,... | collective-permute-start | bytes 73736 | tf_op jit(solution)/shard_map/ppermute | solution.py:315
  40.8 3.5 %collective-permute-start.14 = (f32[8,768]{1,0:T(8,128)S(1)}, f32[8,768]{1,0:T(8,128)S(1)}, u32[]{:S(2)}, u32[]{:S(2)}) collective-permute-start(f32[8,768]{1,0:T(8,128)S(1)} %get-tuple-element.39.stats0), channel_id=1, source_target_pairs={{0,3},{1,2},{2,1},{3,0},{4,7},{5,6},{6,5},{7,4},{8,11},{9,10},{10,... | collective-permute-start | bytes 73736 | tf_op jit(solution)/shard_map/ppermute | solution.py:315
  49.4 19.0 %all-to-all-start.1 = ((bf16[16,64,256]{2,1,0:T(8,128)(2,1)}), bf16[16,64,256]{2,1,0:T(8,128)(2,1)S(1)}, u32[]{:S(2)}, u32[]{:S(2)}) async-start(bf16[16,64,256]{2,1,0:T(8,128)(2,1)} %bitcast.16), calls=%async_computation.1 | async-start | bytes 1048576 | tf_op jit(solution)/shard_map/all_to_all | solution.py:466
  56.6 15.8 %collective-permute-start.17 = (bf16[128,512]{1,0:T(8,128)(2,1)S(1)}, bf16[128,512]{1,0:T(8,128)(2,1)S(1)}, u32[]{:S(2)}, u32[]{:S(2)}) collective-permute-start(bf16[128,512]{1,0:T(8,128)(2,1)S(1)} %get-tuple-element.44), channel_id=1, source_target_pairs={{0,3},{1,2},{2,1},{3,0},{4,7},{5,6},{6,5},{7,4},{8,11},{9,10},{10,... | collective-permute-start | bytes 393224 | tf_op jit(solution)/shard_map/ppermute | solution.py:315
  56.7 18.4 %collective-permute-start.16 = (bf16[128,512]{1,0:T(8,128)(2,1)S(1)}, bf16[128,512]{1,0:T(8,128)(2,1)S(1)}, u32[]{:S(2)}, u32[]{:S(2)}) collective-permute-start(bf16[128,512]{1,0:T(8,128)(2,1)S(1)} %get-tuple-element.43), channel_id=1, source_target_pairs={{0,2},{1,3},{2,0},{3,1},{4,6},{5,7},{6,4},{7,5},{8,10},{9,11},{10,... | collective-permute-start | bytes 393224 | tf_op jit(solution)/shard_map/ppermute | solution.py:315
  58.1 17.0 %collective-permute-start.15 = (bf16[128,512]{1,0:T(8,128)(2,1)S(1)}, bf16[128,512]{1,0:T(8,128)(2,1)S(1)}, u32[]{:S(2)}, u32[]{:S(2)}) collective-permute-start(bf16[128,512]{1,0:T(8,128)(2,1)S(1)} %get-tuple-element.42), channel_id=1, source_target_pairs={{0,1},{1,0},{2,3},{3,2},{4,5},{5,4},{6,7},{7,6},{8,9},{9,8},{10,11... | collective-permute-start | bytes 393224 | tf_op jit(solution)/shard_map/ppermute | solution.py:315
  68.5 7.3 %collective-permute-start.18 = (bf16[16,256]{1,0:T(8,128)(2,1)S(1)}, bf16[16,256]{1,0:T(8,128)(2,1)S(1)}, u32[]{:S(2)}, u32[]{:S(2)}) collective-permute-start(bf16[16,256]{1,0:T(8,128)(2,1)S(1)} %get-tuple-element.54), channel_id=1, source_target_pairs={{0,4},{4,0},{32,36},{36,32},{1,5},{5,1},{33,37},{37,33},{2,6},{6,2... | collective-permute-start | bytes 24584 | tf_op jit(solution)/shard_map/ppermute | solution.py:315
  69.3 7.6 %collective-permute-start.19 = (bf16[16,256]{1,0:T(8,128)(2,1)S(1)}, bf16[16,256]{1,0:T(8,128)(2,1)S(1)}, u32[]{:S(2)}, u32[]{:S(2)}) collective-permute-start(bf16[16,256]{1,0:T(8,128)(2,1)S(1)} %get-tuple-element.53), channel_id=1, source_target_pairs={{0,32},{4,36},{32,0},{36,4},{1,33},{5,37},{33,1},{37,5},{2,34},{6,... | collective-permute-start | bytes 24584 | tf_op jit(solution)/shard_map/ppermute | solution.py:315
  72.4 5.8 %collective-permute-start.20 = (bf16[16,256]{1,0:T(8,128)(2,1)S(1)}, bf16[16,256]{1,0:T(8,128)(2,1)S(1)}, u32[]{:S(2)}, u32[]{:S(2)}) collective-permute-start(bf16[16,256]{1,0:T(8,128)(2,1)S(1)} %get-tuple-element.52), channel_id=1, source_target_pairs={{0,36},{4,32},{32,4},{36,0},{1,37},{5,33},{33,5},{37,1},{2,38},{6,... | collective-permute-start | bytes 24584 | tf_op jit(solution)/shard_map/ppermute | solution.py:315

commit v5 on v4

--- a/solution.py
+++ b/solution.py
@@ -19,7 +19,6 @@
 EXP = ("lh", "lb", "core")
 CLIQUE = ("lb", "core")
 PLANE = ("y", "x")
-RING = (0, 1, 2, 3)
 
 bf16 = jnp.bfloat16
 f32 = jnp.float32
@@ -52,11 +51,11 @@
 
 def expert_kernel(
     flags, ids_far, combine_far, gain_far, resid, out_grad, w_gate, w_up, w_down,
-    give, keep, selector, resid16, grad16, gain,
-    ids, combine, resid_in, grad_in, wide_in, down_in, sems,
+    keys, values, give, keep, selector, resid16, grad16, gain, own_kv, leaving_kv,
+    ids, combine, resid_in, grad_in, wide_in, down_in, keys_in, values_in, sems,
 ):
     hidden_rows = w_down.shape[0]
-    cuts = (sems.shape[0] - 5) // 3
+    cuts = (sems.shape[0] - 7) // 3
     step = w_down.shape[1] // cuts
     heads = [
         pltpu.make_async_copy(source, target, sems.at[i])
@@ -67,6 +66,8 @@
                 (gain_far, gain),
                 (resid, resid_in),
                 (out_grad, grad_in),
+                (keys, keys_in),
+                (values, values_in),
             ]
         )
     ]
@@ -74,7 +75,7 @@
     bodies = [
         [
             pltpu.make_async_copy(
-                source.at[:, span], target.at[pl.ds(row, hidden_rows), span], sems.at[5 + 3 * i + j]
+                source.at[:, span], target.at[pl.ds(row, hidden_rows), span], sems.at[7 + 3 * i + j]
             )
             for j, (source, target, row) in enumerate(
                 [(w_gate, wide_in, 0), (w_up, wide_in, hidden_rows), (w_down, down_in, 0)]
@@ -87,8 +88,18 @@
     for body in bodies[:AHEAD]:
         for copy in body:
             copy.start()
-    for copy in heads[:3]:
+    for copy in heads[:3] + heads[5:]:
         copy.wait()
+    core, high_head, upper_pair = [flags[i : i + 1, 0:1] > 0.5 for i in range(3)]
+    chunk = own_kv.shape[1]
+    for i in range(own_kv.shape[0]):
+        for side, source in enumerate((keys_in, values_in)):
+            p = [source[(4 * i + k) * chunk : (4 * i + k + 1) * chunk] for k in range(4)]
+            mine = jnp.where(upper_pair, jnp.where(core, p[3], p[2]), jnp.where(core, p[1], p[0]))
+            left, right = mine[:, :DH], mine[:, DH:]
+            to = slice(side * DH, (side + 1) * DH)
+            own_kv[i, :, to] = jnp.where(high_head, right, left)
+            leaving_kv[i, :, to] = jnp.where(high_head, left, right)
     rows = ids.shape[1]
     hit = ids[...] == 0
     chosen_row = jnp.sum(jnp.where(hit, 1.0, 0.0), axis=0, keepdims=True)
@@ -254,9 +265,9 @@
 
 
 def backward_kernel(
-    order, q0, q1, q2, q3, grads_in, stats0, stats1, stats2, stats3, kv, weights,
+    q0, q1, q2, q3, grads_in, stats0, stats1, stats2, stats3, kv, weights,
     kv_part, own, part1, part2, part3,
-    q_all, grads, delta, score_grad,
+    q_all, grads, delta, score_grad, kv_near, sems,
 ):
     rows, heads = q0.shape[0], q0.shape[1] // DH
     columns = q_all.shape[0]
@@ -282,22 +293,30 @@
             grads[:, to] = (grads_in[:, to].astype(f32) * near[r : r + 1]).astype(bf16)
 
     key, value = kv[:, :DH], kv[:, DH:]
-    for c in range(0, columns, 2 * rows):
-        at = slice(c, c + 2 * rows)
-        prob_grad = product(value, grads[:, at])
-        score_grad[:, at] = (weights[:, at].astype(f32) * (prob_grad - delta[:, at])).astype(bf16)
-    value_part = product(weights[...], grads[...], 1, 1).astype(bf16)
-    key_part = (product(score_grad[...], q_all[...]) * scale).astype(bf16)
-    group = key.shape[0] // len(order)
-    for g, to in enumerate(order):
-        at, to = slice(g * group, (g + 1) * group), slice(to * group, (to + 1) * group)
-        kv_part[to, :DH] = key_part[at]
-        kv_part[to, DH:] = value_part[at]
+    leaves = []
+    for r in range(0, key.shape[0], 2 * rows):
+        block = slice(r, r + 2 * rows)
+        for c in range(0, columns, 2 * rows):
+            at = slice(c, c + 2 * rows)
+            prob_grad = product(value[block], grads[:, at])
+            weight = weights[block, at].astype(f32)
+            score_grad[block, at] = (weight * (prob_grad - delta[:, at])).astype(bf16)
+        kv_near[block, DH:] = product(weights[block], grads[...], 1, 1).astype(bf16)
+        kv_near[block, :DH] = (product(score_grad[block], q_all[...]) * scale).astype(bf16)
+        part_rows = pl.ds(r, 2 * rows)
+        leaves.append(
+            pltpu.make_async_copy(
+                kv_near.at[part_rows], kv_part.at[part_rows], sems.at[r // (2 * rows)]
+            )
+        )
+        leaves[-1].start()
     for g, part in enumerate([own, part1, part2, part3]):
         total = product(key, score_grad[:, g * wide : (g + 1) * wide], 0, 0)
         for h in range(heads):
             moved = total[:, h * rows : (h + 1) * rows].T * scale
             part[:, h * DH : (h + 1) * DH] = moved.astype(part.dtype)
+    for leave in leaves:
+        leave.wait()
 
 
 def final_kernel(flags, own, lower, upper, both, key_grad, value_grad):
@@ -335,17 +354,10 @@
     n_keys = n_y * n_x * n_hi * n_lh * chunk
     place = jnp.stack([lax.axis_index(CTX), share]).astype(jnp.int32)
     group = lax.axis_index("lh")
-    flags = jnp.where(lax.broadcasted_iota(jnp.int32, (8, 128), 0) == 0, core, group).astype(f32)
-
-    def chunks_of(array, head):
-        split = array.reshape(n_lh, n_share, chunk, n_lh * DH)
-        start = (0, share, 0, head * DH)
-        return lax.dynamic_slice(split, start, (n_lh, 1, chunk, DH))[:, 0]
-
-    def both_of(head):
-        return jnp.concatenate([chunks_of(keys, head), chunks_of(values, head)], axis=2)
-
-    give, keep, selector, resid16, grad16, gain = pl.pallas_call(
+    bits = jnp.stack([core, group, lax.axis_index("lb")])
+    flags = jnp.broadcast_to(bits[:, None], (3, 128)).astype(f32)
+
+    give, keep, selector, resid16, grad16, gain, own_kv, leaving = pl.pallas_call(
         expert_kernel,
         out_shape=(
             shape((CAP, half), bf16),
@@ -354,9 +366,11 @@
             shape((CAP, width), bf16),
             shape((CAP, width), bf16),
             shape((1, width), f32),
+            shape((n_lh, chunk, 2 * DH), bf16),
+            shape((n_lh, chunk, 2 * DH), bf16),
         ),
-        in_specs=[VMEM] + [HBM] * 8,
-        out_specs=(VMEM,) * 6,
+        in_specs=[VMEM] + [HBM] * 10,
+        out_specs=(VMEM,) * 8,
         scratch_shapes=[
             pltpu.VMEM(expert_ids.shape[::-1], jnp.int32),
             pltpu.VMEM(expert_ids.shape[::-1], f32),
@@ -364,7 +378,9 @@
             pltpu.VMEM((rows, width), bf16),
             pltpu.VMEM((2 * hidden, width), bf16),
             pltpu.VMEM((hidden, width), bf16),
-            pltpu.SemaphoreType.DMA((17,)),
+            pltpu.VMEM(keys.shape, bf16),
+            pltpu.VMEM(values.shape, bf16),
+            pltpu.SemaphoreType.DMA((19,)),
         ],
         compiler_params=params(24),
         cost_estimate=cost(10 * CAP * width * hidden, 8 << 20),
@@ -374,12 +390,10 @@
         *map(
             stay,
             (expert_ids.T, combine.T, norm_gain[None, :], resid, out_grad)
-            + (w_gate.T, w_up.T, w_down),
+            + (w_gate.T, w_up.T, w_down, keys, values),
         ),
     )
 
-    own_kv = both_of(group)
-    leaving, give = lax.optimization_barrier((both_of(1 - group), give))
     far_kv = across(leaving, ("hi", "lh"), 3)
     plane_kv = jnp.where(high == 0, jnp.stack([own_kv, far_kv]), jnp.stack([far_kv, own_kv]))
     sent = jnp.broadcast_to(plane_kv[None], (n_y * n_x,) + plane_kv.shape)
@@ -407,8 +421,7 @@
     )(flags, total, other, resid16, grad16, gain, selector, stay(out_grad), stay(w_out))
 
     query_all = shared(queries)
-    tour = list(itertools.product(RING, RING))
-    places = [y * n_x + x for y, x in tour]
+    tour = itertools.product(range(n_y), range(n_x))
     held = [
         ((y * n_hi + hi) * n_x + x, i) for y, x in tour for hi in range(n_hi) for i in range(n_lh)
     ]
@@ -448,16 +461,18 @@
         name="merge",
     )(*shared(attn_grad), out, stats)
     kv_part, query_own, *query_give = pl.pallas_call(
-        functools.partial(backward_kernel, places),
+        backward_kernel,
         out_shape=(shape((n_keys, 2 * DH), bf16), shape((rows, heads * DH), f32))
         + (shape((rows, heads * DH), bf16),) * (n_share - 1),
         in_specs=[VMEM] * (2 * n_share + 3),
-        out_specs=(VMEM,) * (n_share + 1),
+        out_specs=(HBM,) + (VMEM,) * n_share,
         scratch_shapes=[
             pltpu.VMEM((columns, DH), bf16),
             pltpu.VMEM((DH, columns), bf16),
             pltpu.VMEM((1, columns), f32),
             pltpu.VMEM((n_keys, columns), bf16),
+            pltpu.VMEM((n_keys, 2 * DH), bf16),
+            pltpu.SemaphoreType.DMA((n_keys // (2 * rows),)),
         ],
         compiler_params=params(16),
         cost_estimate=cost(4 * pair_flops, 8 << 20),

time: 79.1 us -> 77.9 us (0.985)
  no operation moved by 1% of the time
where the time goes in v5:
time: 77.9 us; the launch traced here: 77.6 us
  starting transfers between devices  38.9 us (50%)
  waiting for transfers between devices  18.1 us (23%)
  Pallas kernels  17.8 us (23%)
  other arithmetic  1.02 us (1%)
  local copies, waits for them, and re-layouts  0.97 us (1%)
  between operations  0.81 us (1%)
    ppermute x21, starting transfers between devices, across(): return lax.ppermute(array, axis, [(i, i ^ mask) for i in range(count)])  24.6 us
    all_to_all x1, waiting for transfers between devices, on_device(): lax.all_to_all(kv_part.reshape(n_y * n_x, n_hi * n_lh * chunk, 2 * DH), P...  9.86 us
    all_to_all x1, starting transfers between devices, on_device(): lax.all_to_all(kv_part.reshape(n_y * n_x, n_hi * n_lh * chunk, 2 * DH), P...  7.23 us
    all_to_all x1, starting transfers between devices, on_device(): kv = lax.all_to_all(sent, PLANE, 0, 0, tiled=True).reshape(-1, 2 * DH)  7.03 us
    ppermute x21, waiting for transfers between devices, across(): return lax.ppermute(array, axis, [(i, i ^ mask) for i in range(count)])  6.09 us
    pallas_call x1, Pallas kernels, on_device(): pl.pallas_call(expert_kernel, out_shape=(shape((CAP, half), bf16), shape(...  4.94 us
    pallas_call x1, Pallas kernels, on_device(): pl.pallas_call(backward_kernel, out_shape=(shape((n_keys, 2 * DH), bf16),...  4.3 us
    pallas_call x1, Pallas kernels, on_device(): pl.pallas_call(late_kernel, out_shape=(shape((rows, width), bf16), shape(...  4.16 us
  transfers between devices with their start and end apart: 23, of which 8 were waited for; matrix products, arithmetic and copies ran while one was open for 2% of the time, Pallas kernels for 10%

profile of v5, /device:TPU:32, one launch (start us, length us, event | category | flops | bytes accessed | tf_op | source)
XLA Modules:
  0.0 77.6 jit_solution(3820812174426961937)
XLA Ops:
  0.6 0.1 add_convert_fusion.3
  0.7 0.1 broadcast_in_dim.6.flags
  0.8 0.0 copy-start
  0.8 4.9 %expert.1 = (bf16[16,2048]{1,0:T(8,128)(2,1)S(1)}, f32[16,2048]{1,0:T(8,128)S(1)}, bf16[16,128]{1,0:T(8,128)(2,1)S(1)}, bf16[16,4096]{1,0:T(8,128)(2,1)S(1)}, bf...) custom-call(f32[3,128]{1,0:T(4,128)S(1)} %broadcast_in_dim.6.flags, ...), custom_call_target="tpu_custom_call" | custom-call | flops 125829120 | bytes 8388608 | tf_op jit(solution)/shard_map/expert/pallas_call | solution.py:360
  5.7 0.1 collective-permute-start
  5.8 0.0 copy-done
  5.8 0.5 collective-permute-start.5
  6.3 5.4 %collective-permute-start.11 = (bf16[2,16,256]{2,1,0:T(8,128)(2,1)S(1)}, bf16[2,16,256]{2,1,0:T(8,128)(2,1)S(1)}, u32[]{:S(2)}, u32[]{:S(2)}) collective-permute-start(bf16[2,16,256]{2,1,0:T(8,128)(2,1)S(1)} %get-tuple-element.35), channel_id=1, source_target_pairs={{0,36},{4,32},{32,4},{36,0},{1,37},{5,33},{33,5},{37,1},{2,38},{6,... | collective-permute-start | bytes 49160 | tf_op jit(solution)/shard_map/ppermute | solution.py:334
  11.7 0.0 collective-permute-done
  11.8 1.1 %collective-permute-start.3 = (bf16[16,2048]{1,0:T(8,128)(2,1)S(1)}, bf16[16,2048]{1,0:T(8,128)(2,1)S(1)}, u32[]{:S(2)}, u32[]{:S(2)}) collective-permute-start(bf16[16,2048]{1,0:T(8,128)(2,1)S(1)} %add_convert_fusion.2), channel_id=1, source_target_pairs={{0,6},{2,4},{4,2},{6,0},{1,7},{3,5},{5,3},{7,1},{8,14},{10,12},{12... | collective-permute-start | bytes 196616 | tf_op jit(solution)/shard_map/ppermute | solution.py:334
  12.8 2.4 %collective-permute-start.2 = (bf16[16,2048]{1,0:T(8,128)(2,1)S(1)}, bf16[16,2048]{1,0:T(8,128)(2,1)S(1)}, u32[]{:S(2)}, u32[]{:S(2)}) collective-permute-start(bf16[16,2048]{1,0:T(8,128)(2,1)S(1)} %add_convert_fusion.2), channel_id=1, source_target_pairs={{0,4},{2,6},{4,0},{6,2},{1,5},{3,7},{5,1},{7,3},{8,12},{10,14},{12... | collective-permute-start | bytes 196616 | tf_op jit(solution)/shard_map/ppermute | solution.py:334
  15.2 0.1 collective-permute-start.1
  15.3 0.0 collective-permute-done.11
  15.3 0.9 %broadcast_in_dim.8 = bf16[16,2,2,16,256]{4,3,2,1,0:T(8,128)(2,1)} broadcast(bf16[2,2,16,256]{3,2,1,0:T(8,128)(2,1)S(1)} %maximum_select_fusion), dimensions={1,2,3,4} | broadcast | bytes 557056 | tf_op jit(solution)/shard_map/broadcast_in_dim | solution.py:399
  16.2 7.0 %all-to-all-start = ((bf16[16,2,2,16,256]{4,3,2,1,0:T(8,128)(2,1)}), bf16[16,2,2,16,256]{4,3,2,1,0:T(8,128)(2,1)S(1)}, u32[]{:S(2)}, u32[]{:S(2)}) async-start(bf16[16,2,2,16,256]{4,3,2,1,0:T(8,128)(2,1)} %broadcast_in_dim.8), calls=%async_computation | async-start | bytes 1048576 | tf_op jit(solution)/shard_map/all_to_all | solution.py:402
  23.3 0.0 collective-permute-done.3
  23.3 0.0 collective-permute-done.2
  23.3 0.0 collective-permute-done.1
  23.3 0.1 collective-permute-start.4
  23.4 2.0 %collective-permute-start.6 = (bf16[128,512]{1,0:T(8,128)(2,1)S(1)}, bf16[128,512]{1,0:T(8,128)(2,1)S(1)}, u32[]{:S(2)}, u32[]{:S(2)}) collective-permute-start(bf16[128,512]{1,0:T(8,128)(2,1)S(1)} %copy-done), channel_id=1, source_target_pairs={{0,2},{1,3},{2,0},{3,1},{4,6},{5,7},{6,4},{7,5},{8,10},{9,11},{10,... | collective-permute-start | bytes 393224 | tf_op jit(solution)/shard_map/ppermute | solution.py:334
  25.4 0.1 collective-permute-start.7
  25.5 0.0 collective-permute-done.4.other
  25.5 0.0 copy-start.1
  25.5 4.2 %late.1 = (bf16[128,4096]{1,0:T(8,128)(2,1)}, bf16[512,128]{1,0:T(8,128)(2,1)S(1)}) custom-call(f32[3,128]{1,0:T(4,128)S(1)} %broadcast_in_dim.6.flags, bf16[16,2048]{1,0:T(8,128)(2,1)S(1)} %add_convert_fusion.1.summed, bf16[16,2048]{1,0:T(8,128)(2,1)S(1)} %collective-permute-done.4.other, bf16[16,4096]{1,0:T(8,128)(2,1)S(1)} %get-tuple-element.28.resid16, ...), custom_call_target="tpu_custom_call" | custom-call | flops 1048576 | bytes 65536 | tf_op jit(solution)/shard_map/late/pallas_call | solution.py:407
  29.7 0.3 collective-permute-start.8
  29.9 1.9 %collective-permute-start.9 = (bf16[512,128]{1,0:T(8,128)(2,1)S(1)}, bf16[512,128]{1,0:T(8,128)(2,1)S(1)}, u32[]{:S(2)}, u32[]{:S(2)}) collective-permute-start(bf16[512,128]{1,0:T(8,128)(2,1)S(1)} %get-tuple-element.33.grad0), channel_id=1, source_target_pairs={{0,2},{1,3},{2,0},{3,1},{4,6},{5,7},{6,4},{7,5},{8,10},{9,11},{10,... | collective-permute-start | bytes 393224 | tf_op jit(solution)/shard_map/ppermute | solution.py:334
  31.8 0.0 collective-permute-done.5.q1
  31.8 0.0 collective-permute-start.10
  31.9 0.1 pad_add_fusion.place
  31.9 0.0 collective-permute-done.6.q2
  31.9 0.1 collective-permute-done.7.q3
  32.0 2.1 %all-to-all-done = bf16[16,2,2,16,256]{4,3,2,1,0:T(8,128)(2,1)S(1)} async-done(((bf16[16,2,2,16,256]{4,3,2,1,0:T(8,128)(2,1)}), bf16[16,2,2,16,256]{4,3,2,1,0:T(8,128)(2,1)S(1)}, u32[]{:S(2)}, u32[]{:S(2)}) %all-to-all-start) | async-done | bytes 524320 | tf_op jit(solution)/shard_map/all_to_all | solution.py:402
  34.1 0.0 copy-done.1
  34.1 3.6 %forward.1 = (bf16[1024,2048]{1,0:T(8,128)(2,1)S(1)}, f32[128,2048]{1,0:T(8,128)S(1)}, f32[8,2048]{1,0:T(8,128)S(1)}) custom-call(s32[2]{0:T(128)S(1)} %pad_add_fusion.place, s32[64]{0:T(128)S(1)} %copy-done.1, bf16[128,512]{1,0:T(8,128)(2,1)S(1)} %copy-done, bf16[128,512]{1,0:T(8,128)(2,1)S(1)} %collective-permute-done.5.q1, ...), custom_call_target="tpu_custom_call" | custom-call | flops 1073741824 | bytes 6291456 | tf_op jit(solution)/shard_map/forward/pallas_call | solution.py:430
  37.7 0.0 collective-permute-done.8.grad1
  37.7 0.0 collective-permute-done.9.grad2
  37.7 0.2 collective-permute-done.10.grad3
  37.9 0.2 merge.1
  38.1 0.5 collective-permute-start.12
  38.6 1.7 %collective-permute-start.13 = (f32[8,768]{1,0:T(8,128)S(1)}, f32[8,768]{1,0:T(8,128)S(1)}, u32[]{:S(2)}, u32[]{:S(2)}) collective-permute-start(f32[8,768]{1,0:T(8,128)S(1)} %get-tuple-element.39.stats0), channel_id=1, source_target_pairs={{0,2},{1,3},{2,0},{3,1},{4,6},{5,7},{6,4},{7,5},{8,10},{9,11},{10,... | collective-permute-start | bytes 73736 | tf_op jit(solution)/shard_map/ppermute | solution.py:334
  40.3 0.0 collective-permute-start.14
  40.3 0.0 collective-permute-done.12.stats1
  40.3 2.1 %collective-permute-done.13.stats2 = f32[8,768]{1,0:T(8,128)S(1)} collective-permute-done((f32[8,768]{1,0:T(8,128)S(1)}, f32[8,768]{1,0:T(8,128)S(1)}, u32[]{:S(2)}, u32[]{:S(2)}) %collective-permute-start.13) | collective-permute-done | bytes 24608 | tf_op jit(solution)/shard_map/ppermute | solution.py:334
  42.4 1.4 %collective-permute-done.14.stats3 = f32[8,768]{1,0:T(8,128)S(1)} collective-permute-done((f32[8,768]{1,0:T(8,128)S(1)}, f32[8,768]{1,0:T(8,128)S(1)}, u32[]{:S(2)}, u32[]{:S(2)}) %collective-permute-start.14) | collective-permute-done | bytes 24608 | tf_op jit(solution)/shard_map/ppermute | solution.py:334
  43.8 4.3 %backward.1 = (bf16[1024,256]{1,0:T(8,128)(2,1)}, f32[128,512]{1,0:T(8,128)S(1)}, bf16[128,512]{1,0:T(8,128)(2,1)S(1)}, bf16[128,512]{1,0:T(8,128)(2,1)S(1)}, bf16[128,512]{1,0:T(8,128)(2,1)S(1)}) custom-call(bf16[128,512]{1,0:T(8,128)(2,1)S(1)} %copy-done, bf16[128,512]{1,0:T(8,128)(2,1)S(1)} %collective-permute-done.5.q1, ...), custom_call_target="tpu_custom_call" | custom-call | flops 2147483648 | bytes 8388608 | tf_op jit(solution)/shard_map/backward/pallas_call | solution.py:463
  48.1 7.2 %all-to-all-start.1 = ((bf16[16,64,256]{2,1,0:T(8,128)(2,1)}), bf16[16,64,256]{2,1,0:T(8,128)(2,1)S(1)}, u32[]{:S(2)}, u32[]{:S(2)}) async-start(bf16[16,64,256]{2,1,0:T(8,128)(2,1)} %bitcast.13), calls=%async_computation.1 | async-start | bytes 1048576 | tf_op jit(solution)/shard_map/all_to_all | solution.py:481
  55.4 0.1 collective-permute-start.17
  55.5 1.4 %collective-permute-start.16 = (bf16[128,512]{1,0:T(8,128)(2,1)S(1)}, bf16[128,512]{1,0:T(8,128)(2,1)S(1)}, u32[]{:S(2)}, u32[]{:S(2)}) collective-permute-start(bf16[128,512]{1,0:T(8,128)(2,1)S(1)} %get-tuple-element.43), channel_id=1, source_target_pairs={{0,2},{1,3},{2,0},{3,1},{4,6},{5,7},{6,4},{7,5},{8,10},{9,11},{10,... | collective-permute-start | bytes 393224 | tf_op jit(solution)/shard_map/ppermute | solution.py:334
  56.9 0.4 collective-permute-start.15
  57.3 9.9 %all-to-all-done.1 = bf16[16,64,256]{2,1,0:T(8,128)(2,1)S(1)} async-done(((bf16[16,64,256]{2,1,0:T(8,128)(2,1)}), bf16[16,64,256]{2,1,0:T(8,128)(2,1)S(1)}, u32[]{:S(2)}, u32[]{:S(2)}) %all-to-all-start.1) | async-done | bytes 524320 | tf_op jit(solution)/shard_map/all_to_all | solution.py:481
  67.2 0.1 reduce_sum.12
  67.3 0.8 %collective-permute-start.18 = (bf16[16,256]{1,0:T(8,128)(2,1)S(1)}, bf16[16,256]{1,0:T(8,128)(2,1)S(1)}, u32[]{:S(2)}, u32[]{:S(2)}) collective-permute-start(bf16[16,256]{1,0:T(8,128)(2,1)S(1)} %get-tuple-element.50), channel_id=1, source_target_pairs={{0,4},{4,0},{32,36},{36,32},{1,5},{5,1},{33,37},{37,33},{2,6},{6,2... | collective-permute-start | bytes 24584 | tf_op jit(solution)/shard_map/ppermute | solution.py:334
  68.1 3.1 %collective-permute-start.19 = (bf16[16,256]{1,0:T(8,128)(2,1)S(1)}, bf16[16,256]{1,0:T(8,128)(2,1)S(1)}, u32[]{:S(2)}, u32[]{:S(2)}) collective-permute-start(bf16[16,256]{1,0:T(8,128)(2,1)S(1)} %get-tuple-element.49), channel_id=1, source_target_pairs={{0,32},{4,36},{32,0},{36,4},{1,33},{5,37},{33,1},{37,5},{2,34},{6,... | collective-permute-start | bytes 24584 | tf_op jit(solution)/shard_map/ppermute | solution.py:334
  71.2 0.0 collective-permute-done.17
  71.2 2.7 %collective-permute-start.20 = (bf16[16,256]{1,0:T(8,128)(2,1)S(1)}, bf16[16,256]{1,0:T(8,128)(2,1)S(1)}, u32[]{:S(2)}, u32[]{:S(2)}) collective-permute-start(bf16[16,256]{1,0:T(8,128)(2,1)S(1)} %get-tuple-element.48), channel_id=1, source_target_pairs={{0,36},{4,32},{32,4},{36,0},{1,37},{5,33},{33,5},{37,1},{2,38},{6,... | collective-permute-start | bytes 24584 | tf_op jit(solution)/shard_map/ppermute | solution.py:334
  73.9 0.0 collective-permute-done.16
  73.9 0.0 collective-permute-done.15
  73.9 0.7 add_convert_fusion
  74.6 0.0 collective-permute-done.18.lower
  74.6 1.1 %collective-permute-done.19.upper = bf16[16,256]{1,0:T(8,128)(2,1)S(1)} collective-permute-done((bf16[16,256]{1,0:T(8,128)(2,1)S(1)}, bf16[16,256]{1,0:T(8,128)(2,1)S(1)}, u32[]{:S(2)}, u32[]{:S(2)}) %collective-permute-start.19) | collective-permute-done | bytes 8224 | tf_op jit(solution)/shard_map/ppermute | solution.py:334
  75.7 1.3 %collective-permute-done.20.both = bf16[16,256]{1,0:T(8,128)(2,1)S(1)} collective-permute-done((bf16[16,256]{1,0:T(8,128)(2,1)S(1)}, bf16[16,256]{1,0:T(8,128)(2,1)S(1)}, u32[]{:S(2)}, u32[]{:S(2)}) %collective-permute-start.20) | collective-permute-done | bytes 8224 | tf_op jit(solution)/shard_map/ppermute | solution.py:334
  76.9 0.6 final.1
  (4 shorter events, 0.1 us)
Async XLA Ops:
  0.8 5.0 %copy-start = (bf16[128,512]{1,0:T(8,128)(2,1)S(1)}, bf16[128,512]{1,0:T(8,128)(2,1)}, u32[]{:S(2)}) copy-start(bf16[128,512]{1,0:T(8,128)(2,1)} %q0.3) | copy-start | bytes 393220
  5.7 6.0 %collective-permute-start = (bf16[16,2048]{1,0:T(8,128)(2,1)S(1)}, bf16[16,2048]{1,0:T(8,128)(2,1)S(1)}, u32[]{:S(2)}, u32[]{:S(2)}) collective-permute-start(bf16[16,2048]{1,0:T(8,128)(2,1)S(1)} %get-tuple-element.27), channel_id=1, source_target_pairs={{0,1},{1,0},{2,3},{3,2},{4,5},{5,4},{6,7},{7,6},{8,9},{9,8},{10,11... | collective-permute-start | bytes 196616 | tf_op jit(solution)/shard_map/ppermute | solution.py:334
  5.8 26.0 %collective-permute-start.5 = (bf16[128,512]{1,0:T(8,128)(2,1)S(1)}, bf16[128,512]{1,0:T(8,128)(2,1)S(1)}, u32[]{:S(2)}, u32[]{:S(2)}) collective-permute-start(bf16[128,512]{1,0:T(8,128)(2,1)S(1)} %copy-done), channel_id=1, source_target_pairs={{0,1},{1,0},{2,3},{3,2},{4,5},{5,4},{6,7},{7,6},{8,9},{9,8},{10,11... | collective-permute-start | bytes 393224 | tf_op jit(solution)/shard_map/ppermute | solution.py:334
  6.3 9.0 %collective-permute-start.11 = (bf16[2,16,256]{2,1,0:T(8,128)(2,1)S(1)}, bf16[2,16,256]{2,1,0:T(8,128)(2,1)S(1)}, u32[]{:S(2)}, u32[]{:S(2)}) collective-permute-start(bf16[2,16,256]{2,1,0:T(8,128)(2,1)S(1)} %get-tuple-element.35), channel_id=1, source_target_pairs={{0,36},{4,32},{32,4},{36,0},{1,37},{5,33},{33,5},{37,1},{2,38},{6,... | collective-permute-start | bytes 49160 | tf_op jit(solution)/shard_map/ppermute | solution.py:334
  11.8 11.5 %collective-permute-start.3 = (bf16[16,2048]{1,0:T(8,128)(2,1)S(1)}, bf16[16,2048]{1,0:T(8,128)(2,1)S(1)}, u32[]{:S(2)}, u32[]{:S(2)}) collective-permute-start(bf16[16,2048]{1,0:T(8,128)(2,1)S(1)} %add_convert_fusion.2), channel_id=1, source_target_pairs={{0,6},{2,4},{4,2},{6,0},{1,7},{3,5},{5,3},{7,1},{8,14},{10,12},{12... | collective-permute-start | bytes 196616 | tf_op jit(solution)/shard_map/ppermute | solution.py:334
  12.8 10.4 %collective-permute-start.2 = (bf16[16,2048]{1,0:T(8,128)(2,1)S(1)}, bf16[16,2048]{1,0:T(8,128)(2,1)S(1)}, u32[]{:S(2)}, u32[]{:S(2)}) collective-permute-start(bf16[16,2048]{1,0:T(8,128)(2,1)S(1)} %add_convert_fusion.2), channel_id=1, source_target_pairs={{0,4},{2,6},{4,0},{6,2},{1,5},{3,7},{5,1},{7,3},{8,12},{10,14},{12... | collective-permute-start | bytes 196616 | tf_op jit(solution)/shard_map/ppermute | solution.py:334
  15.2 8.1 %collective-permute-start.1 = (bf16[16,2048]{1,0:T(8,128)(2,1)S(1)}, bf16[16,2048]{1,0:T(8,128)(2,1)S(1)}, u32[]{:S(2)}, u32[]{:S(2)}) collective-permute-start(bf16[16,2048]{1,0:T(8,128)(2,1)S(1)} %add_convert_fusion.2), channel_id=1, source_target_pairs={{0,2},{2,0},{4,6},{6,4},{1,3},{3,1},{5,7},{7,5},{8,10},{10,8},{12,... | collective-permute-start | bytes 196616 | tf_op jit(solution)/shard_map/ppermute | solution.py:334
  16.2 17.9 %all-to-all-start = ((bf16[16,2,2,16,256]{4,3,2,1,0:T(8,128)(2,1)}), bf16[16,2,2,16,256]{4,3,2,1,0:T(8,128)(2,1)S(1)}, u32[]{:S(2)}, u32[]{:S(2)}) async-start(bf16[16,2,2,16,256]{4,3,2,1,0:T(8,128)(2,1)} %broadcast_in_dim.8), calls=%async_computation | async-start | bytes 1048576 | tf_op jit(solution)/shard_map/all_to_all | solution.py:402
  23.3 2.2 %collective-permute-start.4 = (bf16[16,2048]{1,0:T(8,128)(2,1)S(1)}, bf16[16,2048]{1,0:T(8,128)(2,1)S(1)}, u32[]{:S(2)}, u32[]{:S(2)}) collective-permute-start(bf16[16,2048]{1,0:T(8,128)(2,1)S(1)} %add_convert_fusion.1.summed), channel_id=1, source_target_pairs={{0,1},{1,0},{2,3},{3,2},{4,5},{5,4},{6,7},{7,6},{8,9},{9,8},{10,11... | collective-permute-start | bytes 196616 | tf_op jit(solution)/shard_map/ppermute | solution.py:334
  23.4 8.5 %collective-permute-start.6 = (bf16[128,512]{1,0:T(8,128)(2,1)S(1)}, bf16[128,512]{1,0:T(8,128)(2,1)S(1)}, u32[]{:S(2)}, u32[]{:S(2)}) collective-permute-start(bf16[128,512]{1,0:T(8,128)(2,1)S(1)} %copy-done), channel_id=1, source_target_pairs={{0,2},{1,3},{2,0},{3,1},{4,6},{5,7},{6,4},{7,5},{8,10},{9,11},{10,... | collective-permute-start | bytes 393224 | tf_op jit(solution)/shard_map/ppermute | solution.py:334
  25.4 6.6 %collective-permute-start.7 = (bf16[128,512]{1,0:T(8,128)(2,1)S(1)}, bf16[128,512]{1,0:T(8,128)(2,1)S(1)}, u32[]{:S(2)}, u32[]{:S(2)}) collective-permute-start(bf16[128,512]{1,0:T(8,128)(2,1)S(1)} %copy-done), channel_id=1, source_target_pairs={{0,3},{1,2},{2,1},{3,0},{4,7},{5,6},{6,5},{7,4},{8,11},{9,10},{10,... | collective-permute-start | bytes 393224 | tf_op jit(solution)/shard_map/ppermute | solution.py:334
  25.5 8.6 %copy-start.1 = (s32[64]{0:T(128)S(1)}, s32[64]{0:T(128)}, u32[]{:S(2)}) copy-start(s32[64]{0:T(128)} %spans.1) | copy-start | bytes 772
  29.7 8.1 %collective-permute-start.8 = (bf16[512,128]{1,0:T(8,128)(2,1)S(1)}, bf16[512,128]{1,0:T(8,128)(2,1)S(1)}, u32[]{:S(2)}, u32[]{:S(2)}) collective-permute-start(bf16[512,128]{1,0:T(8,128)(2,1)S(1)} %get-tuple-element.33.grad0), channel_id=1, source_target_pairs={{0,1},{1,0},{2,3},{3,2},{4,5},{5,4},{6,7},{7,6},{8,9},{9,8},{10,11... | collective-permute-start | bytes 393224 | tf_op jit(solution)/shard_map/ppermute | solution.py:334
  29.9 7.8 %collective-permute-start.9 = (bf16[512,128]{1,0:T(8,128)(2,1)S(1)}, bf16[512,128]{1,0:T(8,128)(2,1)S(1)}, u32[]{:S(2)}, u32[]{:S(2)}) collective-permute-start(bf16[512,128]{1,0:T(8,128)(2,1)S(1)} %get-tuple-element.33.grad0), channel_id=1, source_target_pairs={{0,2},{1,3},{2,0},{3,1},{4,6},{5,7},{6,4},{7,5},{8,10},{9,11},{10,... | collective-permute-start | bytes 393224 | tf_op jit(solution)/shard_map/ppermute | solution.py:334
  31.8 6.1 %collective-permute-start.10 = (bf16[512,128]{1,0:T(8,128)(2,1)S(1)}, bf16[512,128]{1,0:T(8,128)(2,1)S(1)}, u32[]{:S(2)}, u32[]{:S(2)}) collective-permute-start(bf16[512,128]{1,0:T(8,128)(2,1)S(1)} %get-tuple-element.33.grad0), channel_id=1, source_target_pairs={{0,3},{1,2},{2,1},{3,0},{4,7},{5,6},{6,5},{7,4},{8,11},{9,10},{10,... | collective-permute-start | bytes 393224 | tf_op jit(solution)/shard_map/ppermute | solution.py:334
  38.1 2.2 %collective-permute-start.12 = (f32[8,768]{1,0:T(8,128)S(1)}, f32[8,768]{1,0:T(8,128)S(1)}, u32[]{:S(2)}, u32[]{:S(2)}) collective-permute-start(f32[8,768]{1,0:T(8,128)S(1)} %get-tuple-element.39.stats0), channel_id=1, source_target_pairs={{0,1},{1,0},{2,3},{3,2},{4,5},{5,4},{6,7},{7,6},{8,9},{9,8},{10,11... | collective-permute-start | bytes 73736 | tf_op jit(solution)/shard_map/ppermute | solution.py:334
  38.6 3.8 %collective-permute-start.13 = (f32[8,768]{1,0:T(8,128)S(1)}, f32[8,768]{1,0:T(8,128)S(1)}, u32[]{:S(2)}, u32[]{:S(2)}) collective-permute-start(f32[8,768]{1,0:T(8,128)S(1)} %get-tuple-element.39.stats0), channel_id=1, source_target_pairs={{0,2},{1,3},{2,0},{3,1},{4,6},{5,7},{6,4},{7,5},{8,10},{9,11},{10,... | collective-permute-start | bytes 73736 | tf_op jit(solution)/shard_map/ppermute | solution.py:334
  40.3 3.5 %collective-permute-start.14 = (f32[8,768]{1,0:T(8,128)S(1)}, f32[8,768]{1,0:T(8,128)S(1)}, u32[]{:S(2)}, u32[]{:S(2)}) collective-permute-start(f32[8,768]{1,0:T(8,128)S(1)} %get-tuple-element.39.stats0), channel_id=1, source_target_pairs={{0,3},{1,2},{2,1},{3,0},{4,7},{5,6},{6,5},{7,4},{8,11},{9,10},{10,... | collective-permute-start | bytes 73736 | tf_op jit(solution)/shard_map/ppermute | solution.py:334
  48.1 19.0 %all-to-all-start.1 = ((bf16[16,64,256]{2,1,0:T(8,128)(2,1)}), bf16[16,64,256]{2,1,0:T(8,128)(2,1)S(1)}, u32[]{:S(2)}, u32[]{:S(2)}) async-start(bf16[16,64,256]{2,1,0:T(8,128)(2,1)} %bitcast.13), calls=%async_computation.1 | async-start | bytes 1048576 | tf_op jit(solution)/shard_map/all_to_all | solution.py:481
  55.4 15.8 %collective-permute-start.17 = (bf16[128,512]{1,0:T(8,128)(2,1)S(1)}, bf16[128,512]{1,0:T(8,128)(2,1)S(1)}, u32[]{:S(2)}, u32[]{:S(2)}) collective-permute-start(bf16[128,512]{1,0:T(8,128)(2,1)S(1)} %get-tuple-element.44), channel_id=1, source_target_pairs={{0,3},{1,2},{2,1},{3,0},{4,7},{5,6},{6,5},{7,4},{8,11},{9,10},{10,... | collective-permute-start | bytes 393224 | tf_op jit(solution)/shard_map/ppermute | solution.py:334
  55.5 18.4 %collective-permute-start.16 = (bf16[128,512]{1,0:T(8,128)(2,1)S(1)}, bf16[128,512]{1,0:T(8,128)(2,1)S(1)}, u32[]{:S(2)}, u32[]{:S(2)}) collective-permute-start(bf16[128,512]{1,0:T(8,128)(2,1)S(1)} %get-tuple-element.43), channel_id=1, source_target_pairs={{0,2},{1,3},{2,0},{3,1},{4,6},{5,7},{6,4},{7,5},{8,10},{9,11},{10,... | collective-permute-start | bytes 393224 | tf_op jit(solution)/shard_map/ppermute | solution.py:334
  56.9 17.0 %collective-permute-start.15 = (bf16[128,512]{1,0:T(8,128)(2,1)S(1)}, bf16[128,512]{1,0:T(8,128)(2,1)S(1)}, u32[]{:S(2)}, u32[]{:S(2)}) collective-permute-start(bf16[128,512]{1,0:T(8,128)(2,1)S(1)} %get-tuple-element.42), channel_id=1, source_target_pairs={{0,1},{1,0},{2,3},{3,2},{4,5},{5,4},{6,7},{7,6},{8,9},{9,8},{10,11... | collective-permute-start | bytes 393224 | tf_op jit(solution)/shard_map/ppermute | solution.py:334
  67.3 7.3 %collective-permute-start.18 = (bf16[16,256]{1,0:T(8,128)(2,1)S(1)}, bf16[16,256]{1,0:T(8,128)(2,1)S(1)}, u32[]{:S(2)}, u32[]{:S(2)}) collective-permute-start(bf16[16,256]{1,0:T(8,128)(2,1)S(1)} %get-tuple-element.50), channel_id=1, source_target_pairs={{0,4},{4,0},{32,36},{36,32},{1,5},{5,1},{33,37},{37,33},{2,6},{6,2... | collective-permute-start | bytes 24584 | tf_op jit(solution)/shard_map/ppermute | solution.py:334
  68.1 7.6 %collective-permute-start.19 = (bf16[16,256]{1,0:T(8,128)(2,1)S(1)}, bf16[16,256]{1,0:T(8,128)(2,1)S(1)}, u32[]{:S(2)}, u32[]{:S(2)}) collective-permute-start(bf16[16,256]{1,0:T(8,128)(2,1)S(1)} %get-tuple-element.49), channel_id=1, source_target_pairs={{0,32},{4,36},{32,0},{36,4},{1,33},{5,37},{33,1},{37,5},{2,34},{6,... | collective-permute-start | bytes 24584 | tf_op jit(solution)/shard_map/ppermute | solution.py:334
  71.2 5.8 %collective-permute-start.20 = (bf16[16,256]{1,0:T(8,128)(2,1)S(1)}, bf16[16,256]{1,0:T(8,128)(2,1)S(1)}, u32[]{:S(2)}, u32[]{:S(2)}) collective-permute-start(bf16[16,256]{1,0:T(8,128)(2,1)S(1)} %get-tuple-element.48), channel_id=1, source_target_pairs={{0,36},{4,32},{32,4},{36,0},{1,37},{5,33},{33,5},{37,1},{2,38},{6,... | collective-permute-start | bytes 24584 | tf_op jit(solution)/shard_map/ppermute | solution.py:334

commit v6 on v5

--- a/solution.py
+++ b/solution.py
@@ -14,7 +14,7 @@
 CAP = 16
 EPS = 1e-06
 LOW = -1e30
-AHEAD = 4
+AHEAD = 8
 CTX = ("y", "hi", "x")
 EXP = ("lh", "lb", "core")
 CLIQUE = ("lb", "core")
@@ -380,7 +380,7 @@
             pltpu.VMEM((hidden, width), bf16),
             pltpu.VMEM(keys.shape, bf16),
             pltpu.VMEM(values.shape, bf16),
-            pltpu.SemaphoreType.DMA((19,)),
+            pltpu.SemaphoreType.DMA((31,)),
         ],
         compiler_params=params(24),
         cost_estimate=cost(10 * CAP * width * hidden, 8 << 20),

time: 77.9 us -> 78 us (level)
  no operation moved by 1% of the time
where the time goes in v6:
time: 78 us; the launch traced here: 77.7 us
  starting transfers between devices  38.9 us (50%)
  waiting for transfers between devices  18 us (23%)
  Pallas kernels  17.9 us (23%)
  other arithmetic  1.02 us (1%)
  local copies, waits for them, and re-layouts  0.97 us (1%)
  between operations  0.81 us (1%)
    ppermute x21, starting transfers between devices, across(): return lax.ppermute(array, axis, [(i, i ^ mask) for i in range(count)])  24.7 us
    all_to_all x1, waiting for transfers between devices, on_device(): lax.all_to_all(kv_part.reshape(n_y * n_x, n_hi * n_lh * chunk, 2 * DH), P...  9.85 us
    all_to_all x1, starting transfers between devices, on_device(): lax.all_to_all(kv_part.reshape(n_y * n_x, n_hi * n_lh * chunk, 2 * DH), P...  7.23 us
    all_to_all x1, starting transfers between devices, on_device(): kv = lax.all_to_all(sent, PLANE, 0, 0, tiled=True).reshape(-1, 2 * DH)  7.03 us
    ppermute x21, waiting for transfers between devices, across(): return lax.ppermute(array, axis, [(i, i ^ mask) for i in range(count)])  6.08 us
    pallas_call x1, Pallas kernels, on_device(): pl.pallas_call(expert_kernel, out_shape=(shape((CAP, half), bf16), shape(...  5.07 us
    pallas_call x1, Pallas kernels, on_device(): pl.pallas_call(backward_kernel, out_shape=(shape((n_keys, 2 * DH), bf16),...  4.3 us
    pallas_call x1, Pallas kernels, on_device(): pl.pallas_call(late_kernel, out_shape=(shape((rows, width), bf16), shape(...  4.15 us
  transfers between devices with their start and end apart: 23, of which 8 were waited for; matrix products, arithmetic and copies ran while one was open for 2% of the time, Pallas kernels for 10%

profile of v6, /device:TPU:32, one launch (start us, length us, event | category | flops | bytes accessed | tf_op | source)
XLA Modules:
  0.0 77.7 jit_solution(11377633111316470933)
XLA Ops:
  0.6 0.1 add_convert_fusion.3
  0.7 0.1 broadcast_in_dim.6.flags
  0.8 0.0 copy-start
  0.8 5.1 %expert.1 = (bf16[16,2048]{1,0:T(8,128)(2,1)S(1)}, f32[16,2048]{1,0:T(8,128)S(1)}, bf16[16,128]{1,0:T(8,128)(2,1)S(1)}, bf16[16,4096]{1,0:T(8,128)(2,1)S(1)}, bf...) custom-call(f32[3,128]{1,0:T(4,128)S(1)} %broadcast_in_dim.6.flags, ...), custom_call_target="tpu_custom_call" | custom-call | flops 125829120 | bytes 8388608 | tf_op jit(solution)/shard_map/expert/pallas_call | solution.py:360
  5.9 0.1 collective-permute-start
  6.0 0.0 copy-done
  6.0 0.5 collective-permute-start.5
  6.5 5.4 %collective-permute-start.11 = (bf16[2,16,256]{2,1,0:T(8,128)(2,1)S(1)}, bf16[2,16,256]{2,1,0:T(8,128)(2,1)S(1)}, u32[]{:S(2)}, u32[]{:S(2)}) collective-permute-start(bf16[2,16,256]{2,1,0:T(8,128)(2,1)S(1)} %get-tuple-element.35), channel_id=1, source_target_pairs={{0,36},{4,32},{32,4},{36,0},{1,37},{5,33},{33,5},{37,1},{2,38},{6,... | collective-permute-start | bytes 49160 | tf_op jit(solution)/shard_map/ppermute | solution.py:334
  11.9 0.0 collective-permute-done
  11.9 1.1 %collective-permute-start.3 = (bf16[16,2048]{1,0:T(8,128)(2,1)S(1)}, bf16[16,2048]{1,0:T(8,128)(2,1)S(1)}, u32[]{:S(2)}, u32[]{:S(2)}) collective-permute-start(bf16[16,2048]{1,0:T(8,128)(2,1)S(1)} %add_convert_fusion.2), channel_id=1, source_target_pairs={{0,6},{2,4},{4,2},{6,0},{1,7},{3,5},{5,3},{7,1},{8,14},{10,12},{12... | collective-permute-start | bytes 196616 | tf_op jit(solution)/shard_map/ppermute | solution.py:334
  13.0 2.4 %collective-permute-start.2 = (bf16[16,2048]{1,0:T(8,128)(2,1)S(1)}, bf16[16,2048]{1,0:T(8,128)(2,1)S(1)}, u32[]{:S(2)}, u32[]{:S(2)}) collective-permute-start(bf16[16,2048]{1,0:T(8,128)(2,1)S(1)} %add_convert_fusion.2), channel_id=1, source_target_pairs={{0,4},{2,6},{4,0},{6,2},{1,5},{3,7},{5,1},{7,3},{8,12},{10,14},{12... | collective-permute-start | bytes 196616 | tf_op jit(solution)/shard_map/ppermute | solution.py:334
  15.3 0.1 collective-permute-start.1
  15.5 0.0 collective-permute-done.11
  15.5 0.9 %broadcast_in_dim.8 = bf16[16,2,2,16,256]{4,3,2,1,0:T(8,128)(2,1)} broadcast(bf16[2,2,16,256]{3,2,1,0:T(8,128)(2,1)S(1)} %maximum_select_fusion), dimensions={1,2,3,4} | broadcast | bytes 557056 | tf_op jit(solution)/shard_map/broadcast_in_dim | solution.py:399
  16.4 7.0 %all-to-all-start = ((bf16[16,2,2,16,256]{4,3,2,1,0:T(8,128)(2,1)}), bf16[16,2,2,16,256]{4,3,2,1,0:T(8,128)(2,1)S(1)}, u32[]{:S(2)}, u32[]{:S(2)}) async-start(bf16[16,2,2,16,256]{4,3,2,1,0:T(8,128)(2,1)} %broadcast_in_dim.8), calls=%async_computation | async-start | bytes 1048576 | tf_op jit(solution)/shard_map/all_to_all | solution.py:402
  23.4 0.0 collective-permute-done.3
  23.4 0.0 collective-permute-done.2
  23.4 0.0 collective-permute-done.1
  23.5 0.1 collective-permute-start.4
  23.6 2.0 %collective-permute-start.6 = (bf16[128,512]{1,0:T(8,128)(2,1)S(1)}, bf16[128,512]{1,0:T(8,128)(2,1)S(1)}, u32[]{:S(2)}, u32[]{:S(2)}) collective-permute-start(bf16[128,512]{1,0:T(8,128)(2,1)S(1)} %copy-done), channel_id=1, source_target_pairs={{0,2},{1,3},{2,0},{3,1},{4,6},{5,7},{6,4},{7,5},{8,10},{9,11},{10,... | collective-permute-start | bytes 393224 | tf_op jit(solution)/shard_map/ppermute | solution.py:334
  25.6 0.1 collective-permute-start.7
  25.6 0.0 collective-permute-done.4.other
  25.6 0.0 copy-start.1
  25.6 4.2 %late.1 = (bf16[128,4096]{1,0:T(8,128)(2,1)}, bf16[512,128]{1,0:T(8,128)(2,1)S(1)}) custom-call(f32[3,128]{1,0:T(4,128)S(1)} %broadcast_in_dim.6.flags, bf16[16,2048]{1,0:T(8,128)(2,1)S(1)} %add_convert_fusion.1.summed, bf16[16,2048]{1,0:T(8,128)(2,1)S(1)} %collective-permute-done.4.other, bf16[16,4096]{1,0:T(8,128)(2,1)S(1)} %get-tuple-element.28.resid16, ...), custom_call_target="tpu_custom_call" | custom-call | flops 1048576 | bytes 65536 | tf_op jit(solution)/shard_map/late/pallas_call | solution.py:407
  29.8 0.3 collective-permute-start.8
  30.1 1.9 %collective-permute-start.9 = (bf16[512,128]{1,0:T(8,128)(2,1)S(1)}, bf16[512,128]{1,0:T(8,128)(2,1)S(1)}, u32[]{:S(2)}, u32[]{:S(2)}) collective-permute-start(bf16[512,128]{1,0:T(8,128)(2,1)S(1)} %get-tuple-element.33.grad0), channel_id=1, source_target_pairs={{0,2},{1,3},{2,0},{3,1},{4,6},{5,7},{6,4},{7,5},{8,10},{9,11},{10,... | collective-permute-start | bytes 393224 | tf_op jit(solution)/shard_map/ppermute | solution.py:334
  32.0 0.0 collective-permute-done.5.q1
  32.0 0.0 collective-permute-start.10
  32.0 0.1 pad_add_fusion.place
  32.1 0.0 collective-permute-done.6.q2
  32.1 0.1 collective-permute-done.7.q3
  32.1 2.1 %all-to-all-done = bf16[16,2,2,16,256]{4,3,2,1,0:T(8,128)(2,1)S(1)} async-done(((bf16[16,2,2,16,256]{4,3,2,1,0:T(8,128)(2,1)}), bf16[16,2,2,16,256]{4,3,2,1,0:T(8,128)(2,1)S(1)}, u32[]{:S(2)}, u32[]{:S(2)}) %all-to-all-start) | async-done | bytes 524320 | tf_op jit(solution)/shard_map/all_to_all | solution.py:402
  34.2 0.0 copy-done.1
  34.2 3.6 %forward.1 = (bf16[1024,2048]{1,0:T(8,128)(2,1)S(1)}, f32[128,2048]{1,0:T(8,128)S(1)}, f32[8,2048]{1,0:T(8,128)S(1)}) custom-call(s32[2]{0:T(128)S(1)} %pad_add_fusion.place, s32[64]{0:T(128)S(1)} %copy-done.1, bf16[128,512]{1,0:T(8,128)(2,1)S(1)} %copy-done, bf16[128,512]{1,0:T(8,128)(2,1)S(1)} %collective-permute-done.5.q1, ...), custom_call_target="tpu_custom_call" | custom-call | flops 1073741824 | bytes 6291456 | tf_op jit(solution)/shard_map/forward/pallas_call | solution.py:430
  37.8 0.0 collective-permute-done.8.grad1
  37.8 0.0 collective-permute-done.9.grad2
  37.9 0.1 collective-permute-done.10.grad3
  38.0 0.2 merge.1
  38.2 0.5 collective-permute-start.12
  38.7 1.7 %collective-permute-start.13 = (f32[8,768]{1,0:T(8,128)S(1)}, f32[8,768]{1,0:T(8,128)S(1)}, u32[]{:S(2)}, u32[]{:S(2)}) collective-permute-start(f32[8,768]{1,0:T(8,128)S(1)} %get-tuple-element.39.stats0), channel_id=1, source_target_pairs={{0,2},{1,3},{2,0},{3,1},{4,6},{5,7},{6,4},{7,5},{8,10},{9,11},{10,... | collective-permute-start | bytes 73736 | tf_op jit(solution)/shard_map/ppermute | solution.py:334
  40.4 0.0 collective-permute-start.14
  40.4 0.0 collective-permute-done.12.stats1
  40.4 2.1 %collective-permute-done.13.stats2 = f32[8,768]{1,0:T(8,128)S(1)} collective-permute-done((f32[8,768]{1,0:T(8,128)S(1)}, f32[8,768]{1,0:T(8,128)S(1)}, u32[]{:S(2)}, u32[]{:S(2)}) %collective-permute-start.13) | collective-permute-done | bytes 24608 | tf_op jit(solution)/shard_map/ppermute | solution.py:334
  42.5 1.4 %collective-permute-done.14.stats3 = f32[8,768]{1,0:T(8,128)S(1)} collective-permute-done((f32[8,768]{1,0:T(8,128)S(1)}, f32[8,768]{1,0:T(8,128)S(1)}, u32[]{:S(2)}, u32[]{:S(2)}) %collective-permute-start.14) | collective-permute-done | bytes 24608 | tf_op jit(solution)/shard_map/ppermute | solution.py:334
  43.9 4.3 %backward.1 = (bf16[1024,256]{1,0:T(8,128)(2,1)}, f32[128,512]{1,0:T(8,128)S(1)}, bf16[128,512]{1,0:T(8,128)(2,1)S(1)}, bf16[128,512]{1,0:T(8,128)(2,1)S(1)}, bf16[128,512]{1,0:T(8,128)(2,1)S(1)}) custom-call(bf16[128,512]{1,0:T(8,128)(2,1)S(1)} %copy-done, bf16[128,512]{1,0:T(8,128)(2,1)S(1)} %collective-permute-done.5.q1, ...), custom_call_target="tpu_custom_call" | custom-call | flops 2147483648 | bytes 8388608 | tf_op jit(solution)/shard_map/backward/pallas_call | solution.py:463
  48.3 7.2 %all-to-all-start.1 = ((bf16[16,64,256]{2,1,0:T(8,128)(2,1)}), bf16[16,64,256]{2,1,0:T(8,128)(2,1)S(1)}, u32[]{:S(2)}, u32[]{:S(2)}) async-start(bf16[16,64,256]{2,1,0:T(8,128)(2,1)} %bitcast.13), calls=%async_computation.1 | async-start | bytes 1048576 | tf_op jit(solution)/shard_map/all_to_all | solution.py:481
  55.5 0.1 collective-permute-start.17
  55.6 1.4 %collective-permute-start.16 = (bf16[128,512]{1,0:T(8,128)(2,1)S(1)}, bf16[128,512]{1,0:T(8,128)(2,1)S(1)}, u32[]{:S(2)}, u32[]{:S(2)}) collective-permute-start(bf16[128,512]{1,0:T(8,128)(2,1)S(1)} %get-tuple-element.43), channel_id=1, source_target_pairs={{0,2},{1,3},{2,0},{3,1},{4,6},{5,7},{6,4},{7,5},{8,10},{9,11},{10,... | collective-permute-start | bytes 393224 | tf_op jit(solution)/shard_map/ppermute | solution.py:334
  57.0 0.4 collective-permute-start.15
  57.4 9.9 %all-to-all-done.1 = bf16[16,64,256]{2,1,0:T(8,128)(2,1)S(1)} async-done(((bf16[16,64,256]{2,1,0:T(8,128)(2,1)}), bf16[16,64,256]{2,1,0:T(8,128)(2,1)S(1)}, u32[]{:S(2)}, u32[]{:S(2)}) %all-to-all-start.1) | async-done | bytes 524320 | tf_op jit(solution)/shard_map/all_to_all | solution.py:481
  67.3 0.1 reduce_sum.12
  67.4 0.8 %collective-permute-start.18 = (bf16[16,256]{1,0:T(8,128)(2,1)S(1)}, bf16[16,256]{1,0:T(8,128)(2,1)S(1)}, u32[]{:S(2)}, u32[]{:S(2)}) collective-permute-start(bf16[16,256]{1,0:T(8,128)(2,1)S(1)} %get-tuple-element.50), channel_id=1, source_target_pairs={{0,4},{4,0},{32,36},{36,32},{1,5},{5,1},{33,37},{37,33},{2,6},{6,2... | collective-permute-start | bytes 24584 | tf_op jit(solution)/shard_map/ppermute | solution.py:334
  68.3 3.0 %collective-permute-start.19 = (bf16[16,256]{1,0:T(8,128)(2,1)S(1)}, bf16[16,256]{1,0:T(8,128)(2,1)S(1)}, u32[]{:S(2)}, u32[]{:S(2)}) collective-permute-start(bf16[16,256]{1,0:T(8,128)(2,1)S(1)} %get-tuple-element.49), channel_id=1, source_target_pairs={{0,32},{4,36},{32,0},{36,4},{1,33},{5,37},{33,1},{37,5},{2,34},{6,... | collective-permute-start | bytes 24584 | tf_op jit(solution)/shard_map/ppermute | solution.py:334
  71.3 0.0 collective-permute-done.17
  71.3 2.7 %collective-permute-start.20 = (bf16[16,256]{1,0:T(8,128)(2,1)S(1)}, bf16[16,256]{1,0:T(8,128)(2,1)S(1)}, u32[]{:S(2)}, u32[]{:S(2)}) collective-permute-start(bf16[16,256]{1,0:T(8,128)(2,1)S(1)} %get-tuple-element.48), channel_id=1, source_target_pairs={{0,36},{4,32},{32,4},{36,0},{1,37},{5,33},{33,5},{37,1},{2,38},{6,... | collective-permute-start | bytes 24584 | tf_op jit(solution)/shard_map/ppermute | solution.py:334
  74.0 0.0 collective-permute-done.16
  74.0 0.0 collective-permute-done.15
  74.0 0.7 add_convert_fusion
  74.7 0.0 collective-permute-done.18.lower
  74.7 1.1 %collective-permute-done.19.upper = bf16[16,256]{1,0:T(8,128)(2,1)S(1)} collective-permute-done((bf16[16,256]{1,0:T(8,128)(2,1)S(1)}, bf16[16,256]{1,0:T(8,128)(2,1)S(1)}, u32[]{:S(2)}, u32[]{:S(2)}) %collective-permute-start.19) | collective-permute-done | bytes 8224 | tf_op jit(solution)/shard_map/ppermute | solution.py:334
  75.8 1.2 %collective-permute-done.20.both = bf16[16,256]{1,0:T(8,128)(2,1)S(1)} collective-permute-done((bf16[16,256]{1,0:T(8,128)(2,1)S(1)}, bf16[16,256]{1,0:T(8,128)(2,1)S(1)}, u32[]{:S(2)}, u32[]{:S(2)}) %collective-permute-start.20) | collective-permute-done | bytes 8224 | tf_op jit(solution)/shard_map/ppermute | solution.py:334
  77.1 0.6 final.1
  (4 shorter events, 0.1 us)
Async XLA Ops:
  0.8 5.2 %copy-start = (bf16[128,512]{1,0:T(8,128)(2,1)S(1)}, bf16[128,512]{1,0:T(8,128)(2,1)}, u32[]{:S(2)}) copy-start(bf16[128,512]{1,0:T(8,128)(2,1)} %q0.3) | copy-start | bytes 393220
  5.9 6.0 %collective-permute-start = (bf16[16,2048]{1,0:T(8,128)(2,1)S(1)}, bf16[16,2048]{1,0:T(8,128)(2,1)S(1)}, u32[]{:S(2)}, u32[]{:S(2)}) collective-permute-start(bf16[16,2048]{1,0:T(8,128)(2,1)S(1)} %get-tuple-element.27), channel_id=1, source_target_pairs={{0,1},{1,0},{2,3},{3,2},{4,5},{5,4},{6,7},{7,6},{8,9},{9,8},{10,11... | collective-permute-start | bytes 196616 | tf_op jit(solution)/shard_map/ppermute | solution.py:334
  6.0 26.0 %collective-permute-start.5 = (bf16[128,512]{1,0:T(8,128)(2,1)S(1)}, bf16[128,512]{1,0:T(8,128)(2,1)S(1)}, u32[]{:S(2)}, u32[]{:S(2)}) collective-permute-start(bf16[128,512]{1,0:T(8,128)(2,1)S(1)} %copy-done), channel_id=1, source_target_pairs={{0,1},{1,0},{2,3},{3,2},{4,5},{5,4},{6,7},{7,6},{8,9},{9,8},{10,11... | collective-permute-start | bytes 393224 | tf_op jit(solution)/shard_map/ppermute | solution.py:334
  6.5 9.0 %collective-permute-start.11 = (bf16[2,16,256]{2,1,0:T(8,128)(2,1)S(1)}, bf16[2,16,256]{2,1,0:T(8,128)(2,1)S(1)}, u32[]{:S(2)}, u32[]{:S(2)}) collective-permute-start(bf16[2,16,256]{2,1,0:T(8,128)(2,1)S(1)} %get-tuple-element.35), channel_id=1, source_target_pairs={{0,36},{4,32},{32,4},{36,0},{1,37},{5,33},{33,5},{37,1},{2,38},{6,... | collective-permute-start | bytes 49160 | tf_op jit(solution)/shard_map/ppermute | solution.py:334
  11.9 11.5 %collective-permute-start.3 = (bf16[16,2048]{1,0:T(8,128)(2,1)S(1)}, bf16[16,2048]{1,0:T(8,128)(2,1)S(1)}, u32[]{:S(2)}, u32[]{:S(2)}) collective-permute-start(bf16[16,2048]{1,0:T(8,128)(2,1)S(1)} %add_convert_fusion.2), channel_id=1, source_target_pairs={{0,6},{2,4},{4,2},{6,0},{1,7},{3,5},{5,3},{7,1},{8,14},{10,12},{12... | collective-permute-start | bytes 196616 | tf_op jit(solution)/shard_map/ppermute | solution.py:334
  13.0 10.4 %collective-permute-start.2 = (bf16[16,2048]{1,0:T(8,128)(2,1)S(1)}, bf16[16,2048]{1,0:T(8,128)(2,1)S(1)}, u32[]{:S(2)}, u32[]{:S(2)}) collective-permute-start(bf16[16,2048]{1,0:T(8,128)(2,1)S(1)} %add_convert_fusion.2), channel_id=1, source_target_pairs={{0,4},{2,6},{4,0},{6,2},{1,5},{3,7},{5,1},{7,3},{8,12},{10,14},{12... | collective-permute-start | bytes 196616 | tf_op jit(solution)/shard_map/ppermute | solution.py:334
  15.3 8.1 %collective-permute-start.1 = (bf16[16,2048]{1,0:T(8,128)(2,1)S(1)}, bf16[16,2048]{1,0:T(8,128)(2,1)S(1)}, u32[]{:S(2)}, u32[]{:S(2)}) collective-permute-start(bf16[16,2048]{1,0:T(8,128)(2,1)S(1)} %add_convert_fusion.2), channel_id=1, source_target_pairs={{0,2},{2,0},{4,6},{6,4},{1,3},{3,1},{5,7},{7,5},{8,10},{10,8},{12,... | collective-permute-start | bytes 196616 | tf_op jit(solution)/shard_map/ppermute | solution.py:334
  16.4 17.9 %all-to-all-start = ((bf16[16,2,2,16,256]{4,3,2,1,0:T(8,128)(2,1)}), bf16[16,2,2,16,256]{4,3,2,1,0:T(8,128)(2,1)S(1)}, u32[]{:S(2)}, u32[]{:S(2)}) async-start(bf16[16,2,2,16,256]{4,3,2,1,0:T(8,128)(2,1)} %broadcast_in_dim.8), calls=%async_computation | async-start | bytes 1048576 | tf_op jit(solution)/shard_map/all_to_all | solution.py:402
  23.5 2.2 %collective-permute-start.4 = (bf16[16,2048]{1,0:T(8,128)(2,1)S(1)}, bf16[16,2048]{1,0:T(8,128)(2,1)S(1)}, u32[]{:S(2)}, u32[]{:S(2)}) collective-permute-start(bf16[16,2048]{1,0:T(8,128)(2,1)S(1)} %add_convert_fusion.1.summed), channel_id=1, source_target_pairs={{0,1},{1,0},{2,3},{3,2},{4,5},{5,4},{6,7},{7,6},{8,9},{9,8},{10,11... | collective-permute-start | bytes 196616 | tf_op jit(solution)/shard_map/ppermute | solution.py:334
  23.6 8.5 %collective-permute-start.6 = (bf16[128,512]{1,0:T(8,128)(2,1)S(1)}, bf16[128,512]{1,0:T(8,128)(2,1)S(1)}, u32[]{:S(2)}, u32[]{:S(2)}) collective-permute-start(bf16[128,512]{1,0:T(8,128)(2,1)S(1)} %copy-done), channel_id=1, source_target_pairs={{0,2},{1,3},{2,0},{3,1},{4,6},{5,7},{6,4},{7,5},{8,10},{9,11},{10,... | collective-permute-start | bytes 393224 | tf_op jit(solution)/shard_map/ppermute | solution.py:334
  25.6 6.6 %collective-permute-start.7 = (bf16[128,512]{1,0:T(8,128)(2,1)S(1)}, bf16[128,512]{1,0:T(8,128)(2,1)S(1)}, u32[]{:S(2)}, u32[]{:S(2)}) collective-permute-start(bf16[128,512]{1,0:T(8,128)(2,1)S(1)} %copy-done), channel_id=1, source_target_pairs={{0,3},{1,2},{2,1},{3,0},{4,7},{5,6},{6,5},{7,4},{8,11},{9,10},{10,... | collective-permute-start | bytes 393224 | tf_op jit(solution)/shard_map/ppermute | solution.py:334
  25.6 8.6 %copy-start.1 = (s32[64]{0:T(128)S(1)}, s32[64]{0:T(128)}, u32[]{:S(2)}) copy-start(s32[64]{0:T(128)} %spans.1) | copy-start | bytes 772
  29.8 8.1 %collective-permute-start.8 = (bf16[512,128]{1,0:T(8,128)(2,1)S(1)}, bf16[512,128]{1,0:T(8,128)(2,1)S(1)}, u32[]{:S(2)}, u32[]{:S(2)}) collective-permute-start(bf16[512,128]{1,0:T(8,128)(2,1)S(1)} %get-tuple-element.33.grad0), channel_id=1, source_target_pairs={{0,1},{1,0},{2,3},{3,2},{4,5},{5,4},{6,7},{7,6},{8,9},{9,8},{10,11... | collective-permute-start | bytes 393224 | tf_op jit(solution)/shard_map/ppermute | solution.py:334
  30.1 7.8 %collective-permute-start.9 = (bf16[512,128]{1,0:T(8,128)(2,1)S(1)}, bf16[512,128]{1,0:T(8,128)(2,1)S(1)}, u32[]{:S(2)}, u32[]{:S(2)}) collective-permute-start(bf16[512,128]{1,0:T(8,128)(2,1)S(1)} %get-tuple-element.33.grad0), channel_id=1, source_target_pairs={{0,2},{1,3},{2,0},{3,1},{4,6},{5,7},{6,4},{7,5},{8,10},{9,11},{10,... | collective-permute-start | bytes 393224 | tf_op jit(solution)/shard_map/ppermute | solution.py:334
  32.0 6.0 %collective-permute-start.10 = (bf16[512,128]{1,0:T(8,128)(2,1)S(1)}, bf16[512,128]{1,0:T(8,128)(2,1)S(1)}, u32[]{:S(2)}, u32[]{:S(2)}) collective-permute-start(bf16[512,128]{1,0:T(8,128)(2,1)S(1)} %get-tuple-element.33.grad0), channel_id=1, source_target_pairs={{0,3},{1,2},{2,1},{3,0},{4,7},{5,6},{6,5},{7,4},{8,11},{9,10},{10,... | collective-permute-start | bytes 393224 | tf_op jit(solution)/shard_map/ppermute | solution.py:334
  38.2 2.2 %collective-permute-start.12 = (f32[8,768]{1,0:T(8,128)S(1)}, f32[8,768]{1,0:T(8,128)S(1)}, u32[]{:S(2)}, u32[]{:S(2)}) collective-permute-start(f32[8,768]{1,0:T(8,128)S(1)} %get-tuple-element.39.stats0), channel_id=1, source_target_pairs={{0,1},{1,0},{2,3},{3,2},{4,5},{5,4},{6,7},{7,6},{8,9},{9,8},{10,11... | collective-permute-start | bytes 73736 | tf_op jit(solution)/shard_map/ppermute | solution.py:334
  38.7 3.8 %collective-permute-start.13 = (f32[8,768]{1,0:T(8,128)S(1)}, f32[8,768]{1,0:T(8,128)S(1)}, u32[]{:S(2)}, u32[]{:S(2)}) collective-permute-start(f32[8,768]{1,0:T(8,128)S(1)} %get-tuple-element.39.stats0), channel_id=1, source_target_pairs={{0,2},{1,3},{2,0},{3,1},{4,6},{5,7},{6,4},{7,5},{8,10},{9,11},{10,... | collective-permute-start | bytes 73736 | tf_op jit(solution)/shard_map/ppermute | solution.py:334
  40.4 3.5 %collective-permute-start.14 = (f32[8,768]{1,0:T(8,128)S(1)}, f32[8,768]{1,0:T(8,128)S(1)}, u32[]{:S(2)}, u32[]{:S(2)}) collective-permute-start(f32[8,768]{1,0:T(8,128)S(1)} %get-tuple-element.39.stats0), channel_id=1, source_target_pairs={{0,3},{1,2},{2,1},{3,0},{4,7},{5,6},{6,5},{7,4},{8,11},{9,10},{10,... | collective-permute-start | bytes 73736 | tf_op jit(solution)/shard_map/ppermute | solution.py:334
  48.3 19.0 %all-to-all-start.1 = ((bf16[16,64,256]{2,1,0:T(8,128)(2,1)}), bf16[16,64,256]{2,1,0:T(8,128)(2,1)S(1)}, u32[]{:S(2)}, u32[]{:S(2)}) async-start(bf16[16,64,256]{2,1,0:T(8,128)(2,1)} %bitcast.13), calls=%async_computation.1 | async-start | bytes 1048576 | tf_op jit(solution)/shard_map/all_to_all | solution.py:481
  55.5 15.8 %collective-permute-start.17 = (bf16[128,512]{1,0:T(8,128)(2,1)S(1)}, bf16[128,512]{1,0:T(8,128)(2,1)S(1)}, u32[]{:S(2)}, u32[]{:S(2)}) collective-permute-start(bf16[128,512]{1,0:T(8,128)(2,1)S(1)} %get-tuple-element.44), channel_id=1, source_target_pairs={{0,3},{1,2},{2,1},{3,0},{4,7},{5,6},{6,5},{7,4},{8,11},{9,10},{10,... | collective-permute-start | bytes 393224 | tf_op jit(solution)/shard_map/ppermute | solution.py:334
  55.6 18.4 %collective-permute-start.16 = (bf16[128,512]{1,0:T(8,128)(2,1)S(1)}, bf16[128,512]{1,0:T(8,128)(2,1)S(1)}, u32[]{:S(2)}, u32[]{:S(2)}) collective-permute-start(bf16[128,512]{1,0:T(8,128)(2,1)S(1)} %get-tuple-element.43), channel_id=1, source_target_pairs={{0,2},{1,3},{2,0},{3,1},{4,6},{5,7},{6,4},{7,5},{8,10},{9,11},{10,... | collective-permute-start | bytes 393224 | tf_op jit(solution)/shard_map/ppermute | solution.py:334
  57.0 17.0 %collective-permute-start.15 = (bf16[128,512]{1,0:T(8,128)(2,1)S(1)}, bf16[128,512]{1,0:T(8,128)(2,1)S(1)}, u32[]{:S(2)}, u32[]{:S(2)}) collective-permute-start(bf16[128,512]{1,0:T(8,128)(2,1)S(1)} %get-tuple-element.42), channel_id=1, source_target_pairs={{0,1},{1,0},{2,3},{3,2},{4,5},{5,4},{6,7},{7,6},{8,9},{9,8},{10,11... | collective-permute-start | bytes 393224 | tf_op jit(solution)/shard_map/ppermute | solution.py:334
  67.4 7.3 %collective-permute-start.18 = (bf16[16,256]{1,0:T(8,128)(2,1)S(1)}, bf16[16,256]{1,0:T(8,128)(2,1)S(1)}, u32[]{:S(2)}, u32[]{:S(2)}) collective-permute-start(bf16[16,256]{1,0:T(8,128)(2,1)S(1)} %get-tuple-element.50), channel_id=1, source_target_pairs={{0,4},{4,0},{32,36},{36,32},{1,5},{5,1},{33,37},{37,33},{2,6},{6,2... | collective-permute-start | bytes 24584 | tf_op jit(solution)/shard_map/ppermute | solution.py:334
  68.3 7.6 %collective-permute-start.19 = (bf16[16,256]{1,0:T(8,128)(2,1)S(1)}, bf16[16,256]{1,0:T(8,128)(2,1)S(1)}, u32[]{:S(2)}, u32[]{:S(2)}) collective-permute-start(bf16[16,256]{1,0:T(8,128)(2,1)S(1)} %get-tuple-element.49), channel_id=1, source_target_pairs={{0,32},{4,36},{32,0},{36,4},{1,33},{5,37},{33,1},{37,5},{2,34},{6,... | collective-permute-start | bytes 24584 | tf_op jit(solution)/shard_map/ppermute | solution.py:334
  71.3 5.8 %collective-permute-start.20 = (bf16[16,256]{1,0:T(8,128)(2,1)S(1)}, bf16[16,256]{1,0:T(8,128)(2,1)S(1)}, u32[]{:S(2)}, u32[]{:S(2)}) collective-permute-start(bf16[16,256]{1,0:T(8,128)(2,1)S(1)} %get-tuple-element.48), channel_id=1, source_target_pairs={{0,36},{4,32},{32,4},{36,0},{1,37},{5,33},{33,5},{37,1},{2,38},{6,... | collective-permute-start | bytes 24584 | tf_op jit(solution)/shard_map/ppermute | solution.py:334
